TPU v7x, 32 devices: a whole 2x2x4 slice. The times are simulated.
32 devices in a mesh: parent: 4 (over x, core), child: 8 (over z, y).
Axes of the slice: x: 2, y: 2, z: 4, core: 2. Of those that a mesh axis runs over, the one named last changes fastest.
Arguments:
- parent_tracer: float32 [2, 50, 64, 192], P(None, None, 'child', 'parent'), may hold values from -6 to 6
- child_tracer: float32 [2, 50, 864, 144], P(None, None, ('parent', 'child')), may hold values from -6 to 6
- strip_cols: int32 [4, 8], replicated, may hold values from 1 to 9, 48 in all within a row
- row_offset: int32 [1], replicated, may hold values from 0 to 16
- parent_wet: int32 [64, 192], P('child', 'parent'), may hold values 0 or 1
- child_wet: int32 [864, 144], P(('parent', 'child')), may hold values 0 or 1
- vert_mix: float32 [2, 49], replicated, may hold values from 0.2 to 5
Outputs:
- parent_next: float32 [2, 50, 64, 192], P(None, None, 'child', 'parent')
- child_next: float32 [2, 50, 864, 144], P(None, None, ('parent', 'child'))
Inputs may be any that keep to these rules, and one draw needn't show every extreme that they name: Each row of strip_cols sums to 48; the largest entry is 9.
All inputs are finite; a program needn't handle non-finite values. No bound on the sum of `parent_wet` or of `child_wet` on one device may be relied on, other than what follows from the above.
Results may differ from a plain program's by a relative error of at most 0.00005.
Values sent between devices are 32-bit elements; how exact they have to be, the bound alone decides.
No kernel may reach another device: no remote copies, remote signals or barrier semaphores. Data moves between devices by JAX's collectives and lax.ppermute only.
A program may use at most 192 MiB of HBM per device.

v0:
```python
import functools

import jax
import jax.numpy as jnp
from jax import lax
from jax.experimental import pallas as pl
from jax.experimental.pallas import tpu as pltpu
from jax.sharding import PartitionSpec as P

diffusion = 0.2
nudging = 0.5
one_ninth = 1.0 / 9.0
LANES = 128
ROWS = 32
HIGH = lax.Precision.HIGHEST

VM = pl.BlockSpec(memory_space=pltpu.VMEM)
SM = pl.BlockSpec(memory_space=pltpu.SMEM)


def params(mib):
    return pltpu.CompilerParams(vmem_limit_bytes=mib << 20)


def my_strip(cols_ref, strips):
    return cols_ref[lax.axis_index("parent"), lax.axis_index("child")]


def strip_starts(cols_ref, strips):
    group = lax.axis_index("parent")
    start = jnp.int32(0)
    starts = []
    for j in range(strips):
        starts.append(start)
        start = start + cols_ref[group, j]
    return starts


def coefficient_kernel(mix_ref, weight_ref, inverse_ref, d_ref, c_ref):
    tracers, levels = mix_ref.shape[0], mix_ref.shape[1] + 1
    lane = lax.broadcasted_iota(jnp.int32, (8, LANES), 1)
    which = lane // levels

    def mixed(k):
        row = jnp.zeros((8, LANES), jnp.float32)
        for t in range(tracers):
            row = jnp.where(which == t, mix_ref[t, k], row)
        return row

    weight = None
    d = None
    for k in range(levels):
        above = mixed(k - 1) if k else jnp.zeros((8, LANES), jnp.float32)
        below = mixed(k) if k < levels - 1 else jnp.zeros((8, LANES), jnp.float32)
        if k == 0:
            weight = 1.0 / (1.0 + below)
        else:
            weight = 1.0 / (1.0 + above + below - above * (above * weight))
        unit = (lane - which * levels == k).astype(jnp.float32)
        d = (unit if k == 0 else unit + above * d) * weight
        d_ref[pl.ds(8 * k, 8), :] = d
        c_ref[pl.ds(8 * k, 8), :] = below * weight
        for t in range(tracers):
            weight_ref[t * levels + k : t * levels + k + 1, :] = jnp.broadcast_to(
                weight[:1, t * levels : t * levels + 1], (1, LANES)
            )
    inverse_ref[...] = jnp.zeros_like(inverse_ref)
    x = None
    for k in reversed(range(levels)):
        x = d_ref[pl.ds(8 * k, 8), :]
        if k < levels - 1:
            x = x + c_ref[pl.ds(8 * k, 8), :] * above_x
        above_x = x
        for t in range(tracers):
            inverse_ref[t * levels + k : t * levels + k + 1, :] = jnp.where(which == t, x, 0.0)[:1]


def prepare_kernel(
    strips, cols_ref, parent_ref, pwet_ref, child_ref, cwet_ref,
    flat_ref, forth_ref, back_ref, left_ref, right_ref, nat_ref,
):
    total, capacity, child_rows = child_ref.shape
    rows, width = pwet_ref.shape
    lane_tiles = (child_rows + LANES - 1) // LANES
    level_rows = (total + 7) // 8 * 8
    wet = pwet_ref[...].astype(jnp.float32)
    for l in range(total):
        nat_ref[l * rows : (l + 1) * rows, :width] = wet * parent_ref[l * rows : (l + 1) * rows, :]
    nat_ref[total * rows : (total + 1) * rows, :width] = wet
    nat_ref[(total + 1) * rows :, :] = jnp.zeros((LANES * rows - (total + 1) * rows, LANES), jnp.float32)
    for r in range(rows):
        turned = nat_ref[pl.ds(r, LANES, stride=rows), :].T
        flat_ref[pl.ds(r, width, stride=rows), :] = turned[:width]
    left_ref[...] = flat_ref[:rows, :]
    right_ref[...] = flat_ref[(width - 1) * rows :, :]
    last = 3 * my_strip(cols_ref, strips) - 1
    for ref, x, r in ((forth_ref, last, rows - 1), (back_ref, 0, 0)):
        cell_wet = cwet_ref[pl.ds(x, 1), :].astype(jnp.float32)
        for l in range(total):
            row = child_ref[l, pl.ds(x, 1), :] * cell_wet
            for t in range(lane_tiles):
                stop = min(child_rows, (t + 1) * LANES)
                ref[t * level_rows + l : t * level_rows + l + 1, : stop - t * LANES] = row[:, t * LANES : stop]
        base = lane_tiles * level_rows
        ref[base : base + width, :] = flat_ref[pl.ds(r, width, stride=rows), :]


def solve_kernel(
    strips, rows,
    cols_ref, offset_ref, mix_ref, flat_ref, before_ref, after_ref, left_ref, right_ref,
    weight_ref, inverse_ref, child_ref, cwet_ref,
    send_ref, pmid_ref, own_ref, cmid_ref,
    explicit_ref, wide_ref, turn_ref, long_ref, d_ref,
):
    total, capacity, child_rows = child_ref.shape
    tracers, levels = mix_ref.shape[0], mix_ref.shape[1] + 1
    width = flat_ref.shape[0] // rows
    narrow = capacity // 3
    covered = child_rows // 3
    all_rows = strips * rows
    lane_tiles = (child_rows + LANES - 1) // LANES
    level_rows = (total + 7) // 8 * 8
    base = lane_tiles * level_rows
    member = lax.axis_index("child")
    starts = strip_starts(cols_ref, strips)
    last = 3 * my_strip(cols_ref, strips) - 1
    offset = offset_ref[0]

    has_before = (member > 0).astype(jnp.float32)
    has_after = (member < strips - 1).astype(jnp.float32)
    lane = lax.broadcasted_iota(jnp.int32, (rows, LANES), 1)
    for x in range(width):
        here = flat_ref[x * rows : (x + 1) * rows, :]
        west = left_ref[...] if x == 0 else flat_ref[(x - 1) * rows : x * rows, :]
        east = right_ref[...] if x == width - 1 else flat_ref[(x + 1) * rows : (x + 2) * rows, :]
        south = jnp.concatenate([has_before * before_ref[base + x : base + x + 1, :], here[:-1]], axis=0)
        north = jnp.concatenate([here[1:], has_after * after_ref[base + x : base + x + 1, :]], axis=0)
        wet = here[:, total : total + 1]
        laplace = north + south + east + west - 4.0 * here
        explicit_ref[x * rows : (x + 1) * rows, :] = wet * (here + diffusion * laplace)
    solved = jnp.dot(explicit_ref[...], inverse_ref[...], precision=HIGH, preferred_element_type=jnp.float32)
    flat_lane = lax.broadcasted_iota(jnp.int32, (width * rows, LANES), 1)
    wide_ref[: width * rows, :] = jnp.where(flat_lane == total, flat_ref[...], solved)
    wide_ref[width * rows :, :] = jnp.zeros((narrow * rows, LANES), jnp.float32)
    pmid_ref[...] = wide_ref[: width * rows, :]
    for j in range(strips):
        send_ref[j, : narrow * rows, :] = wide_ref[pl.ds(pl.multiple_of(starts[j] * rows, rows), narrow * rows), :]

    column = lax.broadcasted_iota(jnp.int32, (capacity, 1), 0)
    is_last = (column == last).astype(jnp.float32)
    mask = cwet_ref[...].astype(jnp.float32) * (column <= last).astype(jnp.float32)
    side = jnp.zeros((capacity, 1), jnp.float32)
    end = jnp.zeros((1, child_rows), jnp.float32)

    def edge(ref, l):
        parts = []
        for t in range(lane_tiles):
            stop = min(child_rows, (t + 1) * LANES)
            parts.append(ref[pl.ds(t * level_rows + l, 1), : stop - t * LANES])
        return jnp.concatenate(parts, axis=1)

    def explicit(l):
        begin = mask * child_ref[l]
        west = jnp.concatenate([edge(before_ref, l), begin[:-1]], axis=0)
        east = jnp.concatenate([begin[1:], end], axis=0) + is_last * edge(after_ref, l)
        south = jnp.concatenate([side, begin[:, :-1]], axis=1)
        north = jnp.concatenate([begin[:, 1:], side], axis=1)
        return mask * (begin + diffusion * (east + west + north + south - 4.0 * begin))

    def forward(k, carry):
        held = []
        for t in range(tracers):
            l = t * levels + k
            above = jnp.where(k > 0, mix_ref[t, jnp.maximum(k - 1, 0)], 0.0)
            d = (explicit(l) + above * carry[t]) * weight_ref[pl.ds(l, 1), :1]
            d_ref[l] = d
            held.append(d)
        return tuple(held)

    blank = jnp.zeros((capacity, child_rows), jnp.float32)
    lax.fori_loop(0, levels, forward, (blank,) * tracers)

    def backward(step, carry):
        k = levels - 1 - step
        held = []
        for t in range(tracers):
            l = t * levels + k
            below = jnp.where(k < levels - 1, mix_ref[t, jnp.minimum(k, levels - 2)], 0.0)
            x = d_ref[l] + (below * weight_ref[pl.ds(l, 1), :1]) * carry[t]
            for tile in range(lane_tiles):
                stop = min(child_rows, (tile + 1) * LANES)
                at = pl.ds(pl.multiple_of((tile * total + l) * ROWS, ROWS), capacity)
                cmid_ref[at, : stop - tile * LANES] = x[:, tile * LANES : stop]
            held.append(x)
        return tuple(held)

    lax.fori_loop(0, levels, backward, (blank,) * tracers)

    own_ref[...] = jnp.zeros_like(own_ref)
    turn_ref[...] = jnp.zeros_like(turn_ref)
    y = lax.broadcasted_iota(jnp.int32, (1, child_rows), 1)
    at_end = ((y == 0) | (y == child_rows - 1)).astype(jnp.float32)
    for q in range(narrow):
        for t in range(lane_tiles):
            stop = min(child_rows, (t + 1) * LANES)
            part = sum(
                cmid_ref[pl.ds(t * total * ROWS + 3 * q + dx, total, stride=ROWS), :] for dx in range(3)
            )
            turn_ref[:total, t * LANES : stop] = part[:, : stop - t * LANES]
        count = (mask[3 * q : 3 * q + 1] + mask[3 * q + 1 : 3 * q + 2] + mask[3 * q + 2 : 3 * q + 3]) * at_end
        turn_ref[total : total + 1, :child_rows] = count
        for t in range(lane_tiles):
            long_ref[t * LANES : (t + 1) * LANES, :] = turn_ref[:, t * LANES : (t + 1) * LANES].T
        mean = one_ninth * (
            long_ref[pl.ds(0, covered, stride=3), :]
            + long_ref[pl.ds(1, covered, stride=3), :]
            + long_ref[pl.ds(2, covered, stride=3), :]
        )
        own_ref[pl.ds(q * all_rows + offset, covered), :] = mean
    for k in range(strips):
        for q in range(narrow):
            send_ref[k, (narrow + q) * rows : (narrow + q + 1) * rows, :] = own_ref[
                q * all_rows + k * rows : q * all_rows + (k + 1) * rows, :
            ]


def finish_kernel(
    strips, rows, total,
    cols_ref, offset_ref, got_ref, own_ref, pmid_ref, inverse_ref, cmid_ref, cwet_ref,
    pnext_ref, cnext_ref,
    panel_ref, wide_ref, ends_ref, long_ref, add_ref, turn_ref, nat_ref,
):
    capacity, child_rows = cwet_ref.shape
    width = pmid_ref.shape[0] // rows
    narrow = capacity // 3
    covered = child_rows // 3
    all_rows = strips * rows
    lane_tiles = (child_rows + LANES - 1) // LANES
    padded = (narrow + 7) // 8 * 8
    member = lax.axis_index("child")
    starts = strip_starts(cols_ref, strips)
    last = 3 * my_strip(cols_ref, strips) - 1
    offset = offset_ref[0]

    ends_ref[...] = jnp.zeros_like(ends_ref)
    for q in range(narrow):
        for k in range(strips):
            panel_ref[q * all_rows + k * rows : q * all_rows + (k + 1) * rows, :] = got_ref[
                k, q * rows : (q + 1) * rows, :
            ]
        ends_ref[q : q + 1, :] = panel_ref[pl.ds(q * all_rows + offset, 1), :]
        ends_ref[padded + q : padded + q + 1, :] = panel_ref[pl.ds(q * all_rows + offset + covered - 1, 1), :]
    solved_ends = jnp.dot(ends_ref[...], inverse_ref[...], precision=HIGH, preferred_element_type=jnp.float32)
    f = lax.broadcasted_iota(jnp.int32, (covered, 1), 0)
    first_row = (f == 0).astype(jnp.float32)
    last_row = (f == covered - 1).astype(jnp.float32)
    long_ref[...] = jnp.zeros_like(long_ref)
    for q in range(narrow):
        low = solved_ends[q : q + 1]
        high = solved_ends[padded + q : padded + q + 1]
        panel = panel_ref[pl.ds(q * all_rows + offset, covered), :]
        mean = own_ref[pl.ds(q * all_rows + offset, covered), :]
        coarse = mean + diffusion * mean[:, total : total + 1] * (first_row * low + last_row * high)
        gap = nudging * (panel - coarse)
        for dy in range(3):
            long_ref[pl.ds(dy, covered, stride=3), :] = gap
        long_ref[0:1, :] = long_ref[0:1, :] + diffusion * low
        long_ref[child_rows - 1 : child_rows, :] = long_ref[child_rows - 1 : child_rows, :] + diffusion * high
        for t in range(lane_tiles):
            turned = long_ref[t * LANES : (t + 1) * LANES, :].T
            for dx in range(3):
                add_ref[pl.ds(t * total * ROWS + 3 * q + dx, total, stride=ROWS), :] = turned[:total]
    column = lax.broadcasted_iota(jnp.int32, (capacity, 1), 0)
    mask = cwet_ref[...].astype(jnp.float32) * (column <= last).astype(jnp.float32)

    def write(l, carry):
        for t in range(lane_tiles):
            stop = min(child_rows, (t + 1) * LANES)
            at = pl.ds(pl.multiple_of((t * total + l) * ROWS, ROWS), capacity)
            lanes = slice(t * LANES, stop)
            size = stop - t * LANES
            cnext_ref[l, :, lanes] = mask[:, lanes] * (cmid_ref[at, :size] + add_ref[at, :size])
        return carry

    lax.fori_loop(0, total, write, 0)

    for j in range(strips):
        wide_ref[pl.ds(pl.multiple_of(starts[j] * rows, rows), narrow * rows), :] = got_ref[j, narrow * rows :, :]
    mean = wide_ref[: width * rows, :]
    twice = jnp.dot(pmid_ref[...], inverse_ref[...], precision=HIGH, preferred_element_type=jnp.float32)
    coarse = mean + diffusion * mean[:, total : total + 1] * twice
    row = member * rows + lax.broadcasted_iota(jnp.int32, (width * rows, 1), 0) % rows
    inside = (row >= offset) & (row < offset + covered)
    turn_ref[: width * rows, :] = pmid_ref[:, total : total + 1] * jnp.where(inside, coarse, pmid_ref[...])
    turn_ref[width * rows :, :] = jnp.zeros((turn_ref.shape[0] - width * rows, LANES), jnp.float32)
    for r in range(rows):
        turned = turn_ref[pl.ds(r, LANES, stride=rows), :].T
        nat_ref[pl.ds(r, LANES, stride=rows), :] = turned
    pnext_ref[...] = nat_ref[: total * rows, :width]


def body(parent_tracer, child_tracer, strip_cols, row_offset, parent_wet, child_wet, vert_mix):
    tracers, levels, rows, width = parent_tracer.shape
    capacity, child_rows = child_wet.shape
    strips = lax.axis_size("child")
    total = tracers * levels
    narrow = capacity // 3
    all_rows = rows * strips
    lane_tiles = (child_rows + LANES - 1) // LANES
    level_rows = (total + 7) // 8 * 8
    message = lane_tiles * level_rows + width
    f32 = lambda *s: jax.ShapeDtypeStruct(s, jnp.float32)
    mem = lambda *s: pltpu.VMEM(s, jnp.float32)
    parent_flat = parent_tracer.reshape(total * rows, width)
    child_flat = child_tracer.reshape(total, capacity, child_rows)

    flat, forth, back, left_edge, right_edge = pl.pallas_call(
        functools.partial(prepare_kernel, strips),
        in_specs=[SM, VM, VM, VM, VM],
        out_specs=[VM] * 5,
        out_shape=[
            f32(width * rows, LANES), f32(message, LANES), f32(message, LANES), f32(rows, LANES), f32(rows, LANES),
        ],
        scratch_shapes=[mem(LANES * rows, LANES)],
        compiler_params=params(24),
        name="prepare",
    )(strip_cols, parent_flat, parent_wet, child_flat, child_wet)

    groups = lax.axis_size("parent")
    devices = groups * strips
    right_edge = lax.ppermute(right_edge, "parent", [(i, i + 1) for i in range(groups - 1)])
    left_edge = lax.ppermute(left_edge, "parent", [(i + 1, i) for i in range(groups - 1)])
    forth = lax.ppermute(forth, ("parent", "child"), [(i, i + 1) for i in range(devices - 1)])
    back = lax.ppermute(back, ("parent", "child"), [(i + 1, i) for i in range(devices - 1)])

    weights, inverse = pl.pallas_call(
        coefficient_kernel,
        in_specs=[SM],
        out_specs=[VM, VM],
        out_shape=[f32(level_rows, LANES), f32(LANES, LANES)],
        scratch_shapes=[mem(8 * levels, LANES), mem(8 * levels, LANES)],
        compiler_params=params(8),
        name="coefficients",
    )(vert_mix)

    send, parent_mid, own, child_mid = pl.pallas_call(
        functools.partial(solve_kernel, strips, rows),
        in_specs=[SM, SM, SM] + [VM] * 9,
        out_specs=[VM] * 4,
        out_shape=[
            f32(strips, 2 * narrow * rows, LANES),
            f32(width * rows, LANES),
            f32(narrow * all_rows, LANES),
            f32(lane_tiles * total * ROWS, LANES),
        ],
        scratch_shapes=[
            mem(width * rows, LANES),
            mem((width + narrow) * rows, LANES),
            mem(LANES, lane_tiles * LANES),
            mem(lane_tiles * LANES, LANES),
            mem(total, capacity, child_rows),
        ],
        compiler_params=params(40),
        name="solve",
    )(
        strip_cols, row_offset, vert_mix, flat, forth, back, right_edge, left_edge,
        weights, inverse, child_flat, child_wet,
    )

    got = lax.all_to_all(send, "child", 0, 0)

    turn_rows = max(width, LANES) * rows
    parent_next, child_next = pl.pallas_call(
        functools.partial(finish_kernel, strips, rows, total),
        in_specs=[SM, SM] + [VM] * 6,
        out_specs=[VM, VM],
        out_shape=[f32(total * rows, width), f32(total, capacity, child_rows)],
        scratch_shapes=[
            mem(narrow * all_rows, LANES),
            mem((width + narrow) * rows, LANES),
            mem(2 * ((narrow + 7) // 8 * 8), LANES),
            mem(lane_tiles * LANES, LANES),
            mem(lane_tiles * total * ROWS, LANES),
            mem(turn_rows, LANES),
            mem(LANES * rows, LANES),
        ],
        compiler_params=params(40),
        name="finish",
    )(strip_cols, row_offset, got, own, parent_mid, inverse, child_mid, child_wet)
    return parent_next.reshape(parent_tracer.shape), child_next.reshape(child_tracer.shape)


def solution(mesh):
    return jax.shard_map(
        body,
        mesh=mesh,
        in_specs=(
            P(None, None, "child", "parent"),
            P(None, None, ("parent", "child"), None),
            P(),
            P(),
            P("child", "parent"),
            P(("parent", "child"), None),
            P(),
        ),
        out_specs=(P(None, None, "child", "parent"), P(None, None, ("parent", "child"), None)),
        check_vma=False,
    )
```

profile of v0, /device:TPU:0, one launch (start us, length us, event | category | flops | bytes accessed | tf_op | source)
XLA Modules:
  0.0 62.9 jit_solution(987090507783456517)
XLA Ops:
  0.6 0.0 copy-start.1
  0.6 0.0 copy-start.2
  0.7 0.0 copy-start.3
  0.7 1.3 %copy.9 = f32[2,50,8,48]{3,2,1,0:T(8,128)S(1)} copy(f32[2,50,8,48]{1,3,2,0:T(8,128)} %param.7) | data formatting | bytes 307200 | tf_op args[0]
  1.9 2.2 %copy.10 = f32[2,50,27,144]{3,2,1,0:T(8,128)S(1)} copy(f32[2,50,27,144]{3,0,2,1:T(2,128)} %param.8) | data formatting | bytes 3110400 | tf_op args[1]
  4.2 0.0 copy-start.4
  4.2 0.0 copy-done.1
  4.2 0.0 copy-done.2
  4.2 0.0 copy-done.3
  4.2 0.9 %prepare.1 = (f32[384,128]{1,0:T(8,128)S(1)}, f32[256,128]{1,0:T(8,128)S(1)}, f32[256,128]{1,0:T(8,128)S(1)}, f32[8,128]{1,0:T(8,128)S(1)}, f32[8,128]{1,0:T(8,128)S(1)}) custom-call(s32[4,8]{1,0:T(4,128)S(1)} %copy-done.2, f32[800,48]{1,0:T(8,128)S(1)} %bitcast.7, s32[8,48]{1,0:T(8,128)S(1)} %copy-done.3, f32[100,27,144]{2,1,0:T(8,128)S(1)} %bitcast.4, ...), custom_call_target="tpu_custom_call" | custom-call | tf_op jit(solution)/shard_map/prepare/pallas_call | solution.py:317
  5.1 4.9 %collective-permute-start = (f32[256,128]{1,0:T(8,128)S(1)}, f32[256,128]{1,0:T(8,128)S(1)}, u32[]{:S(2)}, u32[]{:S(2)}) collective-permute-start(f32[256,128]{1,0:T(8,128)S(1)} %get-tuple-element.16), channel_id=1, source_target_pairs={{0,1},{1,2},{2,3},{3,4},{4,5},{5,6},{6,7},{7,8},{8,9},{9,10},{10,1... | collective-permute-start | bytes 393224 | tf_op jit(solution)/shard_map/ppermute | solution.py:333
  10.0 1.3 %collective-permute-start.1 = (f32[256,128]{1,0:T(8,128)S(1)}, f32[256,128]{1,0:T(8,128)S(1)}, u32[]{:S(2)}, u32[]{:S(2)}) collective-permute-start(f32[256,128]{1,0:T(8,128)S(1)} %get-tuple-element.17), channel_id=1, source_target_pairs={{1,0},{2,1},{3,2},{4,3},{5,4},{6,5},{7,6},{8,7},{9,8},{10,9},{11,1... | collective-permute-start | bytes 393224 | tf_op jit(solution)/shard_map/ppermute | solution.py:334
  11.3 5.7 %collective-permute-start.2 = (f32[8,128]{1,0:T(8,128)S(1)}, f32[8,128]{1,0:T(8,128)S(1)}, u32[]{:S(2)}, u32[]{:S(2)}) collective-permute-start(f32[8,128]{1,0:T(8,128)S(1)} %get-tuple-element.18), channel_id=1, source_target_pairs={{0,8},{8,16},{16,24},{1,9},{9,17},{17,25},{2,10},{10,18},{18,26},{... | collective-permute-start | bytes 12296 | tf_op jit(solution)/shard_map/ppermute | solution.py:331
  17.0 1.3 %collective-permute-start.3 = (f32[8,128]{1,0:T(8,128)S(1)}, f32[8,128]{1,0:T(8,128)S(1)}, u32[]{:S(2)}, u32[]{:S(2)}) collective-permute-start(f32[8,128]{1,0:T(8,128)S(1)} %get-tuple-element.19), channel_id=1, source_target_pairs={{8,0},{16,8},{24,16},{9,1},{17,9},{25,17},{10,2},{18,10},{26,18},{... | collective-permute-start | bytes 12296 | tf_op jit(solution)/shard_map/ppermute | solution.py:332
  18.9 0.0 copy-done.4
  19.0 1.1 %coefficients.1 = (f32[104,128]{1,0:T(8,128)S(1)}, f32[128,128]{1,0:T(8,128)S(1)}) custom-call(f32[2,49]{1,0:T(2,128)S(1)} %copy-done.4), custom_call_target="tpu_custom_call" | custom-call | tf_op jit(solution)/shard_map/coefficients/pallas_call | solution.py:336
  20.1 0.0 collective-permute-done.2.left_ref
  20.1 1.8 %collective-permute-done.3.right_ref = f32[8,128]{1,0:T(8,128)S(1)} collective-permute-done((f32[8,128]{1,0:T(8,128)S(1)}, f32[8,128]{1,0:T(8,128)S(1)}, u32[]{:S(2)}, u32[]{:S(2)}) %collective-permute-start.3) | collective-permute-done | bytes 4128 | tf_op jit(solution)/shard_map/ppermute | solution.py:332
  21.8 0.0 collective-permute-done.before_ref
  21.8 0.0 collective-permute-done.1.after_ref
  21.8 11.3 %solve.1 = (f32[8,144,128]{2,1,0:T(8,128)S(1)}, f32[384,128]{1,0:T(8,128)S(1)}, f32[576,128]{1,0:T(8,128)S(1)}, f32[6400,128]{1,0:T(8,128)S(1)}) custom-call(s32[4,8]{1,0:T(4,128)S(1)} %copy-done.2, s32[1]{0:T(128)S(6)} %copy.13.offset_ref, f32[2,49]{1,0:T(2,128)S(1)} %copy-done.4, f32[384,128]{1,0:T(8,128)S(1)} %get-tuple-element.15.flat_ref, ...), custom_call_target="tpu_custom_call" | custom-call | tf_op jit(solution)/shard_map/solve/pallas_call | solution.py:346
  33.2 19.0 %all_to_all.5.got_ref = f32[8,144,128]{2,1,0:T(8,128)S(1)} all-to-all(f32[8,144,128]{2,1,0:T(8,128)S(1)} %get-tuple-element.22), channel_id=1, replica_groups=mesh['parent'=4,'child'=8] {'child'}, dimensions={0} | all-to-all | bytes 1179648 | tf_op jit(solution)/shard_map/all_to_all | solution.py:370
  52.2 4.1 %finish.1 = (f32[800,48]{1,0:T(8,128)S(1)}, f32[100,27,144]{2,1,0:T(8,128)S(1)}) custom-call(s32[4,8]{1,0:T(4,128)S(1)} %copy-done.2, s32[1]{0:T(128)S(6)} %copy.13.offset_ref, f32[8,144,128]{2,1,0:T(8,128)S(1)} %all_to_all.5.got_ref, f32[576,128]{1,0:T(8,128)S(1)} %get-tuple-element.23.own_ref, f32[384,128]{1,0:T(8,128)S(1)} %get-tuple-element.24.pmid_ref, ...), custom_call_target="tpu_custom_call" | custom-call | tf_op jit(solution)/shard_map/finish/pallas_call | solution.py:373
  56.2 0.0 copy-start
  56.3 0.7 %copy-done = f32[800,48]{1,0:T(8,128)} copy-done((f32[800,48]{1,0:T(8,128)}, f32[800,48]{1,0:T(8,128)S(1)}, u32[]{:S(2)}) %copy-start) | copy-done | bytes 153624
  57.0 2.0 %copy.11 = f32[2,50,8,48]{1,3,2,0:T(8,128)} copy(f32[2,50,8,48]{3,2,1,0:T(8,128)} %bitcast.8) | data formatting | bytes 307200
  59.0 3.9 %copy.12 = f32[2,50,27,144]{3,0,2,1:T(2,128)} copy(f32[2,50,27,144]{3,2,1,0:T(8,128)S(1)} %bitcast.6) | data formatting | bytes 3110400
Async XLA Ops:
  0.6 3.5 %copy-start.1 = (s32[27,144]{1,0:T(8,128)S(1)}, s32[27,144]{1,0:T(8,128)}, u32[]{:S(2)}) copy-start(s32[27,144]{1,0:T(8,128)} %cwet_ref.5) | copy-start | bytes 46660
  0.6 3.5 %copy-start.2 = (s32[4,8]{1,0:T(4,128)S(1)}, s32[4,8]{1,0:T(4,128)}, u32[]{:S(2)}) copy-start(s32[4,8]{1,0:T(4,128)} %cols_ref.5) | copy-start | bytes 388
  0.7 3.5 %copy-start.3 = (s32[8,48]{1,0:T(8,128)S(1)}, s32[8,48]{1,0:T(8,128)}, u32[]{:S(2)}) copy-start(s32[8,48]{1,0:T(8,128)} %pwet_ref.1) | copy-start | bytes 4612
  4.2 14.8 %copy-start.4 = (f32[2,49]{1,0:T(2,128)S(1)}, f32[2,49]{1,0:T(2,128)}, u32[]{:S(2)}) copy-start(f32[2,49]{1,0:T(2,128)} %mix_ref.3) | copy-start | bytes 1180
  5.1 16.7 %collective-permute-start = (f32[256,128]{1,0:T(8,128)S(1)}, f32[256,128]{1,0:T(8,128)S(1)}, u32[]{:S(2)}, u32[]{:S(2)}) collective-permute-start(f32[256,128]{1,0:T(8,128)S(1)} %get-tuple-element.16), channel_id=1, source_target_pairs={{0,1},{1,2},{2,3},{3,4},{4,5},{5,6},{6,7},{7,8},{8,9},{9,10},{10,1... | collective-permute-start | bytes 393224 | tf_op jit(solution)/shard_map/ppermute | solution.py:333
  10.0 11.8 %collective-permute-start.1 = (f32[256,128]{1,0:T(8,128)S(1)}, f32[256,128]{1,0:T(8,128)S(1)}, u32[]{:S(2)}, u32[]{:S(2)}) collective-permute-start(f32[256,128]{1,0:T(8,128)S(1)} %get-tuple-element.17), channel_id=1, source_target_pairs={{1,0},{2,1},{3,2},{4,3},{5,4},{6,5},{7,6},{8,7},{9,8},{10,9},{11,1... | collective-permute-start | bytes 393224 | tf_op jit(solution)/shard_map/ppermute | solution.py:334
  11.3 8.8 %collective-permute-start.2 = (f32[8,128]{1,0:T(8,128)S(1)}, f32[8,128]{1,0:T(8,128)S(1)}, u32[]{:S(2)}, u32[]{:S(2)}) collective-permute-start(f32[8,128]{1,0:T(8,128)S(1)} %get-tuple-element.18), channel_id=1, source_target_pairs={{0,8},{8,16},{16,24},{1,9},{9,17},{17,25},{2,10},{10,18},{18,26},{... | collective-permute-start | bytes 12296 | tf_op jit(solution)/shard_map/ppermute | solution.py:331
  17.0 4.8 %collective-permute-start.3 = (f32[8,128]{1,0:T(8,128)S(1)}, f32[8,128]{1,0:T(8,128)S(1)}, u32[]{:S(2)}, u32[]{:S(2)}) collective-permute-start(f32[8,128]{1,0:T(8,128)S(1)} %get-tuple-element.19), channel_id=1, source_target_pairs={{8,0},{16,8},{24,16},{9,1},{17,9},{25,17},{10,2},{18,10},{26,18},{... | collective-permute-start | bytes 12296 | tf_op jit(solution)/shard_map/ppermute | solution.py:332
  56.2 0.8 %copy-start = (f32[800,48]{1,0:T(8,128)}, f32[800,48]{1,0:T(8,128)S(1)}, u32[]{:S(2)}) copy-start(f32[800,48]{1,0:T(8,128)S(1)} %get-tuple-element.26) | copy-start | bytes 460804
where the time goes:
time: 64 us; the launch traced here: 62.9 us
  blocking collectives  19 us (30%)
  Pallas kernels  17.4 us (27%)
  starting transfers between devices  13.1 us (20%)
  local copies, waits for them, and re-layouts  10.2 us (16%)
  waiting for transfers between devices  1.76 us (3%)
  between operations  1.43 us (2%)
    all_to_all x1, blocking collectives, body(): got = lax.all_to_all(send, 'child', 0, 0)  19 us
    pallas_call x1, Pallas kernels, body(): pl.pallas_call(functools.partial(solve_kernel, strips, rows), in_specs=[S...  11.3 us
    unnamed x14, local copies, waits for them, and re-layouts  10.2 us
    ppermute x1, starting transfers between devices, body(): lax.ppermute(right_edge, 'parent', [(i, i + 1) for i in range(groups - 1)])  5.68 us
    ppermute x1, starting transfers between devices, body(): lax.ppermute(forth, ('parent', 'child'), [(i, i + 1) for i in range(devic...  4.88 us
    pallas_call x1, Pallas kernels, body(): pl.pallas_call(functools.partial(finish_kernel, strips, rows, total), in_...  4.08 us
    ppermute x1, waiting for transfers between devices, body(): lax.ppermute(left_edge, 'parent', [(i + 1, i) for i in range(groups - 1)])  1.75 us
    ppermute x1, starting transfers between devices, body(): lax.ppermute(back, ('parent', 'child'), [(i + 1, i) for i in range(device...  1.29 us
  transfers between devices with their start and end apart: 4, of which 1 were waited for; matrix products, arithmetic and copies ran while one was open for 0% of the time, Pallas kernels for 2%

commit v1 on v0

v1 whole, which is shorter than its diff:
```python
import functools

import jax
import jax.numpy as jnp
from jax import lax
from jax.experimental import pallas as pl
from jax.experimental.pallas import tpu as pltpu
from jax.sharding import PartitionSpec as P

diffusion = 0.2
nudging = 0.5
one_ninth = 1.0 / 9.0
LANES = 128
HIGH = lax.Precision.HIGHEST

VM = pl.BlockSpec(memory_space=pltpu.VMEM)
SM = pl.BlockSpec(memory_space=pltpu.SMEM)


def params(mib):
    return pltpu.CompilerParams(vmem_limit_bytes=mib << 20)


def up(n, m):
    return (n + m - 1) // m * m


def tile_list(child_rows):
    return [(t, min(LANES, child_rows - t * LANES)) for t in range((child_rows + LANES - 1) // LANES)]


def my_cols(cols_ref):
    return cols_ref[lax.axis_index("parent"), lax.axis_index("child")]


def strip_starts(cols_ref, strips):
    group = lax.axis_index("parent")
    start = jnp.int32(0)
    starts = []
    for j in range(strips):
        starts.append(start)
        start = start + cols_ref[group, j]
    return starts


def coefficient_kernel(mix_ref, weight_ref, carry_ref, back_ref, inverse_ref, d_ref, c_ref):
    tracers, levels = mix_ref.shape[0], mix_ref.shape[1] + 1
    slot = LANES // tracers
    lane = lax.broadcasted_iota(jnp.int32, (8, LANES), 1)
    by_lane = lane // slot
    by_row = lax.broadcasted_iota(jnp.int32, (8, LANES), 0) % tracers
    none = jnp.zeros((8, LANES), jnp.float32)

    def mixed(k, which):
        row = none
        if 0 <= k < levels - 1:
            for t in range(tracers):
                row = jnp.where(which == t, mix_ref[t, k], row)
        return row

    weights = [none, none]
    d = none
    for k in range(levels):
        for n, which in enumerate((by_row, by_lane)):
            above, below = mixed(k - 1, which), mixed(k, which)
            w = 1.0 / (1.0 + above + below - above * (above * weights[n]))
            weights[n] = w
            at = pl.ds(8 * k, 8)
            if n == 0:
                weight_ref[at, :] = w
                carry_ref[at, :] = above * w
                back_ref[at, :] = below * w
            else:
                unit = (lane - which * slot == k).astype(jnp.float32)
                d = (unit + above * d) * w
                d_ref[at, :] = d
                c_ref[at, :] = below * w
    inverse_ref[...] = jnp.zeros_like(inverse_ref)
    x = none
    for k in reversed(range(levels)):
        x = d_ref[pl.ds(8 * k, 8), :] + c_ref[pl.ds(8 * k, 8), :] * x
        for t in range(tracers):
            inverse_ref[t * slot + k : t * slot + k + 1, :] = jnp.where(by_lane == t, x, 0.0)[:1]


def prepare_kernel(
    cols_ref, parent_ref, pwet_ref, child_ref, cwet_ref,
    flat_ref, forth_ref, back_ref, left_ref, right_ref, turn_ref, row_ref,
):
    levels, capacity, tracers, child_rows = child_ref.shape
    rows, width = pwet_ref.shape
    slot = LANES // tracers
    level_rows = up(tracers * levels, 8)
    tiles = tile_list(child_rows)
    turn_ref[:rows, :width] = pwet_ref[...].astype(jnp.float32)
    row_ref[...] = jnp.zeros_like(row_ref)
    wet = turn_ref[...].T
    for r in range(rows):
        cell = wet[:width, r : r + 1]
        for t in range(tracers):
            row_ref[r, :, t * slot : t * slot + levels] = cell * parent_ref[t, r]
        row_ref[r, :, levels : levels + 1] = cell
        flat_ref[pl.ds(r, width, stride=rows), :] = row_ref[r]
    left_ref[...] = flat_ref[:rows, :]
    right_ref[...] = flat_ref[(width - 1) * rows :, :]
    flat_child = child_ref.reshape(levels * capacity * tracers, child_rows)
    last = 3 * my_cols(cols_ref) - 1
    base = len(tiles) * level_rows
    for ref, x, r in ((forth_ref, last, rows - 1), (back_ref, 0, 0)):
        cell = cwet_ref[pl.ds(x, 1), :].astype(jnp.float32)
        for l in range(levels):
            pair = flat_child[pl.ds(pl.multiple_of((l * capacity + x) * tracers, tracers), tracers), :] * cell
            for n, size in tiles:
                at = n * level_rows + l * tracers
                ref[at : at + tracers, :size] = pair[:, n * LANES : n * LANES + size]
        ref[base : base + width, :] = row_ref[r]


def masks(cols_ref, cwet_ref, mask_ref, tracers):
    capacity, child_rows = cwet_ref.shape
    column = lax.broadcasted_iota(jnp.int32, (capacity, 1), 0)
    mask = cwet_ref[...].astype(jnp.float32) * (column < 3 * my_cols(cols_ref)).astype(jnp.float32)
    mask_ref[...] = jnp.zeros_like(mask_ref)
    for n, size in tile_list(child_rows):
        part = mask[:, n * LANES : n * LANES + size]
        if size < LANES:
            part = jnp.concatenate([part, jnp.zeros((capacity, LANES - size), jnp.float32)], axis=1)
        for t in range(tracers):
            mask_ref[n, pl.ds(t, capacity, stride=tracers), :] = part
    return mask


def solve_kernel(
    strips, rows,
    cols_ref, offset_ref, flat_ref, before_ref, after_ref, left_ref, right_ref,
    weight_ref, carry_ref, back_ref, inverse_ref, child_ref, cwet_ref,
    send_ref, pmid_ref, own_ref, cmid_ref,
    explicit_ref, wide_ref, mask_ref, begin_ref, d_ref, turn_ref, end_ref, long_ref,
):
    levels, capacity, tracers, child_rows = child_ref.shape
    slot = LANES // tracers
    width = flat_ref.shape[0] // rows
    narrow = capacity // 3
    covered = child_rows // 3
    all_rows = strips * rows
    tiles = tile_list(child_rows)
    level_rows = up(tracers * levels, 8)
    base = len(tiles) * level_rows
    live = capacity * tracers
    stored = up(live, 8)
    stride = begin_ref.shape[1] // levels
    member = lax.axis_index("child")
    starts = strip_starts(cols_ref, strips)
    offset = offset_ref[0]

    has_before = (member > 0).astype(jnp.float32)
    has_after = (member < strips - 1).astype(jnp.float32)
    for x in range(width):
        here = flat_ref[x * rows : (x + 1) * rows, :]
        west = left_ref[...] if x == 0 else flat_ref[(x - 1) * rows : x * rows, :]
        east = right_ref[...] if x == width - 1 else flat_ref[(x + 1) * rows : (x + 2) * rows, :]
        south = jnp.concatenate([has_before * before_ref[base + x : base + x + 1, :], here[:-1]], axis=0)
        north = jnp.concatenate([here[1:], has_after * after_ref[base + x : base + x + 1, :]], axis=0)
        wet = here[:, levels : levels + 1]
        laplace = north + south + east + west - 4.0 * here
        explicit_ref[x * rows : (x + 1) * rows, :] = wet * (here + diffusion * laplace)
    solved = jnp.dot(explicit_ref[...], inverse_ref[...], precision=HIGH, preferred_element_type=jnp.float32)
    lane = lax.broadcasted_iota(jnp.int32, (width * rows, LANES), 1)
    solved = jnp.where(lane == levels, flat_ref[...], solved)
    wide_ref[: width * rows, :] = solved
    wide_ref[width * rows :, :] = jnp.zeros((narrow * rows, LANES), jnp.float32)
    pmid_ref[...] = solved
    for j in range(strips):
        send_ref[j, : narrow * rows, :] = wide_ref[pl.ds(pl.multiple_of(starts[j] * rows, rows), narrow * rows), :]

    mask = masks(cols_ref, cwet_ref, mask_ref, tracers)
    flat_child = child_ref.reshape(levels * live, child_rows)
    lane = lax.broadcasted_iota(jnp.int32, (stored, LANES), 1)
    past = 8 + 3 * tracers * my_cols(cols_ref)
    for n, size in tiles:
        if size < LANES:
            begin_ref[n] = jnp.zeros((levels * stride, LANES), jnp.float32)

    def begin(l, carry):
        cells = flat_child[pl.ds(pl.multiple_of(l * live, 2), live), :]
        start = pl.multiple_of(l * stride, 8)
        for n, size in tiles:
            part = cells[:, n * LANES : n * LANES + size] * mask_ref[n, :live, :size]
            begin_ref[n, pl.ds(start + 8, live), :size] = part
            edge = pl.ds(n * level_rows + l * tracers, tracers)
            begin_ref[n, pl.ds(start + 8 - tracers, tracers), :size] = before_ref[edge, :size]
            begin_ref[n, pl.ds(start + past, tracers), :size] = after_ref[edge, :size]
        return carry

    lax.fori_loop(0, levels, begin, 0, unroll=2)

    def by_rows(factor, value):
        return (factor[None] * value.reshape(stored // 8, 8, LANES)).reshape(stored, LANES)

    def forward(l, carry):
        start = pl.multiple_of(l * stride, 8)
        coef = pl.ds(pl.multiple_of(l * 8, 8), 8)
        cells = [begin_ref[n, pl.ds(start + 8, stored), :] for n, _ in tiles]
        lower = [pltpu.roll(c, 1, 1) for c in cells]
        upper = [pltpu.roll(c, LANES - 1, 1) for c in cells]
        held = []
        for n, size in tiles:
            south = jnp.where(lane == 0, lower[n - 1] if n else 0.0, lower[n])
            if n + 1 < len(tiles):
                north = jnp.where(lane == LANES - 1, upper[n + 1], upper[n])
            else:
                north = jnp.where(lane == size - 1, 0.0, upper[n])
            west = begin_ref[n, pl.ds(start + 8 - tracers, stored), :]
            east = begin_ref[n, pl.ds(start + 8 + tracers, stored), :]
            explicit = (diffusion * mask_ref[n]) * (cells[n] + west + east + south + north)
            d = by_rows(weight_ref[coef, :], explicit) + by_rows(carry_ref[coef, :], carry[n])
            d_ref[n, pl.ds(pl.multiple_of(l * stored, 8), stored), :] = d
            held.append(d)
        return tuple(held)

    blank = jnp.zeros((stored, LANES), jnp.float32)
    lax.fori_loop(0, levels, forward, (blank,) * len(tiles), unroll=2)

    def backward(step, carry):
        l = levels - 1 - step
        coef = pl.ds(pl.multiple_of(l * 8, 8), 8)
        at = pl.ds(pl.multiple_of(l * stored, 8), stored)
        held = []
        for n, _ in tiles:
            x = d_ref[n, at, :] + by_rows(back_ref[coef, :], carry[n])
            cmid_ref[n, at, :] = x
            held.append(x)
        return tuple(held)

    lax.fori_loop(0, levels, backward, (blank,) * len(tiles), unroll=2)

    own_ref[...] = jnp.zeros_like(own_ref)
    turn_ref[...] = jnp.zeros_like(turn_ref)
    end_ref[...] = jnp.zeros_like(end_ref)
    y = lax.broadcasted_iota(jnp.int32, (1, child_rows), 1)
    at_end = ((y == 0) | (y == child_rows - 1)).astype(jnp.float32)
    tail, tail_size = tiles[-1]
    packs = LANES // tail_size
    for q in range(narrow):
        count = (mask[3 * q : 3 * q + 1] + mask[3 * q + 1 : 3 * q + 2] + mask[3 * q + 2 : 3 * q + 3]) * at_end
        for n, size in tiles:
            into, low = (turn_ref, 0) if n < tail else (end_ref.at[q // packs], (q % packs) * size)
            for t in range(tracers):
                part = sum(
                    cmid_ref[n, pl.ds((3 * q + dx) * tracers + t, levels, stride=stored), :] for dx in range(3)
                )
                into[t * slot : t * slot + levels, low : low + size] = part[:, :size]
            into[levels : levels + 1, low : low + size] = count[:, n * LANES : n * LANES + size]
            if n < tail:
                long_ref[q * child_rows + n * LANES : q * child_rows + n * LANES + size, :] = turn_ref[...].T
    for part in range((narrow + packs - 1) // packs):
        turned = end_ref[part].T
        for q in range(part * packs, min(narrow, (part + 1) * packs)):
            low = (q % packs) * tail_size
            high = (q + 1) * child_rows
            long_ref[high - tail_size : high, :] = turned[low : low + tail_size]
    for q in range(narrow):
        mean = one_ninth * (
            long_ref[pl.ds(q * child_rows, covered, stride=3), :]
            + long_ref[pl.ds(q * child_rows + 1, covered, stride=3), :]
            + long_ref[pl.ds(q * child_rows + 2, covered, stride=3), :]
        )
        own_ref[pl.ds(q * all_rows + offset, covered), :] = mean
    for k in range(strips):
        for q in range(narrow):
            send_ref[k, (narrow + q) * rows : (narrow + q + 1) * rows, :] = own_ref[
                q * all_rows + k * rows : q * all_rows + (k + 1) * rows, :
            ]


def finish_kernel(
    strips, rows,
    cols_ref, offset_ref, got_ref, own_ref, pmid_ref, inverse_ref, cmid_ref, cwet_ref,
    pnext_ref, cnext_ref,
    panel_ref, wide_ref, ends_ref, long_ref, end_ref, add_ref, mask_ref, next_ref,
):
    levels, capacity, tracers, child_rows = cnext_ref.shape
    slot = LANES // tracers
    width = pmid_ref.shape[0] // rows
    narrow = capacity // 3
    covered = child_rows // 3
    all_rows = strips * rows
    tiles = tile_list(child_rows)
    live = capacity * tracers
    stored = up(live, 8)
    padded = up(narrow, 8)
    member = lax.axis_index("child")
    starts = strip_starts(cols_ref, strips)
    offset = offset_ref[0]
    masks(cols_ref, cwet_ref, mask_ref, tracers)

    ends_ref[...] = jnp.zeros_like(ends_ref)
    for q in range(narrow):
        for k in range(strips):
            panel_ref[q * all_rows + k * rows : q * all_rows + (k + 1) * rows, :] = got_ref[
                k, q * rows : (q + 1) * rows, :
            ]
        ends_ref[q : q + 1, :] = panel_ref[pl.ds(q * all_rows + offset, 1), :]
        ends_ref[padded + q : padded + q + 1, :] = panel_ref[pl.ds(q * all_rows + offset + covered - 1, 1), :]
    solved_ends = jnp.dot(ends_ref[...], inverse_ref[...], precision=HIGH, preferred_element_type=jnp.float32)
    f = lax.broadcasted_iota(jnp.int32, (covered, 1), 0)
    first_row = (f == 0).astype(jnp.float32)
    last_row = (f == covered - 1).astype(jnp.float32)
    tail, tail_size = tiles[-1]
    packs = LANES // tail_size

    def spread(turned, n, q):
        for t in range(tracers):
            part = turned[t * slot : t * slot + levels]
            for dx in range(3):
                add_ref[n, pl.ds((3 * q + dx) * tracers + t, levels, stride=stored), :] = part

    for q in range(narrow):
        low = solved_ends[q : q + 1]
        high = solved_ends[padded + q : padded + q + 1]
        panel = panel_ref[pl.ds(q * all_rows + offset, covered), :]
        mean = own_ref[pl.ds(q * all_rows + offset, covered), :]
        coarse = mean + diffusion * mean[:, levels : levels + 1] * (first_row * low + last_row * high)
        gap = nudging * (panel - coarse)
        base = q * child_rows
        for dy in range(3):
            long_ref[pl.ds(base + dy, covered, stride=3), :] = gap
        long_ref[base : base + 1, :] = gap[:1] + diffusion * low
        long_ref[base + child_rows - 1 : base + child_rows, :] = gap[covered - 1 :] + diffusion * high
        for n, size in tiles[:-1]:
            spread(long_ref[base + n * LANES : base + n * LANES + size, :].T, n, q)
        at = (q % packs) * tail_size
        end_ref[q // packs, at : at + tail_size, :] = long_ref[base + child_rows - tail_size : base + child_rows, :]
    for part in range((narrow + packs - 1) // packs):
        turned = end_ref[part].T
        for q in range(part * packs, min(narrow, (part + 1) * packs)):
            shift = (q % packs) * tail_size
            spread(pltpu.roll(turned, (LANES - shift) % LANES, 1) if shift else turned, tail, q)

    flat_next = cnext_ref.reshape(levels * live, child_rows)

    def write(l, carry):
        at = pl.ds(pl.multiple_of(l * stored, 8), live)
        parts = [
            (mask_ref[n, :live, :] * (cmid_ref[n, at, :] + add_ref[n, at, :]))[:, :size] for n, size in tiles
        ]
        flat_next[pl.ds(pl.multiple_of(l * live, 2), live), :] = jnp.concatenate(parts, axis=1)
        return carry

    lax.fori_loop(0, levels, write, 0, unroll=2)

    for j in range(strips):
        wide_ref[pl.ds(pl.multiple_of(starts[j] * rows, rows), narrow * rows), :] = got_ref[j, narrow * rows :, :]
    mean = wide_ref[: width * rows, :]
    pmid = pmid_ref[...]
    twice = jnp.dot(pmid, inverse_ref[...], precision=HIGH, preferred_element_type=jnp.float32)
    coarse = mean + diffusion * mean[:, levels : levels + 1] * twice
    row = member * rows + lax.broadcasted_iota(jnp.int32, (width * rows, 1), 0) % rows
    inside = (row >= offset) & (row < offset + covered)
    next_ref[...] = pmid[:, levels : levels + 1] * jnp.where(inside, coarse, pmid)
    for r in range(rows):
        block = next_ref[pl.ds(r, width, stride=rows), :]
        for t in range(tracers):
            pnext_ref[t, r] = block[:, t * slot : t * slot + levels]


def body(parent_tracer, child_tracer, strip_cols, row_offset, parent_wet, child_wet, vert_mix):
    tracers, levels, rows, width = parent_tracer.shape
    capacity, child_rows = child_wet.shape
    strips = lax.axis_size("child")
    narrow = capacity // 3
    all_rows = rows * strips
    tiles = tile_list(child_rows)
    lane_tiles = len(tiles)
    packed = -(-narrow // (LANES // tiles[-1][1]))
    stored = up(capacity * tracers, 8)
    stride = stored + 16
    message = lane_tiles * up(tracers * levels, 8) + width
    f32 = lambda *s: jax.ShapeDtypeStruct(s, jnp.float32)
    mem = lambda *s: pltpu.VMEM(s, jnp.float32)
    parent = jnp.transpose(parent_tracer, (0, 2, 3, 1))
    child = jnp.transpose(child_tracer, (1, 2, 0, 3))

    flat, forth, back, left_edge, right_edge = pl.pallas_call(
        prepare_kernel,
        in_specs=[SM, VM, VM, VM, VM],
        out_specs=[VM] * 5,
        out_shape=[
            f32(width * rows, LANES), f32(message, LANES), f32(message, LANES), f32(rows, LANES), f32(rows, LANES),
        ],
        scratch_shapes=[mem(LANES, LANES), mem(rows, width, LANES)],
        compiler_params=params(16),
        name="prepare",
    )(strip_cols, parent, parent_wet, child, child_wet)

    groups = lax.axis_size("parent")
    devices = groups * strips
    right_edge = lax.ppermute(right_edge, "parent", [(i, i + 1) for i in range(groups - 1)])
    left_edge = lax.ppermute(left_edge, "parent", [(i + 1, i) for i in range(groups - 1)])
    forth = lax.ppermute(forth, ("parent", "child"), [(i, i + 1) for i in range(devices - 1)])
    back = lax.ppermute(back, ("parent", "child"), [(i + 1, i) for i in range(devices - 1)])

    weight, carry, below, inverse = pl.pallas_call(
        coefficient_kernel,
        in_specs=[SM],
        out_specs=[VM] * 4,
        out_shape=[f32(8 * levels, LANES)] * 3 + [f32(LANES, LANES)],
        scratch_shapes=[mem(8 * levels, LANES), mem(8 * levels, LANES)],
        compiler_params=params(8),
        name="coefficients",
    )(vert_mix)

    send, parent_mid, own, child_mid = pl.pallas_call(
        functools.partial(solve_kernel, strips, rows),
        in_specs=[SM, SM] + [VM] * 11,
        out_specs=[VM] * 4,
        out_shape=[
            f32(strips, 2 * narrow * rows, LANES),
            f32(width * rows, LANES),
            f32(narrow * all_rows, LANES),
            f32(lane_tiles, levels * stored, LANES),
        ],
        scratch_shapes=[
            mem(width * rows, LANES),
            mem((width + narrow) * rows, LANES),
            mem(lane_tiles, stored, LANES),
            mem(lane_tiles, levels * stride, LANES),
            mem(lane_tiles, levels * stored, LANES),
            mem(LANES, LANES),
            mem(packed, LANES, LANES),
            mem(narrow * child_rows, LANES),
        ],
        compiler_params=params(32),
        name="solve",
    )(
        strip_cols, row_offset, flat, forth, back, right_edge, left_edge,
        weight, carry, below, inverse, child, child_wet,
    )

    got = lax.all_to_all(send, "child", 0, 0)

    parent_next, child_next = pl.pallas_call(
        functools.partial(finish_kernel, strips, rows),
        in_specs=[SM, SM] + [VM] * 6,
        out_specs=[VM, VM],
        out_shape=[f32(*parent.shape), f32(*child.shape)],
        scratch_shapes=[
            mem(narrow * all_rows, LANES),
            mem((width + narrow) * rows, LANES),
            mem(2 * up(narrow, 8), LANES),
            mem(narrow * child_rows, LANES),
            mem(packed, LANES, LANES),
            mem(lane_tiles, levels * stored, LANES),
            mem(lane_tiles, stored, LANES),
            mem(width * rows, LANES),
        ],
        compiler_params=params(32),
        name="finish",
    )(strip_cols, row_offset, got, own, parent_mid, inverse, child_mid, child_wet)
    return jnp.transpose(parent_next, (0, 3, 1, 2)), jnp.transpose(child_next, (2, 0, 1, 3))


def solution(mesh):
    return jax.shard_map(
        body,
        mesh=mesh,
        in_specs=(
            P(None, None, "child", "parent"),
            P(None, None, ("parent", "child"), None),
            P(),
            P(),
            P("child", "parent"),
            P(("parent", "child"), None),
            P(),
        ),
        out_specs=(P(None, None, "child", "parent"), P(None, None, ("parent", "child"), None)),
        check_vma=False,
    )
```

time: 64 us -> 54.7 us (0.85)
  the two profiles are of different devices: /device:TPU:0 before, /device:TPU:1 now
where the time goes in v1:
time: 54.7 us; the launch traced here: 54.3 us
  blocking collectives  17.8 us (33%)
  starting transfers between devices  15.6 us (29%)
  Pallas kernels  13.4 us (24%)
  local copies, waits for them, and re-layouts  4.92 us (9%)
  between operations  1.4 us (3%)
  waiting for transfers between devices  1.22 us (2%)
    all_to_all x1, blocking collectives, body(): got = lax.all_to_all(send, 'child', 0, 0)  17.8 us
    pallas_call x1, Pallas kernels, body(): pl.pallas_call(functools.partial(solve_kernel, strips, rows), in_specs=[S...  6.87 us
    ppermute x1, starting transfers between devices, body(): lax.ppermute(back, ('parent', 'child'), [(i + 1, i) for i in range(device...  5.52 us
    unnamed x18, local copies, waits for them, and re-layouts  4.92 us
    pallas_call x1, Pallas kernels, body(): pl.pallas_call(functools.partial(finish_kernel, strips, rows), in_specs=[...  4.38 us
    ppermute x1, starting transfers between devices, body(): lax.ppermute(right_edge, 'parent', [(i, i + 1) for i in range(groups - 1)])  4.17 us
    ppermute x1, starting transfers between devices, body(): lax.ppermute(forth, ('parent', 'child'), [(i, i + 1) for i in range(devic...  3.98 us
    ppermute x1, starting transfers between devices, body(): lax.ppermute(left_edge, 'parent', [(i + 1, i) for i in range(groups - 1)])  1.92 us
  transfers between devices with their start and end apart: 4, of which 1 were waited for; matrix products, arithmetic and copies ran while one was open for 0% of the time, Pallas kernels for 2%

profile of v1, /device:TPU:1, one launch (start us, length us, event | category | flops | bytes accessed | tf_op | source)
XLA Modules:
  0.0 54.3 jit_solution(871539869663182601)
XLA Ops:
  0.6 0.0 copy-start.6
  0.6 0.0 copy-start.8
  0.7 0.0 copy-start
  0.7 1.8 %copy-done = f32[2,50,27,144]{3,0,2,1:T(2,128)S(1)} copy-done((f32[2,50,27,144]{3,0,2,1:T(2,128)S(1)}, f32[2,50,27,144]{3,0,2,1:T(2,128)}, u32[]{:S(2)}) %copy-start) | copy-done | bytes 1555224
  2.4 0.0 copy-start.2
  2.4 1.0 %copy-done.2 = f32[2,50,8,48]{1,3,2,0:T(8,128)S(1)} copy-done((f32[2,50,8,48]{1,3,2,0:T(8,128)S(1)}, f32[2,50,8,48]{1,3,2,0:T(8,128)}, u32[]{:S(2)}) %copy-start.2) | copy-done | bytes 153624
  3.4 0.0 copy-start.3
  3.4 0.8 %copy-done.3 = s32[27,144]{1,0:T(8,128)S(1)} copy-done((s32[27,144]{1,0:T(8,128)S(1)}, s32[27,144]{1,0:T(8,128)}, u32[]{:S(2)}) %copy-start.3) | copy-done | bytes 15576
  4.2 0.0 copy-start.5
  4.2 0.7 %copy-done.5 = s32[4,8]{1,0:T(4,128)S(1)} copy-done((s32[4,8]{1,0:T(4,128)S(1)}, s32[4,8]{1,0:T(4,128)}, u32[]{:S(2)}) %copy-start.5) | copy-done | bytes 152
  4.9 0.0 copy-start.7
  4.9 0.7 %copy-done.7 = s32[8,48]{1,0:T(8,128)S(1)} copy-done((s32[8,48]{1,0:T(8,128)S(1)}, s32[8,48]{1,0:T(8,128)}, u32[]{:S(2)}) %copy-start.7) | copy-done | bytes 1560
  5.6 0.0 copy-start.1
  5.6 0.0 copy-start.4
  5.6 1.0 %prepare.1 = (f32[384,128]{1,0:T(8,128)S(1)}, f32[256,128]{1,0:T(8,128)S(1)}, f32[256,128]{1,0:T(8,128)S(1)}, f32[8,128]{1,0:T(8,128)S(1)}, f32[8,128]{1,0:T(8,128)S(1)}) custom-call(s32[4,8]{1,0:T(4,128)S(1)} %copy-done.5, f32[2,8,48,50]{3,2,1,0:T(8,128)S(1)} %bitcast.6, s32[8,48]{1,0:T(8,128)S(1)} %copy-done.7, f32[50,27,2,144]{3,2,1,0:T(2,128)S(1)} %bitcast.4, ...), custom_call_target="tpu_custom_call" | custom-call | tf_op jit(solution)/shard_map/prepare/pallas_call | solution.py:384
  6.6 4.0 %collective-permute-start = (f32[256,128]{1,0:T(8,128)S(1)}, f32[256,128]{1,0:T(8,128)S(1)}, u32[]{:S(2)}, u32[]{:S(2)}) collective-permute-start(f32[256,128]{1,0:T(8,128)S(1)} %get-tuple-element.18), channel_id=1, source_target_pairs={{0,1},{1,2},{2,3},{3,4},{4,5},{5,6},{6,7},{7,8},{8,9},{9,10},{10,1... | collective-permute-start | bytes 393224 | tf_op jit(solution)/shard_map/ppermute | solution.py:400
  10.6 5.5 %collective-permute-start.1 = (f32[256,128]{1,0:T(8,128)S(1)}, f32[256,128]{1,0:T(8,128)S(1)}, u32[]{:S(2)}, u32[]{:S(2)}) collective-permute-start(f32[256,128]{1,0:T(8,128)S(1)} %get-tuple-element.19), channel_id=1, source_target_pairs={{1,0},{2,1},{3,2},{4,3},{5,4},{6,5},{7,6},{8,7},{9,8},{10,9},{11,1... | collective-permute-start | bytes 393224 | tf_op jit(solution)/shard_map/ppermute | solution.py:401
  16.1 4.2 %collective-permute-start.2 = (f32[8,128]{1,0:T(8,128)S(1)}, f32[8,128]{1,0:T(8,128)S(1)}, u32[]{:S(2)}, u32[]{:S(2)}) collective-permute-start(f32[8,128]{1,0:T(8,128)S(1)} %get-tuple-element.20), channel_id=1, source_target_pairs={{0,8},{8,16},{16,24},{1,9},{9,17},{17,25},{2,10},{10,18},{18,26},{... | collective-permute-start | bytes 12296 | tf_op jit(solution)/shard_map/ppermute | solution.py:398
  20.3 1.9 %collective-permute-start.3 = (f32[8,128]{1,0:T(8,128)S(1)}, f32[8,128]{1,0:T(8,128)S(1)}, u32[]{:S(2)}, u32[]{:S(2)}) collective-permute-start(f32[8,128]{1,0:T(8,128)S(1)} %get-tuple-element.21), channel_id=1, source_target_pairs={{8,0},{16,8},{24,16},{9,1},{17,9},{25,17},{10,2},{18,10},{26,18},{... | collective-permute-start | bytes 12296 | tf_op jit(solution)/shard_map/ppermute | solution.py:399
  22.8 0.0 copy-done.8
  22.9 1.1 %coefficients.1 = (f32[400,128]{1,0:T(8,128)S(1)}, f32[400,128]{1,0:T(8,128)S(1)}, f32[400,128]{1,0:T(8,128)S(1)}, f32[128,128]{1,0:T(8,128)S(1)}) custom-call(f32[2,49]{1,0:T(2,128)S(1)} %copy-done.8), custom_call_target="tpu_custom_call" | custom-call | tf_op jit(solution)/shard_map/coefficients/pallas_call | solution.py:403
  24.0 0.0 collective-permute-done.2.left_ref
  24.0 1.2 %collective-permute-done.3.right_ref = f32[8,128]{1,0:T(8,128)S(1)} collective-permute-done((f32[8,128]{1,0:T(8,128)S(1)}, f32[8,128]{1,0:T(8,128)S(1)}, u32[]{:S(2)}, u32[]{:S(2)}) %collective-permute-start.3) | collective-permute-done | bytes 4128 | tf_op jit(solution)/shard_map/ppermute | solution.py:399
  25.2 0.0 collective-permute-done.before_ref
  25.2 0.0 collective-permute-done.1.after_ref
  25.2 0.0 copy-done.6
  25.2 0.0 copy-done.1
  25.2 0.0 copy-done.4
  25.2 6.9 %solve.1 = (f32[8,144,128]{2,1,0:T(8,128)S(1)}, f32[384,128]{1,0:T(8,128)S(1)}, f32[576,128]{1,0:T(8,128)S(1)}, f32[2,2800,128]{2,1,0:T(8,128)S(1)}) custom-call(s32[4,8]{1,0:T(4,128)S(1)} %copy-done.6, s32[1]{0:T(128)S(6)} %copy.9.offset_ref, f32[384,128]{1,0:T(8,128)S(1)} %get-tuple-element.17.flat_ref, f32[256,128]{1,0:T(8,128)S(1)} %collective-permute-done.before_ref, ...), custom_call_target="tpu_custom_call" | custom-call | tf_op jit(solution)/shard_map/solve/pallas_call | solution.py:413
  32.1 17.8 %all_to_all.5.got_ref = f32[8,144,128]{2,1,0:T(8,128)S(1)} all-to-all(f32[8,144,128]{2,1,0:T(8,128)S(1)} %get-tuple-element.26), channel_id=1, replica_groups=mesh['parent'=4,'child'=8] {'child'}, dimensions={0} | all-to-all | bytes 1179648 | tf_op jit(solution)/shard_map/all_to_all | solution.py:440
  49.9 4.4 %finish.1 = (f32[2,8,48,50]{3,2,1,0:T(8,128)}, f32[50,27,2,144]{3,2,1,0:T(2,128)}) custom-call(s32[4,8]{1,0:T(4,128)S(1)} %copy-done.6, s32[1]{0:T(128)S(6)} %copy.9.offset_ref, f32[8,144,128]{2,1,0:T(8,128)S(1)} %all_to_all.5.got_ref, f32[576,128]{1,0:T(8,128)S(1)} %get-tuple-element.27.own_ref, f32[384,128]{1,0:T(8,128)S(1)} %get-tuple-element.28.pmid_ref, ...), custom_call_target="tpu_custom_call" | custom-call | tf_op jit(solution)/shard_map/finish/pallas_call | solution.py:442
Async XLA Ops:
  0.6 24.6 %copy-start.6 = (s32[4,8]{1,0:T(4,128)S(1)}, s32[4,8]{1,0:T(4,128)}, u32[]{:S(2)}) copy-start(s32[4,8]{1,0:T(4,128)} %cols_ref.5) | copy-start | bytes 388
  0.6 22.2 %copy-start.8 = (f32[2,49]{1,0:T(2,128)S(1)}, f32[2,49]{1,0:T(2,128)}, u32[]{:S(2)}) copy-start(f32[2,49]{1,0:T(2,128)} %mix_ref.1) | copy-start | bytes 1180
  0.7 1.8 %copy-start = (f32[2,50,27,144]{3,0,2,1:T(2,128)S(1)}, f32[2,50,27,144]{3,0,2,1:T(2,128)}, u32[]{:S(2)}) copy-start(f32[2,50,27,144]{3,0,2,1:T(2,128)} %param.8) | copy-start | bytes 4665604
  2.4 1.0 %copy-start.2 = (f32[2,50,8,48]{1,3,2,0:T(8,128)S(1)}, f32[2,50,8,48]{1,3,2,0:T(8,128)}, u32[]{:S(2)}) copy-start(f32[2,50,8,48]{1,3,2,0:T(8,128)} %param.7) | copy-start | bytes 460804
  3.4 0.8 %copy-start.3 = (s32[27,144]{1,0:T(8,128)S(1)}, s32[27,144]{1,0:T(8,128)}, u32[]{:S(2)}) copy-start(s32[27,144]{1,0:T(8,128)} %cwet_ref.5) | copy-start | bytes 46660
  4.2 0.7 %copy-start.5 = (s32[4,8]{1,0:T(4,128)S(1)}, s32[4,8]{1,0:T(4,128)}, u32[]{:S(2)}) copy-start(s32[4,8]{1,0:T(4,128)} %cols_ref.5) | copy-start | bytes 388
  4.9 0.7 %copy-start.7 = (s32[8,48]{1,0:T(8,128)S(1)}, s32[8,48]{1,0:T(8,128)}, u32[]{:S(2)}) copy-start(s32[8,48]{1,0:T(8,128)} %pwet_ref.1) | copy-start | bytes 4612
  5.6 19.6 %copy-start.1 = (f32[2,50,27,144]{3,0,2,1:T(2,128)S(1)}, f32[2,50,27,144]{3,0,2,1:T(2,128)}, u32[]{:S(2)}) copy-start(f32[2,50,27,144]{3,0,2,1:T(2,128)} %param.8) | copy-start | bytes 4665604
  5.6 19.6 %copy-start.4 = (s32[27,144]{1,0:T(8,128)S(1)}, s32[27,144]{1,0:T(8,128)}, u32[]{:S(2)}) copy-start(s32[27,144]{1,0:T(8,128)} %cwet_ref.5) | copy-start | bytes 46660
  6.6 18.6 %collective-permute-start = (f32[256,128]{1,0:T(8,128)S(1)}, f32[256,128]{1,0:T(8,128)S(1)}, u32[]{:S(2)}, u32[]{:S(2)}) collective-permute-start(f32[256,128]{1,0:T(8,128)S(1)} %get-tuple-element.18), channel_id=1, source_target_pairs={{0,1},{1,2},{2,3},{3,4},{4,5},{5,6},{6,7},{7,8},{8,9},{9,10},{10,1... | collective-permute-start | bytes 393224 | tf_op jit(solution)/shard_map/ppermute | solution.py:400
  10.6 14.6 %collective-permute-start.1 = (f32[256,128]{1,0:T(8,128)S(1)}, f32[256,128]{1,0:T(8,128)S(1)}, u32[]{:S(2)}, u32[]{:S(2)}) collective-permute-start(f32[256,128]{1,0:T(8,128)S(1)} %get-tuple-element.19), channel_id=1, source_target_pairs={{1,0},{2,1},{3,2},{4,3},{5,4},{6,5},{7,6},{8,7},{9,8},{10,9},{11,1... | collective-permute-start | bytes 393224 | tf_op jit(solution)/shard_map/ppermute | solution.py:401
  16.1 7.9 %collective-permute-start.2 = (f32[8,128]{1,0:T(8,128)S(1)}, f32[8,128]{1,0:T(8,128)S(1)}, u32[]{:S(2)}, u32[]{:S(2)}) collective-permute-start(f32[8,128]{1,0:T(8,128)S(1)} %get-tuple-element.20), channel_id=1, source_target_pairs={{0,8},{8,16},{16,24},{1,9},{9,17},{17,25},{2,10},{10,18},{18,26},{... | collective-permute-start | bytes 12296 | tf_op jit(solution)/shard_map/ppermute | solution.py:398
  20.3 4.9 %collective-permute-start.3 = (f32[8,128]{1,0:T(8,128)S(1)}, f32[8,128]{1,0:T(8,128)S(1)}, u32[]{:S(2)}, u32[]{:S(2)}) collective-permute-start(f32[8,128]{1,0:T(8,128)S(1)} %get-tuple-element.21), channel_id=1, source_target_pairs={{8,0},{16,8},{24,16},{9,1},{17,9},{25,17},{10,2},{18,10},{26,18},{... | collective-permute-start | bytes 12296 | tf_op jit(solution)/shard_map/ppermute | solution.py:399

commit v2 on v1

--- a/solution.py
+++ b/solution.py
@@ -15,10 +15,15 @@
 
 VM = pl.BlockSpec(memory_space=pltpu.VMEM)
 SM = pl.BlockSpec(memory_space=pltpu.SMEM)
+HBM = pl.BlockSpec(memory_space=pltpu.HBM)
 
 
 def params(mib):
     return pltpu.CompilerParams(vmem_limit_bytes=mib << 20)
+
+
+def in_hbm(x):
+    return pltpu.with_memory_space_constraint(x, pltpu.HBM)
 
 
 def up(n, m):
@@ -84,17 +89,31 @@
 
 
 def prepare_kernel(
-    cols_ref, parent_ref, pwet_ref, child_ref, cwet_ref,
-    flat_ref, forth_ref, back_ref, left_ref, right_ref, turn_ref, row_ref,
+    cols_hbm, parent_hbm, pwet_hbm, child_hbm, cwet_hbm,
+    flat_ref, forth_ref, back_ref, left_ref, right_ref,
+    cols_ref, parent_ref, pwet_ref, cwet_ref, edge_ref, turn_ref, row_ref, sems,
 ):
-    levels, capacity, tracers, child_rows = child_ref.shape
+    levels, capacity, tracers, child_rows = child_hbm.shape
     rows, width = pwet_ref.shape
     slot = LANES // tracers
     level_rows = up(tracers * levels, 8)
     tiles = tile_list(child_rows)
+    fetch_cols = pltpu.make_async_copy(cols_hbm, cols_ref, sems.at[0])
+    fetch_pwet = pltpu.make_async_copy(pwet_hbm, pwet_ref, sems.at[1])
+    fetch_parent = pltpu.make_async_copy(parent_hbm, parent_ref, sems.at[2])
+    fetch_cwet = pltpu.make_async_copy(cwet_hbm, cwet_ref, sems.at[3])
+    fetch_first = pltpu.make_async_copy(child_hbm.at[:, pl.ds(0, 1)], edge_ref.at[1], sems.at[4])
+    for fetch in (fetch_cols, fetch_pwet, fetch_parent, fetch_first, fetch_cwet):
+        fetch.start()
+    fetch_cols.wait()
+    last = 3 * my_cols(cols_ref) - 1
+    fetch_last = pltpu.make_async_copy(child_hbm.at[:, pl.ds(last, 1)], edge_ref.at[0], sems.at[5])
+    fetch_last.start()
+    row_ref[...] = jnp.zeros_like(row_ref)
+    fetch_pwet.wait()
     turn_ref[:rows, :width] = pwet_ref[...].astype(jnp.float32)
-    row_ref[...] = jnp.zeros_like(row_ref)
     wet = turn_ref[...].T
+    fetch_parent.wait()
     for r in range(rows):
         cell = wet[:width, r : r + 1]
         for t in range(tracers):
@@ -103,16 +122,15 @@
         flat_ref[pl.ds(r, width, stride=rows), :] = row_ref[r]
     left_ref[...] = flat_ref[:rows, :]
     right_ref[...] = flat_ref[(width - 1) * rows :, :]
-    flat_child = child_ref.reshape(levels * capacity * tracers, child_rows)
-    last = 3 * my_cols(cols_ref) - 1
+    fetch_cwet.wait()
     base = len(tiles) * level_rows
-    for ref, x, r in ((forth_ref, last, rows - 1), (back_ref, 0, 0)):
+    fetch_first.wait()
+    fetch_last.wait()
+    for side, (ref, x, r) in enumerate(((forth_ref, last, rows - 1), (back_ref, 0, 0))):
         cell = cwet_ref[pl.ds(x, 1), :].astype(jnp.float32)
-        for l in range(levels):
-            pair = flat_child[pl.ds(pl.multiple_of((l * capacity + x) * tracers, tracers), tracers), :] * cell
-            for n, size in tiles:
-                at = n * level_rows + l * tracers
-                ref[at : at + tracers, :size] = pair[:, n * LANES : n * LANES + size]
+        pairs = edge_ref.at[side].reshape(levels * tracers, child_rows)[...] * cell
+        for n, size in tiles:
+            ref[n * level_rows : n * level_rows + levels * tracers, :size] = pairs[:, n * LANES : n * LANES + size]
         ref[base : base + width, :] = row_ref[r]
 
 
@@ -131,13 +149,20 @@
 
 
 def solve_kernel(
-    strips, rows,
+    groups, strips, rows,
     cols_ref, offset_ref, flat_ref, before_ref, after_ref, left_ref, right_ref,
-    weight_ref, carry_ref, back_ref, inverse_ref, child_ref, cwet_ref,
+    weight_ref, carry_ref, back_ref, inverse_ref, child_hbm, cwet_ref,
     send_ref, pmid_ref, own_ref, cmid_ref,
-    explicit_ref, wide_ref, mask_ref, begin_ref, d_ref, turn_ref, end_ref, long_ref,
+    explicit_ref, wide_ref, mask_ref, begin_ref, d_ref, turn_ref, end_ref, long_ref, child_ref, sems,
 ):
     levels, capacity, tracers, child_rows = child_ref.shape
+    chunks = sems.shape[0]
+    step = -(-levels // chunks)
+    fetches = []
+    for c in range(chunks):
+        part = pl.ds(c * step, min(levels, (c + 1) * step) - c * step)
+        fetches.append(pltpu.make_async_copy(child_hbm.at[part], child_ref.at[part], sems.at[c]))
+        fetches[-1].start()
     slot = LANES // tracers
     width = flat_ref.shape[0] // rows
     narrow = capacity // 3
@@ -153,12 +178,17 @@
     starts = strip_starts(cols_ref, strips)
     offset = offset_ref[0]
 
+    group = lax.axis_index("parent")
     has_before = (member > 0).astype(jnp.float32)
     has_after = (member < strips - 1).astype(jnp.float32)
+    has_left = (group > 0).astype(jnp.float32)
+    has_right = (group < groups - 1).astype(jnp.float32)
+    chain_before = jnp.maximum(has_before, has_left)
+    chain_after = jnp.maximum(has_after, has_right)
     for x in range(width):
         here = flat_ref[x * rows : (x + 1) * rows, :]
-        west = left_ref[...] if x == 0 else flat_ref[(x - 1) * rows : x * rows, :]
-        east = right_ref[...] if x == width - 1 else flat_ref[(x + 1) * rows : (x + 2) * rows, :]
+        west = has_left * left_ref[...] if x == 0 else flat_ref[(x - 1) * rows : x * rows, :]
+        east = has_right * right_ref[...] if x == width - 1 else flat_ref[(x + 1) * rows : (x + 2) * rows, :]
         south = jnp.concatenate([has_before * before_ref[base + x : base + x + 1, :], here[:-1]], axis=0)
         north = jnp.concatenate([here[1:], has_after * after_ref[base + x : base + x + 1, :]], axis=0)
         wet = here[:, levels : levels + 1]
@@ -188,11 +218,13 @@
             part = cells[:, n * LANES : n * LANES + size] * mask_ref[n, :live, :size]
             begin_ref[n, pl.ds(start + 8, live), :size] = part
             edge = pl.ds(n * level_rows + l * tracers, tracers)
-            begin_ref[n, pl.ds(start + 8 - tracers, tracers), :size] = before_ref[edge, :size]
-            begin_ref[n, pl.ds(start + past, tracers), :size] = after_ref[edge, :size]
+            begin_ref[n, pl.ds(start + 8 - tracers, tracers), :size] = chain_before * before_ref[edge, :size]
+            begin_ref[n, pl.ds(start + past, tracers), :size] = chain_after * after_ref[edge, :size]
         return carry
 
-    lax.fori_loop(0, levels, begin, 0, unroll=2)
+    for c in range(chunks):
+        fetches[c].wait()
+        lax.fori_loop(c * step, min(levels, (c + 1) * step), begin, 0, unroll=2)
 
     def by_rows(factor, value):
         return (factor[None] * value.reshape(stored // 8, 8, LANES)).reshape(stored, LANES)
@@ -274,12 +306,12 @@
 
 
 def finish_kernel(
-    strips, rows,
+    strips, rows, chunks,
     cols_ref, offset_ref, got_ref, own_ref, pmid_ref, inverse_ref, cmid_ref, cwet_ref,
-    pnext_ref, cnext_ref,
-    panel_ref, wide_ref, ends_ref, long_ref, end_ref, add_ref, mask_ref, next_ref,
+    pnext_hbm, cnext_hbm,
+    panel_ref, wide_ref, ends_ref, long_ref, end_ref, add_ref, mask_ref, next_ref, pkeep_ref, ckeep_ref, sems,
 ):
-    levels, capacity, tracers, child_rows = cnext_ref.shape
+    levels, capacity, tracers, child_rows = cnext_hbm.shape
     slot = LANES // tracers
     width = pmid_ref.shape[0] // rows
     narrow = capacity // 3
@@ -293,6 +325,22 @@
     starts = strip_starts(cols_ref, strips)
     offset = offset_ref[0]
     masks(cols_ref, cwet_ref, mask_ref, tracers)
+
+    for j in range(strips):
+        wide_ref[pl.ds(pl.multiple_of(starts[j] * rows, rows), narrow * rows), :] = got_ref[j, narrow * rows :, :]
+    mean = wide_ref[: width * rows, :]
+    pmid = pmid_ref[...]
+    twice = jnp.dot(pmid, inverse_ref[...], precision=HIGH, preferred_element_type=jnp.float32)
+    coarse = mean + diffusion * mean[:, levels : levels + 1] * twice
+    row = member * rows + lax.broadcasted_iota(jnp.int32, (width * rows, 1), 0) % rows
+    inside = (row >= offset) & (row < offset + covered)
+    next_ref[...] = pmid[:, levels : levels + 1] * jnp.where(inside, coarse, pmid)
+    for r in range(rows):
+        block = next_ref[pl.ds(r, width, stride=rows), :]
+        for t in range(tracers):
+            pkeep_ref[t, r] = block[:, t * slot : t * slot + levels]
+    send_parent = pltpu.make_async_copy(pkeep_ref, pnext_hbm, sems.at[0])
+    send_parent.start()
 
     ends_ref[...] = jnp.zeros_like(ends_ref)
     for q in range(narrow):
@@ -337,7 +385,7 @@
             shift = (q % packs) * tail_size
             spread(pltpu.roll(turned, (LANES - shift) % LANES, 1) if shift else turned, tail, q)
 
-    flat_next = cnext_ref.reshape(levels * live, child_rows)
+    flat_next = ckeep_ref.reshape(levels * live, child_rows)
 
     def write(l, carry):
         at = pl.ds(pl.multiple_of(l * stored, 8), live)
@@ -347,21 +395,20 @@
         flat_next[pl.ds(pl.multiple_of(l * live, 2), live), :] = jnp.concatenate(parts, axis=1)
         return carry
 
-    lax.fori_loop(0, levels, write, 0, unroll=2)
-
-    for j in range(strips):
-        wide_ref[pl.ds(pl.multiple_of(starts[j] * rows, rows), narrow * rows), :] = got_ref[j, narrow * rows :, :]
-    mean = wide_ref[: width * rows, :]
-    pmid = pmid_ref[...]
-    twice = jnp.dot(pmid, inverse_ref[...], precision=HIGH, preferred_element_type=jnp.float32)
-    coarse = mean + diffusion * mean[:, levels : levels + 1] * twice
-    row = member * rows + lax.broadcasted_iota(jnp.int32, (width * rows, 1), 0) % rows
-    inside = (row >= offset) & (row < offset + covered)
-    next_ref[...] = pmid[:, levels : levels + 1] * jnp.where(inside, coarse, pmid)
-    for r in range(rows):
-        block = next_ref[pl.ds(r, width, stride=rows), :]
-        for t in range(tracers):
-            pnext_ref[t, r] = block[:, t * slot : t * slot + levels]
+    sends = [send_parent]
+    step = -(-levels // chunks)
+    for c in range(chunks):
+        low, high = c * step, min(levels, (c + 1) * step)
+        lax.fori_loop(low, high, write, 0, unroll=2)
+        part = pl.ds(low, high - low)
+        sends.append(pltpu.make_async_copy(ckeep_ref.at[part], cnext_hbm.at[part], sems.at[1 + c]))
+        sends[-1].start()
+    for send in sends:
+        send.wait()
+
+
+def ring(block, axes, count, step):
+    return lax.ppermute(block, axes, [(i, (i + step) % count) for i in range(count)])
 
 
 def body(parent_tracer, child_tracer, strip_cols, row_offset, parent_wet, child_wet, vert_mix):
@@ -375,6 +422,7 @@
     packed = -(-narrow // (LANES // tiles[-1][1]))
     stored = up(capacity * tracers, 8)
     stride = stored + 16
+    chunks = 5
     message = lane_tiles * up(tracers * levels, 8) + width
     f32 = lambda *s: jax.ShapeDtypeStruct(s, jnp.float32)
     mem = lambda *s: pltpu.VMEM(s, jnp.float32)
@@ -383,22 +431,31 @@
 
     flat, forth, back, left_edge, right_edge = pl.pallas_call(
         prepare_kernel,
-        in_specs=[SM, VM, VM, VM, VM],
+        in_specs=[HBM] * 5,
         out_specs=[VM] * 5,
         out_shape=[
             f32(width * rows, LANES), f32(message, LANES), f32(message, LANES), f32(rows, LANES), f32(rows, LANES),
         ],
-        scratch_shapes=[mem(LANES, LANES), mem(rows, width, LANES)],
+        scratch_shapes=[
+            pltpu.SMEM(strip_cols.shape, jnp.int32),
+            mem(*parent.shape),
+            pltpu.VMEM(parent_wet.shape, jnp.int32),
+            pltpu.VMEM(child_wet.shape, jnp.int32),
+            mem(2, levels, 1, tracers, child_rows),
+            mem(LANES, LANES),
+            mem(rows, width, LANES),
+            pltpu.SemaphoreType.DMA((6,)),
+        ],
         compiler_params=params(16),
         name="prepare",
-    )(strip_cols, parent, parent_wet, child, child_wet)
+    )(*(in_hbm(x) for x in (strip_cols, parent, parent_wet, child, child_wet)))
 
     groups = lax.axis_size("parent")
     devices = groups * strips
-    right_edge = lax.ppermute(right_edge, "parent", [(i, i + 1) for i in range(groups - 1)])
-    left_edge = lax.ppermute(left_edge, "parent", [(i + 1, i) for i in range(groups - 1)])
-    forth = lax.ppermute(forth, ("parent", "child"), [(i, i + 1) for i in range(devices - 1)])
-    back = lax.ppermute(back, ("parent", "child"), [(i + 1, i) for i in range(devices - 1)])
+    right_edge = ring(right_edge, "parent", groups, 1)
+    left_edge = ring(left_edge, "parent", groups, -1)
+    forth = ring(forth, ("parent", "child"), devices, 1)
+    back = ring(back, ("parent", "child"), devices, -1)
 
     weight, carry, below, inverse = pl.pallas_call(
         coefficient_kernel,
@@ -411,8 +468,8 @@
     )(vert_mix)
 
     send, parent_mid, own, child_mid = pl.pallas_call(
-        functools.partial(solve_kernel, strips, rows),
-        in_specs=[SM, SM] + [VM] * 11,
+        functools.partial(solve_kernel, groups, strips, rows),
+        in_specs=[SM, SM] + [VM] * 9 + [HBM, VM],
         out_specs=[VM] * 4,
         out_shape=[
             f32(strips, 2 * narrow * rows, LANES),
@@ -429,20 +486,22 @@
             mem(LANES, LANES),
             mem(packed, LANES, LANES),
             mem(narrow * child_rows, LANES),
+            mem(*child.shape),
+            pltpu.SemaphoreType.DMA((chunks,)),
         ],
         compiler_params=params(32),
         name="solve",
     )(
         strip_cols, row_offset, flat, forth, back, right_edge, left_edge,
-        weight, carry, below, inverse, child, child_wet,
+        weight, carry, below, inverse, in_hbm(child), child_wet,
     )
 
     got = lax.all_to_all(send, "child", 0, 0)
 
     parent_next, child_next = pl.pallas_call(
-        functools.partial(finish_kernel, strips, rows),
+        functools.partial(finish_kernel, strips, rows, chunks),
         in_specs=[SM, SM] + [VM] * 6,
-        out_specs=[VM, VM],
+        out_specs=[HBM, HBM],
         out_shape=[f32(*parent.shape), f32(*child.shape)],
         scratch_shapes=[
             mem(narrow * all_rows, LANES),
@@ -453,6 +512,9 @@
             mem(lane_tiles, levels * stored, LANES),
             mem(lane_tiles, stored, LANES),
             mem(width * rows, LANES),
+            mem(*parent.shape),
+            mem(*child.shape),
+            pltpu.SemaphoreType.DMA((1 + chunks,)),
         ],
         compiler_params=params(32),
         name="finish",

time: 54.7 us -> 46.6 us (0.85)
  the two profiles are of different devices: /device:TPU:1 before, /device:TPU:0 now
where the time goes in v2:
time: 46.6 us; the launch traced here: 46.4 us
  blocking collectives  21.9 us (47%)
  Pallas kernels  14.1 us (30%)
  starting transfers between devices  8.24 us (18%)
  between operations  1.36 us (3%)
  waiting for transfers between devices  0.77 us (2%)
    all_to_all x1, blocking collectives, body(): got = lax.all_to_all(send, 'child', 0, 0)  21.9 us
    ppermute x4, starting transfers between devices, ring(): lax.ppermute(block, axes, [(i, (i + step) % count) for i in range(count)])  8.24 us
    pallas_call x1, Pallas kernels, body(): pl.pallas_call(functools.partial(solve_kernel, groups, strips, rows), in_...  7.73 us
    pallas_call x1, Pallas kernels, body(): pl.pallas_call(functools.partial(finish_kernel, strips, rows, chunks), in...  3.39 us
    pallas_call x1, Pallas kernels, body(): pl.pallas_call(prepare_kernel, in_specs=[HBM] * 5, out_specs=[VM] * 5, ou...  1.88 us
    pallas_call x1, Pallas kernels, body(): pl.pallas_call(coefficient_kernel, in_specs=[SM], out_specs=[VM] * 4, out...  1.11 us
  transfers between devices with their start and end apart: 4, of which 2 were waited for; matrix products, arithmetic and copies ran while one was open for 0% of the time, Pallas kernels for 2%

profile of v2, /device:TPU:0, one launch (start us, length us, event | category | flops | bytes accessed | tf_op | source)
XLA Modules:
  0.0 46.4 jit_solution(17475397601761857959)
XLA Ops:
  0.6 0.0 copy-start
  0.6 0.0 copy-start.1
  0.7 0.0 copy-start.2
  0.7 1.9 %prepare.1 = (f32[384,128]{1,0:T(8,128)S(1)}, f32[256,128]{1,0:T(8,128)S(1)}, f32[256,128]{1,0:T(8,128)S(1)}, f32[8,128]{1,0:T(8,128)S(1)}, f32[8,128]{1,0:T(8,128)S(1)}) custom-call(s32[4,8]{1,0:T(4,128)} %cols_ref.3, f32[2,8,48,50]{3,2,1,0:T(8,128)} %bitcast.6, s32[8,48]{1,0:T(8,128)} %pwet_hbm.1, f32[50,27,2,144]{3,2,1,0:T(2,128)} %bitcast.4, ...), custom_call_target="tpu_custom_call" | custom-call | tf_op jit(solution)/shard_map/prepare/pallas_call | solution.py:432
  2.5 3.0 %collective-permute-start = (f32[256,128]{1,0:T(8,128)S(1)}, f32[256,128]{1,0:T(8,128)S(1)}, u32[]{:S(2)}, u32[]{:S(2)}) collective-permute-start(f32[256,128]{1,0:T(8,128)S(1)} %get-tuple-element.18), channel_id=1, source_target_pairs={{0,1},{1,2},{2,3},{3,4},{4,5},{5,6},{6,7},{7,8},{8,9},{9,10},{10,1... | collective-permute-start | bytes 393224 | tf_op jit(solution)/shard_map/ppermute | solution.py:411
  5.6 3.5 %collective-permute-start.1 = (f32[256,128]{1,0:T(8,128)S(1)}, f32[256,128]{1,0:T(8,128)S(1)}, u32[]{:S(2)}, u32[]{:S(2)}) collective-permute-start(f32[256,128]{1,0:T(8,128)S(1)} %get-tuple-element.19), channel_id=1, source_target_pairs={{0,31},{1,0},{2,1},{3,2},{4,3},{5,4},{6,5},{7,6},{8,7},{9,8},{10,9... | collective-permute-start | bytes 393224 | tf_op jit(solution)/shard_map/ppermute | solution.py:411
  9.0 0.0 collective-permute-start.2
  9.0 1.7 %collective-permute-start.3 = (f32[8,128]{1,0:T(8,128)S(1)}, f32[8,128]{1,0:T(8,128)S(1)}, u32[]{:S(2)}, u32[]{:S(2)}) collective-permute-start(f32[8,128]{1,0:T(8,128)S(1)} %get-tuple-element.21), channel_id=1, source_target_pairs={{0,24},{8,0},{16,8},{24,16},{1,25},{9,1},{17,9},{25,17},{2,26},{10... | collective-permute-start | bytes 12296 | tf_op jit(solution)/shard_map/ppermute | solution.py:411
  11.4 0.0 copy-done.2
  11.4 1.1 %coefficients.1 = (f32[400,128]{1,0:T(8,128)S(1)}, f32[400,128]{1,0:T(8,128)S(1)}, f32[400,128]{1,0:T(8,128)S(1)}, f32[128,128]{1,0:T(8,128)S(1)}) custom-call(f32[2,49]{1,0:T(2,128)S(1)} %copy-done.2), custom_call_target="tpu_custom_call" | custom-call | tf_op jit(solution)/shard_map/coefficients/pallas_call | solution.py:460
  12.6 0.0 collective-permute-done.2.left_ref
  12.6 0.0 collective-permute-done.3.right_ref
  12.6 0.3 collective-permute-done.before_ref
  12.9 0.4 collective-permute-done.1.after_ref
  13.3 0.0 copy-done
  13.3 0.0 copy-done.1
  13.4 7.7 %solve.1 = (f32[8,144,128]{2,1,0:T(8,128)S(1)}, f32[384,128]{1,0:T(8,128)S(1)}, f32[576,128]{1,0:T(8,128)S(1)}, f32[2,2800,128]{2,1,0:T(8,128)S(1)}) custom-call(s32[4,8]{1,0:T(4,128)S(1)} %copy-done.1, s32[1]{0:T(128)S(6)} %copy.9.offset_ref, f32[384,128]{1,0:T(8,128)S(1)} %get-tuple-element.17.flat_ref, f32[256,128]{1,0:T(8,128)S(1)} %collective-permute-done.before_ref, ...), custom_call_target="tpu_custom_call" | custom-call | tf_op jit(solution)/shard_map/solve/pallas_call | solution.py:470
  21.1 21.9 %all_to_all.5.got_ref = f32[8,144,128]{2,1,0:T(8,128)S(1)} all-to-all(f32[8,144,128]{2,1,0:T(8,128)S(1)} %get-tuple-element.26), channel_id=1, replica_groups=mesh['parent'=4,'child'=8] {'child'}, dimensions={0} | all-to-all | bytes 1179648 | tf_op jit(solution)/shard_map/all_to_all | solution.py:499
  43.0 3.4 %finish.1 = (f32[2,8,48,50]{3,2,1,0:T(8,128)}, f32[50,27,2,144]{3,2,1,0:T(2,128)}) custom-call(s32[4,8]{1,0:T(4,128)S(1)} %copy-done.1, s32[1]{0:T(128)S(6)} %copy.9.offset_ref, f32[8,144,128]{2,1,0:T(8,128)S(1)} %all_to_all.5.got_ref, f32[576,128]{1,0:T(8,128)S(1)} %get-tuple-element.27.own_ref, f32[384,128]{1,0:T(8,128)S(1)} %get-tuple-element.28.pmid_ref, ...), custom_call_target="tpu_custom_call" | custom-call | tf_op jit(solution)/shard_map/finish/pallas_call | solution.py:501
Async XLA Ops:
  0.6 12.7 %copy-start = (s32[27,144]{1,0:T(8,128)S(1)}, s32[27,144]{1,0:T(8,128)}, u32[]{:S(2)}) copy-start(s32[27,144]{1,0:T(8,128)} %cwet_ref.3) | copy-start | bytes 46660
  0.6 12.7 %copy-start.1 = (s32[4,8]{1,0:T(4,128)S(1)}, s32[4,8]{1,0:T(4,128)}, u32[]{:S(2)}) copy-start(s32[4,8]{1,0:T(4,128)} %cols_ref.3) | copy-start | bytes 388
  0.7 10.8 %copy-start.2 = (f32[2,49]{1,0:T(2,128)S(1)}, f32[2,49]{1,0:T(2,128)}, u32[]{:S(2)}) copy-start(f32[2,49]{1,0:T(2,128)} %mix_ref.1) | copy-start | bytes 1180
  2.5 10.4 %collective-permute-start = (f32[256,128]{1,0:T(8,128)S(1)}, f32[256,128]{1,0:T(8,128)S(1)}, u32[]{:S(2)}, u32[]{:S(2)}) collective-permute-start(f32[256,128]{1,0:T(8,128)S(1)} %get-tuple-element.18), channel_id=1, source_target_pairs={{0,1},{1,2},{2,3},{3,4},{4,5},{5,6},{6,7},{7,8},{8,9},{9,10},{10,1... | collective-permute-start | bytes 393224 | tf_op jit(solution)/shard_map/ppermute | solution.py:411
  5.6 7.8 %collective-permute-start.1 = (f32[256,128]{1,0:T(8,128)S(1)}, f32[256,128]{1,0:T(8,128)S(1)}, u32[]{:S(2)}, u32[]{:S(2)}) collective-permute-start(f32[256,128]{1,0:T(8,128)S(1)} %get-tuple-element.19), channel_id=1, source_target_pairs={{0,31},{1,0},{2,1},{3,2},{4,3},{5,4},{6,5},{7,6},{8,7},{9,8},{10,9... | collective-permute-start | bytes 393224 | tf_op jit(solution)/shard_map/ppermute | solution.py:411
  9.0 3.5 %collective-permute-start.2 = (f32[8,128]{1,0:T(8,128)S(1)}, f32[8,128]{1,0:T(8,128)S(1)}, u32[]{:S(2)}, u32[]{:S(2)}) collective-permute-start(f32[8,128]{1,0:T(8,128)S(1)} %get-tuple-element.20), channel_id=1, source_target_pairs={{0,8},{8,16},{16,24},{24,0},{1,9},{9,17},{17,25},{25,1},{2,10},{10... | collective-permute-start | bytes 12296 | tf_op jit(solution)/shard_map/ppermute | solution.py:411
  9.0 3.5 %collective-permute-start.3 = (f32[8,128]{1,0:T(8,128)S(1)}, f32[8,128]{1,0:T(8,128)S(1)}, u32[]{:S(2)}, u32[]{:S(2)}) collective-permute-start(f32[8,128]{1,0:T(8,128)S(1)} %get-tuple-element.21), channel_id=1, source_target_pairs={{0,24},{8,0},{16,8},{24,16},{1,25},{9,1},{17,9},{25,17},{2,26},{10... | collective-permute-start | bytes 12296 | tf_op jit(solution)/shard_map/ppermute | solution.py:411

commit v3 on v2

--- a/solution.py
+++ b/solution.py
@@ -48,7 +48,7 @@
     return starts
 
 
-def coefficient_kernel(mix_ref, weight_ref, carry_ref, back_ref, inverse_ref, d_ref, c_ref):
+def coefficients(mix_ref, weight_ref, carry_ref, back_ref, inverse_ref, d_ref, c_ref):
     tracers, levels = mix_ref.shape[0], mix_ref.shape[1] + 1
     slot = LANES // tracers
     lane = lax.broadcasted_iota(jnp.int32, (8, LANES), 1)
@@ -148,21 +148,61 @@
     return mask
 
 
-def solve_kernel(
-    groups, strips, rows,
-    cols_ref, offset_ref, flat_ref, before_ref, after_ref, left_ref, right_ref,
-    weight_ref, carry_ref, back_ref, inverse_ref, child_hbm, cwet_ref,
-    send_ref, pmid_ref, own_ref, cmid_ref,
-    explicit_ref, wide_ref, mask_ref, begin_ref, d_ref, turn_ref, end_ref, long_ref, child_ref, sems,
+def inner_kernel(
+    cols_ref, mix_ref, child_ref, cwet_ref,
+    weight_ref, carry_ref, back_ref, inverse_ref, explicit_ref,
+    mask_ref, begin_ref, d_ref, c_ref,
 ):
     levels, capacity, tracers, child_rows = child_ref.shape
-    chunks = sems.shape[0]
-    step = -(-levels // chunks)
-    fetches = []
-    for c in range(chunks):
-        part = pl.ds(c * step, min(levels, (c + 1) * step) - c * step)
-        fetches.append(pltpu.make_async_copy(child_hbm.at[part], child_ref.at[part], sems.at[c]))
-        fetches[-1].start()
+    tiles = tile_list(child_rows)
+    live = capacity * tracers
+    stored = up(live, 8)
+    stride = begin_ref.shape[1] // levels
+    coefficients(mix_ref, weight_ref, carry_ref, back_ref, inverse_ref, d_ref, c_ref)
+    masks(cols_ref, cwet_ref, mask_ref, tracers)
+    flat_child = child_ref.reshape(levels * live, child_rows)
+    lane = lax.broadcasted_iota(jnp.int32, (stored, LANES), 1)
+    gap = jnp.zeros((tracers, LANES), jnp.float32)
+    after = stored - live + tracers
+
+    def explicit(l, carry):
+        cells = flat_child[pl.ds(pl.multiple_of(l * live, 2), live), :]
+        start = pl.multiple_of(l * stride, 8)
+        for n, size in tiles:
+            part = cells[:, n * LANES : n * LANES + size] * mask_ref[n, :live, :size]
+            if size < LANES:
+                part = jnp.concatenate([part, jnp.zeros((live, LANES - size), jnp.float32)], axis=1)
+            begin_ref[n, pl.ds(start + 8, live), :] = part
+            begin_ref[n, pl.ds(start + 8 - tracers, tracers), :] = gap
+            begin_ref[n, pl.ds(start + 8 + live, after), :] = jnp.zeros((after, LANES), jnp.float32)
+        here = [begin_ref[n, pl.ds(start + 8, stored), :] for n, _ in tiles]
+        lower = [pltpu.roll(c, 1, 1) for c in here]
+        upper = [pltpu.roll(c, LANES - 1, 1) for c in here]
+        for n, size in tiles:
+            south = jnp.where(lane == 0, lower[n - 1] if n else 0.0, lower[n])
+            if n + 1 < len(tiles):
+                north = jnp.where(lane == LANES - 1, upper[n + 1], upper[n])
+            else:
+                north = jnp.where(lane == size - 1, 0.0, upper[n])
+            west = begin_ref[n, pl.ds(start + 8 - tracers, stored), :]
+            east = begin_ref[n, pl.ds(start + 8 + tracers, stored), :]
+            explicit_ref[n, pl.ds(pl.multiple_of(l * stored, 8), stored), :] = (diffusion * mask_ref[n]) * (
+                here[n] + west + east + south + north
+            )
+        return carry
+
+    lax.fori_loop(0, levels, explicit, 0, unroll=10 if levels % 10 == 0 else 1)
+
+
+def pack_kernel(
+    groups, strips, rows, tracers, levels,
+    cols_ref, offset_ref, flat_ref, before_ref, after_ref, left_ref, right_ref, inverse_ref, explicit_ref, cwet_ref,
+    *refs,
+):
+    send_refs = refs[:strips]
+    pmid_ref, own_ref, halo_ref, step_ref, wide_ref, turn_ref, end_ref, long_ref, start_ref = refs[strips:]
+    capacity, child_rows = cwet_ref.shape
+    stored = up(capacity * tracers, 8)
     slot = LANES // tracers
     width = flat_ref.shape[0] // rows
     narrow = capacity // 3
@@ -171,20 +211,16 @@
     tiles = tile_list(child_rows)
     level_rows = up(tracers * levels, 8)
     base = len(tiles) * level_rows
-    live = capacity * tracers
-    stored = up(live, 8)
-    stride = begin_ref.shape[1] // levels
-    member = lax.axis_index("child")
-    starts = strip_starts(cols_ref, strips)
+    group, member = lax.axis_index("parent"), lax.axis_index("child")
     offset = offset_ref[0]
-
-    group = lax.axis_index("parent")
+    cols = my_cols(cols_ref)
+    for j, start in enumerate(strip_starts(cols_ref, strips)):
+        start_ref[j] = start
+
     has_before = (member > 0).astype(jnp.float32)
     has_after = (member < strips - 1).astype(jnp.float32)
     has_left = (group > 0).astype(jnp.float32)
     has_right = (group < groups - 1).astype(jnp.float32)
-    chain_before = jnp.maximum(has_before, has_left)
-    chain_after = jnp.maximum(has_after, has_right)
     for x in range(width):
         here = flat_ref[x * rows : (x + 1) * rows, :]
         west = has_left * left_ref[...] if x == 0 else flat_ref[(x - 1) * rows : x * rows, :]
@@ -193,78 +229,29 @@
         north = jnp.concatenate([here[1:], has_after * after_ref[base + x : base + x + 1, :]], axis=0)
         wet = here[:, levels : levels + 1]
         laplace = north + south + east + west - 4.0 * here
-        explicit_ref[x * rows : (x + 1) * rows, :] = wet * (here + diffusion * laplace)
-    solved = jnp.dot(explicit_ref[...], inverse_ref[...], precision=HIGH, preferred_element_type=jnp.float32)
+        step_ref[x * rows : (x + 1) * rows, :] = wet * (here + diffusion * laplace)
+    solved = jnp.dot(step_ref[...], inverse_ref[...], precision=HIGH, preferred_element_type=jnp.float32)
     lane = lax.broadcasted_iota(jnp.int32, (width * rows, LANES), 1)
     solved = jnp.where(lane == levels, flat_ref[...], solved)
     wide_ref[: width * rows, :] = solved
     wide_ref[width * rows :, :] = jnp.zeros((narrow * rows, LANES), jnp.float32)
     pmid_ref[...] = solved
-    for j in range(strips):
-        send_ref[j, : narrow * rows, :] = wide_ref[pl.ds(pl.multiple_of(starts[j] * rows, rows), narrow * rows), :]
-
-    mask = masks(cols_ref, cwet_ref, mask_ref, tracers)
-    flat_child = child_ref.reshape(levels * live, child_rows)
-    lane = lax.broadcasted_iota(jnp.int32, (stored, LANES), 1)
-    past = 8 + 3 * tracers * my_cols(cols_ref)
+    for s in range(strips):
+        start = start_ref[member ^ s]
+        send_refs[s][: narrow * rows, :] = wide_ref[pl.ds(pl.multiple_of(start * rows, rows), narrow * rows), :]
+
+    column = lax.broadcasted_iota(jnp.int32, (capacity, 1), 0)
+    mask = cwet_ref[...].astype(jnp.float32) * (column < 3 * cols).astype(jnp.float32)
+    west_mask = (diffusion * jnp.maximum(has_before, has_left)) * mask[:1]
+    east_wet = cwet_ref[pl.ds(3 * cols - 1, 1), :].astype(jnp.float32)
+    east_mask = (diffusion * jnp.maximum(has_after, has_right)) * east_wet
+    halo_ref[...] = jnp.zeros_like(halo_ref)
     for n, size in tiles:
-        if size < LANES:
-            begin_ref[n] = jnp.zeros((levels * stride, LANES), jnp.float32)
-
-    def begin(l, carry):
-        cells = flat_child[pl.ds(pl.multiple_of(l * live, 2), live), :]
-        start = pl.multiple_of(l * stride, 8)
-        for n, size in tiles:
-            part = cells[:, n * LANES : n * LANES + size] * mask_ref[n, :live, :size]
-            begin_ref[n, pl.ds(start + 8, live), :size] = part
-            edge = pl.ds(n * level_rows + l * tracers, tracers)
-            begin_ref[n, pl.ds(start + 8 - tracers, tracers), :size] = chain_before * before_ref[edge, :size]
-            begin_ref[n, pl.ds(start + past, tracers), :size] = chain_after * after_ref[edge, :size]
-        return carry
-
-    for c in range(chunks):
-        fetches[c].wait()
-        lax.fori_loop(c * step, min(levels, (c + 1) * step), begin, 0, unroll=2)
-
-    def by_rows(factor, value):
-        return (factor[None] * value.reshape(stored // 8, 8, LANES)).reshape(stored, LANES)
-
-    def forward(l, carry):
-        start = pl.multiple_of(l * stride, 8)
-        coef = pl.ds(pl.multiple_of(l * 8, 8), 8)
-        cells = [begin_ref[n, pl.ds(start + 8, stored), :] for n, _ in tiles]
-        lower = [pltpu.roll(c, 1, 1) for c in cells]
-        upper = [pltpu.roll(c, LANES - 1, 1) for c in cells]
-        held = []
-        for n, size in tiles:
-            south = jnp.where(lane == 0, lower[n - 1] if n else 0.0, lower[n])
-            if n + 1 < len(tiles):
-                north = jnp.where(lane == LANES - 1, upper[n + 1], upper[n])
-            else:
-                north = jnp.where(lane == size - 1, 0.0, upper[n])
-            west = begin_ref[n, pl.ds(start + 8 - tracers, stored), :]
-            east = begin_ref[n, pl.ds(start + 8 + tracers, stored), :]
-            explicit = (diffusion * mask_ref[n]) * (cells[n] + west + east + south + north)
-            d = by_rows(weight_ref[coef, :], explicit) + by_rows(carry_ref[coef, :], carry[n])
-            d_ref[n, pl.ds(pl.multiple_of(l * stored, 8), stored), :] = d
-            held.append(d)
-        return tuple(held)
-
-    blank = jnp.zeros((stored, LANES), jnp.float32)
-    lax.fori_loop(0, levels, forward, (blank,) * len(tiles), unroll=2)
-
-    def backward(step, carry):
-        l = levels - 1 - step
-        coef = pl.ds(pl.multiple_of(l * 8, 8), 8)
-        at = pl.ds(pl.multiple_of(l * stored, 8), stored)
-        held = []
-        for n, _ in tiles:
-            x = d_ref[n, at, :] + by_rows(back_ref[coef, :], carry[n])
-            cmid_ref[n, at, :] = x
-            held.append(x)
-        return tuple(held)
-
-    lax.fori_loop(0, levels, backward, (blank,) * len(tiles), unroll=2)
+        part = slice(n * LANES, n * LANES + size)
+        for l in range(levels):
+            edge = slice(n * level_rows + l * tracers, n * level_rows + (l + 1) * tracers)
+            halo_ref[n, 8 * l : 8 * l + tracers, :size] = west_mask[:, part] * before_ref[edge, :size]
+            halo_ref[n, 8 * l + tracers : 8 * l + 2 * tracers, :size] = east_mask[:, part] * after_ref[edge, :size]
 
     own_ref[...] = jnp.zeros_like(own_ref)
     turn_ref[...] = jnp.zeros_like(turn_ref)
@@ -275,12 +262,15 @@
     packs = LANES // tail_size
     for q in range(narrow):
         count = (mask[3 * q : 3 * q + 1] + mask[3 * q + 1 : 3 * q + 2] + mask[3 * q + 2 : 3 * q + 3]) * at_end
+        is_last = (cols == q + 1).astype(jnp.float32)
         for n, size in tiles:
             into, low = (turn_ref, 0) if n < tail else (end_ref.at[q // packs], (q % packs) * size)
             for t in range(tracers):
-                part = sum(
-                    cmid_ref[n, pl.ds((3 * q + dx) * tracers + t, levels, stride=stored), :] for dx in range(3)
-                )
+                part = is_last * halo_ref[n, pl.ds(tracers + t, levels, stride=8), :]
+                if q == 0:
+                    part = part + halo_ref[n, pl.ds(t, levels, stride=8), :]
+                for dx in range(3):
+                    part = part + explicit_ref[n, pl.ds((3 * q + dx) * tracers + t, levels, stride=stored), :]
                 into[t * slot : t * slot + levels, low : low + size] = part[:, :size]
             into[levels : levels + 1, low : low + size] = count[:, n * LANES : n * LANES + size]
             if n < tail:
@@ -298,19 +288,80 @@
             + long_ref[pl.ds(q * child_rows + 2, covered, stride=3), :]
         )
         own_ref[pl.ds(q * all_rows + offset, covered), :] = mean
-    for k in range(strips):
+    for s in range(strips):
+        band = (member ^ s) * rows
         for q in range(narrow):
-            send_ref[k, (narrow + q) * rows : (narrow + q + 1) * rows, :] = own_ref[
-                q * all_rows + k * rows : q * all_rows + (k + 1) * rows, :
+            send_refs[s][(narrow + q) * rows : (narrow + q + 1) * rows, :] = own_ref[
+                pl.ds(pl.multiple_of(q * all_rows + band, rows), rows), :
             ]
+
+
+def level_kernel(
+    tracers, levels, capacity,
+    cols_ref, weight_ref, carry_ref, back_ref, inverse_ref, explicit_ref, halo_ref, own_ref,
+    cmid_ref, mean_ref,
+    d_ref, h_ref,
+):
+    count = explicit_ref.shape[0]
+    stored = explicit_ref.shape[1] // levels
+    past = 3 * tracers * my_cols(cols_ref) - tracers
+
+    def by_rows(factor, value):
+        return (factor[None] * value.reshape(stored // 8, 8, LANES)).reshape(stored, LANES)
+
+    def forward(l, carry):
+        at = pl.ds(pl.multiple_of(l * stored, 8), stored)
+        coef = pl.ds(pl.multiple_of(l * 8, 8), 8)
+        weight, above = weight_ref[coef, :], carry_ref[coef, :]
+        held = []
+        for n in range(count):
+            d = by_rows(weight, explicit_ref[n, at, :]) + by_rows(above, carry[2 * n])
+            h = weight * halo_ref[n, coef, :] + above * carry[2 * n + 1]
+            d_ref[n, at, :] = d
+            h_ref[n, coef, :] = h
+            held += [d, h]
+        return tuple(held)
+
+    blank = (jnp.zeros((stored, LANES), jnp.float32), jnp.zeros((8, LANES), jnp.float32)) * count
+    unroll = 5 if levels % 5 == 0 else 1
+    lax.fori_loop(0, levels, forward, blank, unroll=unroll)
+
+    def backward(step, carry):
+        l = levels - 1 - step
+        start = pl.multiple_of(l * stored, 8)
+        at = pl.ds(start, stored)
+        coef = pl.ds(pl.multiple_of(l * 8, 8), 8)
+        below = back_ref[coef, :]
+        held = []
+        for n in range(count):
+            x = d_ref[n, at, :] + by_rows(below, carry[2 * n])
+            h = h_ref[n, coef, :] + below * carry[2 * n + 1]
+            cmid_ref[n, at, :] = x
+            first = pl.ds(start, tracers)
+            cmid_ref[n, first, :] = cmid_ref[n, first, :] + h[:tracers]
+            last = pl.ds(start + past, tracers)
+            cmid_ref[n, last, :] = cmid_ref[n, last, :] + h[tracers : 2 * tracers]
+            held += [x, h]
+        return tuple(held)
+
+    lax.fori_loop(0, levels, backward, blank, unroll=unroll)
+    own = own_ref[...]
+    solved = jnp.dot(own, inverse_ref[...], precision=HIGH, preferred_element_type=jnp.float32)
+    lane = lax.broadcasted_iota(jnp.int32, own.shape, 1)
+    mean_ref[...] = jnp.where(lane == levels, own, solved)
 
 
 def finish_kernel(
     strips, rows, chunks,
-    cols_ref, offset_ref, got_ref, own_ref, pmid_ref, inverse_ref, cmid_ref, cwet_ref,
-    pnext_hbm, cnext_hbm,
-    panel_ref, wide_ref, ends_ref, long_ref, end_ref, add_ref, mask_ref, next_ref, pkeep_ref, ckeep_ref, sems,
+    cols_ref, offset_ref, own_ref, pmid_ref, inverse_ref, cmid_ref, cwet_ref,
+    *refs,
 ):
+    got_refs = refs[:strips]
+    (
+        pnext_hbm, cnext_hbm,
+        panel_ref, wide_ref, ends_ref, long_ref, end_ref, add_ref, mask_ref, next_ref, pkeep_ref, ckeep_ref,
+        start_ref, sems,
+    ) = refs[strips:]
     levels, capacity, tracers, child_rows = cnext_hbm.shape
     slot = LANES // tracers
     width = pmid_ref.shape[0] // rows
@@ -322,32 +373,17 @@
     stored = up(live, 8)
     padded = up(narrow, 8)
     member = lax.axis_index("child")
-    starts = strip_starts(cols_ref, strips)
+    group = lax.axis_index("parent")
+    for j, start in enumerate(strip_starts(cols_ref, strips)):
+        start_ref[j] = start
     offset = offset_ref[0]
     masks(cols_ref, cwet_ref, mask_ref, tracers)
 
-    for j in range(strips):
-        wide_ref[pl.ds(pl.multiple_of(starts[j] * rows, rows), narrow * rows), :] = got_ref[j, narrow * rows :, :]
-    mean = wide_ref[: width * rows, :]
-    pmid = pmid_ref[...]
-    twice = jnp.dot(pmid, inverse_ref[...], precision=HIGH, preferred_element_type=jnp.float32)
-    coarse = mean + diffusion * mean[:, levels : levels + 1] * twice
-    row = member * rows + lax.broadcasted_iota(jnp.int32, (width * rows, 1), 0) % rows
-    inside = (row >= offset) & (row < offset + covered)
-    next_ref[...] = pmid[:, levels : levels + 1] * jnp.where(inside, coarse, pmid)
-    for r in range(rows):
-        block = next_ref[pl.ds(r, width, stride=rows), :]
-        for t in range(tracers):
-            pkeep_ref[t, r] = block[:, t * slot : t * slot + levels]
-    send_parent = pltpu.make_async_copy(pkeep_ref, pnext_hbm, sems.at[0])
-    send_parent.start()
-
     ends_ref[...] = jnp.zeros_like(ends_ref)
     for q in range(narrow):
-        for k in range(strips):
-            panel_ref[q * all_rows + k * rows : q * all_rows + (k + 1) * rows, :] = got_ref[
-                k, q * rows : (q + 1) * rows, :
-            ]
+        for s in range(strips):
+            at = pl.ds(pl.multiple_of(q * all_rows + (member ^ s) * rows, rows), rows)
+            panel_ref[at, :] = got_refs[s][q * rows : (q + 1) * rows, :]
         ends_ref[q : q + 1, :] = panel_ref[pl.ds(q * all_rows + offset, 1), :]
         ends_ref[padded + q : padded + q + 1, :] = panel_ref[pl.ds(q * all_rows + offset + covered - 1, 1), :]
     solved_ends = jnp.dot(ends_ref[...], inverse_ref[...], precision=HIGH, preferred_element_type=jnp.float32)
@@ -395,7 +431,7 @@
         flat_next[pl.ds(pl.multiple_of(l * live, 2), live), :] = jnp.concatenate(parts, axis=1)
         return carry
 
-    sends = [send_parent]
+    sends = []
     step = -(-levels // chunks)
     for c in range(chunks):
         low, high = c * step, min(levels, (c + 1) * step)
@@ -403,6 +439,29 @@
         part = pl.ds(low, high - low)
         sends.append(pltpu.make_async_copy(ckeep_ref.at[part], cnext_hbm.at[part], sems.at[1 + c]))
         sends[-1].start()
+
+    for s in range(strips):
+        j = member ^ s
+        start, cols = start_ref[j], cols_ref[group, j]
+        for q in range(narrow):
+            to = jnp.where(q < cols, start + q, width + q)
+            wide_ref[pl.ds(pl.multiple_of(to * rows, rows), rows), :] = got_refs[s][
+                (narrow + q) * rows : (narrow + q + 1) * rows, :
+            ]
+    pmid = pmid_ref[...]
+    mean = wide_ref[: width * rows, :]
+    mean = mean + diffusion * mean[:, levels : levels + 1] * pmid
+    coarse = jnp.dot(mean, inverse_ref[...], precision=HIGH, preferred_element_type=jnp.float32)
+    row = member * rows + lax.broadcasted_iota(jnp.int32, (width * rows, 1), 0) % rows
+    inside = (row >= offset) & (row < offset + covered)
+    next_ref[...] = pmid[:, levels : levels + 1] * jnp.where(inside, coarse, pmid)
+    for r in range(rows):
+        block = next_ref[pl.ds(r, width, stride=rows), :]
+        for t in range(tracers):
+            pkeep_ref[t, r] = block[:, t * slot : t * slot + levels]
+    send_parent = pltpu.make_async_copy(pkeep_ref, pnext_hbm, sems.at[0])
+    send_parent.start()
+    sends.append(send_parent)
     for send in sends:
         send.wait()
 
@@ -457,50 +516,57 @@
     forth = ring(forth, ("parent", "child"), devices, 1)
     back = ring(back, ("parent", "child"), devices, -1)
 
-    weight, carry, below, inverse = pl.pallas_call(
-        coefficient_kernel,
-        in_specs=[SM],
-        out_specs=[VM] * 4,
-        out_shape=[f32(8 * levels, LANES)] * 3 + [f32(LANES, LANES)],
-        scratch_shapes=[mem(8 * levels, LANES), mem(8 * levels, LANES)],
-        compiler_params=params(8),
-        name="coefficients",
-    )(vert_mix)
-
-    send, parent_mid, own, child_mid = pl.pallas_call(
-        functools.partial(solve_kernel, groups, strips, rows),
-        in_specs=[SM, SM] + [VM] * 9 + [HBM, VM],
-        out_specs=[VM] * 4,
-        out_shape=[
-            f32(strips, 2 * narrow * rows, LANES),
-            f32(width * rows, LANES),
-            f32(narrow * all_rows, LANES),
-            f32(lane_tiles, levels * stored, LANES),
+    weight, carry, below, inverse, explicit = pl.pallas_call(
+        inner_kernel,
+        in_specs=[SM, SM, VM, VM],
+        out_specs=[VM] * 5,
+        out_shape=[f32(8 * levels, LANES)] * 3 + [f32(LANES, LANES), f32(lane_tiles, levels * stored, LANES)],
+        scratch_shapes=[
+            mem(lane_tiles, stored, LANES),
+            mem(lane_tiles, levels * stride, LANES),
+            mem(8 * levels, LANES),
+            mem(8 * levels, LANES),
         ],
+        compiler_params=params(16),
+        name="inner",
+    )(strip_cols, vert_mix, child, child_wet)
+
+    block = f32(2 * narrow * rows, LANES)
+    *blocks, parent_mid, own, halo = pl.pallas_call(
+        functools.partial(pack_kernel, groups, strips, rows, tracers, levels),
+        in_specs=[SM, SM] + [VM] * 8,
+        out_specs=[VM] * (strips + 3),
+        out_shape=[block] * strips
+        + [f32(width * rows, LANES), f32(narrow * all_rows, LANES), f32(lane_tiles, 8 * levels, LANES)],
         scratch_shapes=[
             mem(width * rows, LANES),
             mem((width + narrow) * rows, LANES),
-            mem(lane_tiles, stored, LANES),
-            mem(lane_tiles, levels * stride, LANES),
-            mem(lane_tiles, levels * stored, LANES),
             mem(LANES, LANES),
             mem(packed, LANES, LANES),
             mem(narrow * child_rows, LANES),
-            mem(*child.shape),
-            pltpu.SemaphoreType.DMA((chunks,)),
+            pltpu.SMEM((strips,), jnp.int32),
         ],
-        compiler_params=params(32),
-        name="solve",
-    )(
-        strip_cols, row_offset, flat, forth, back, right_edge, left_edge,
-        weight, carry, below, inverse, in_hbm(child), child_wet,
-    )
-
-    got = lax.all_to_all(send, "child", 0, 0)
+        compiler_params=params(16),
+        name="pack",
+    )(strip_cols, row_offset, flat, forth, back, right_edge, left_edge, inverse, explicit, child_wet)
+
+    got = [blocks[0]] + [
+        lax.ppermute(blocks[s], "child", [(i, i ^ s) for i in range(strips)]) for s in range(1, strips)
+    ]
+
+    child_mid, mean = pl.pallas_call(
+        functools.partial(level_kernel, tracers, levels, capacity),
+        in_specs=[SM] + [VM] * 7,
+        out_specs=[VM, VM],
+        out_shape=[f32(lane_tiles, levels * stored, LANES), f32(narrow * all_rows, LANES)],
+        scratch_shapes=[mem(lane_tiles, levels * stored, LANES), mem(lane_tiles, 8 * levels, LANES)],
+        compiler_params=params(16),
+        name="levels",
+    )(strip_cols, weight, carry, below, inverse, explicit, halo, own)
 
     parent_next, child_next = pl.pallas_call(
         functools.partial(finish_kernel, strips, rows, chunks),
-        in_specs=[SM, SM] + [VM] * 6,
+        in_specs=[SM, SM] + [VM] * (5 + strips),
         out_specs=[HBM, HBM],
         out_shape=[f32(*parent.shape), f32(*child.shape)],
         scratch_shapes=[
@@ -514,11 +580,12 @@
             mem(width * rows, LANES),
             mem(*parent.shape),
             mem(*child.shape),
+            pltpu.SMEM((strips,), jnp.int32),
             pltpu.SemaphoreType.DMA((1 + chunks,)),
         ],
-        compiler_params=params(32),
+        compiler_params=params(24),
         name="finish",
-    )(strip_cols, row_offset, got, own, parent_mid, inverse, child_mid, child_wet)
+    )(strip_cols, row_offset, mean, parent_mid, inverse, child_mid, child_wet, *got)
     return jnp.transpose(parent_next, (0, 3, 1, 2)), jnp.transpose(child_next, (2, 0, 1, 3))
 
 

time: 46.6 us -> 38 us (0.82)
  blocking collectives: 21.9 us -> 0 us
  starting transfers between devices: 8.24 us -> 19.4 us
  waiting for transfers between devices: 0.77 us -> 3.11 us
    all_to_all x1 -> x0, blocking collectives: 21.9 us -> none  [body(): got = lax.all_to_all(send, 'child', 0, 0)]
    ppermute x0 -> x7, starting transfers between devices: none -> 11.2 us  [body(): lax.ppermute(blocks[s], 'child', [(i, i ^ s) for i in range(strips)])]
    ppermute x0 -> x7, waiting for transfers between devices: none -> 3.1 us  [body(): lax.ppermute(blocks[s], 'child', [(i, i ^ s) for i in range(strips)])]
    pallas_call x2 -> x3, Pallas kernels: 8.84 us -> 7.97 us  [the longest x1 3.93 us: body(): pl.pallas_call(inner_kernel, in_specs=[SM, SM, VM, VM], out_specs=[VM] *...]
    ppermute x4, waiting for transfers between devices: 0.77 us -> 0.01 us  [ring(): lax.ppermute(block, axes, [(i, (i + step) % count) for i in range(count)])]
  transfers between devices with their start and end apart: 4 -> 11, of which waited for: 2 -> 2; matrix products, arithmetic and copies ran while one was open for 0% -> 0% of each run, Pallas kernels for 2% -> 17%
where the time goes in v3:
time: 38 us; the launch traced here: 37.8 us
  starting transfers between devices  19.4 us (51%)
  Pallas kernels  13.8 us (36%)
  waiting for transfers between devices  3.11 us (8%)
  between operations  1.43 us (4%)
    ppermute x7, starting transfers between devices, body(): lax.ppermute(blocks[s], 'child', [(i, i ^ s) for i in range(strips)])  11.2 us
    ppermute x4, starting transfers between devices, ring(): lax.ppermute(block, axes, [(i, (i + step) % count) for i in range(count)])  8.24 us
    pallas_call x1, Pallas kernels, body(): pl.pallas_call(inner_kernel, in_specs=[SM, SM, VM, VM], out_specs=[VM] *...  3.93 us
    pallas_call x1, Pallas kernels, body(): pl.pallas_call(functools.partial(finish_kernel, strips, rows, chunks), in...  3.76 us
    ppermute x7, waiting for transfers between devices, body(): lax.ppermute(blocks[s], 'child', [(i, i ^ s) for i in range(strips)])  3.1 us
    pallas_call x1, Pallas kernels, body(): pl.pallas_call(functools.partial(level_kernel, tracers, levels, capacity)...  2.41 us
    pallas_call x1, Pallas kernels, body(): pl.pallas_call(prepare_kernel, in_specs=[HBM] * 5, out_specs=[VM] * 5, ou...  2.08 us
    pallas_call x1, Pallas kernels, body(): pl.pallas_call(functools.partial(pack_kernel, groups, strips, rows, trace...  1.63 us
  transfers between devices with their start and end apart: 11, of which 2 were waited for; matrix products, arithmetic and copies ran while one was open for 0% of the time, Pallas kernels for 17%

profile of v3, /device:TPU:0, one launch (start us, length us, event | category | flops | bytes accessed | tf_op | source)
XLA Modules:
  0.0 37.8 jit_solution(7013550678029633886)
XLA Ops:
  0.6 0.0 copy-start.2
  0.6 0.0 copy-start.1
  0.7 0.0 copy-start
  0.7 0.0 copy-start.3
  0.7 2.1 %prepare.1 = (f32[384,128]{1,0:T(8,128)S(1)}, f32[256,128]{1,0:T(8,128)S(1)}, f32[256,128]{1,0:T(8,128)S(1)}, f32[8,128]{1,0:T(8,128)S(1)}, f32[8,128]{1,0:T(8,128)S(1)}) custom-call(s32[4,8]{1,0:T(4,128)} %cols_ref.7, f32[2,8,48,50]{3,2,1,0:T(8,128)} %bitcast.6, s32[8,48]{1,0:T(8,128)} %pwet_hbm.1, f32[50,27,2,144]{3,2,1,0:T(2,128)} %bitcast.4, ...), custom_call_target="tpu_custom_call" | custom-call | tf_op jit(solution)/shard_map/prepare/pallas_call | solution.py:491
  2.8 3.0 %collective-permute-start = (f32[256,128]{1,0:T(8,128)S(1)}, f32[256,128]{1,0:T(8,128)S(1)}, u32[]{:S(2)}, u32[]{:S(2)}) collective-permute-start(f32[256,128]{1,0:T(8,128)S(1)} %get-tuple-element.33), channel_id=1, source_target_pairs={{0,1},{1,2},{2,3},{3,4},{4,5},{5,6},{6,7},{7,8},{8,9},{9,10},{10,1... | collective-permute-start | bytes 393224 | tf_op jit(solution)/shard_map/ppermute | solution.py:470
  5.8 3.5 %collective-permute-start.1 = (f32[256,128]{1,0:T(8,128)S(1)}, f32[256,128]{1,0:T(8,128)S(1)}, u32[]{:S(2)}, u32[]{:S(2)}) collective-permute-start(f32[256,128]{1,0:T(8,128)S(1)} %get-tuple-element.34), channel_id=1, source_target_pairs={{0,31},{1,0},{2,1},{3,2},{4,3},{5,4},{6,5},{7,6},{8,7},{9,8},{10,9... | collective-permute-start | bytes 393224 | tf_op jit(solution)/shard_map/ppermute | solution.py:470
  9.3 0.0 collective-permute-start.2
  9.3 1.7 %collective-permute-start.3 = (f32[8,128]{1,0:T(8,128)S(1)}, f32[8,128]{1,0:T(8,128)S(1)}, u32[]{:S(2)}, u32[]{:S(2)}) collective-permute-start(f32[8,128]{1,0:T(8,128)S(1)} %get-tuple-element.36), channel_id=1, source_target_pairs={{0,24},{8,0},{16,8},{24,16},{1,25},{9,1},{17,9},{25,17},{2,26},{10... | collective-permute-start | bytes 12296 | tf_op jit(solution)/shard_map/ppermute | solution.py:470
  11.7 0.0 copy-done.2
  11.7 3.9 %inner.1 = (f32[400,128]{1,0:T(8,128)S(1)}, f32[400,128]{1,0:T(8,128)S(1)}, f32[400,128]{1,0:T(8,128)S(1)}, f32[128,128]{1,0:T(8,128)S(1)}, f32[2,2800,128]{2,1,0:T(8,128)S(1)}) custom-call(s32[4,8]{1,0:T(4,128)S(1)} %copy-done.2, f32[2,49]{1,0:T(2,128)S(1)} %copy-done.3, f32[50,27,2,144]{3,2,1,0:T(2,128)S(1)} %bitcast.5, s32[27,144]{1,0:T(8,128)S(1)} %copy-done.1), custom_call_target="tpu_custom_call" | custom-call | tf_op jit(solution)/shard_map/inner/pallas_call | solution.py:519
  15.6 0.0 collective-permute-done.2.left_ref
  15.6 0.0 collective-permute-done.3.right_ref
  15.7 0.0 collective-permute-done.before_ref
  15.7 0.0 collective-permute-done.1.after_ref
  15.7 1.6 %pack.1 = (f32[144,128]{1,0:T(8,128)S(1)}, f32[144,128]{1,0:T(8,128)S(1)}, f32[144,128]{1,0:T(8,128)S(1)}, f32[144,128]{1,0:T(8,128)S(1)}, f32[144,128]{1,0:T(8,...) custom-call(s32[4,8]{1,0:T(4,128)S(1)} %copy-done.2, ...), custom_call_target="tpu_custom_call" | custom-call | tf_op jit(solution)/shard_map/pack/pallas_call | solution.py:535
  17.3 0.1 collective-permute-start.4
  17.4 0.1 collective-permute-start.5
  17.5 3.4 %collective-permute-start.6 = (f32[144,128]{1,0:T(8,128)S(1)}, f32[144,128]{1,0:T(8,128)S(1)}, u32[]{:S(2)}, u32[]{:S(2)}) collective-permute-start(f32[144,128]{1,0:T(8,128)S(1)} %get-tuple-element.45), channel_id=1, source_target_pairs={{0,3},{1,2},{2,1},{3,0},{4,7},{5,6},{6,5},{7,4},{8,11},{9,10},{10,... | collective-permute-start | bytes 221192 | tf_op jit(solution)/shard_map/ppermute | solution.py:554
  20.9 0.5 %collective-permute-start.7 = (f32[144,128]{1,0:T(8,128)S(1)}, f32[144,128]{1,0:T(8,128)S(1)}, u32[]{:S(2)}, u32[]{:S(2)}) collective-permute-start(f32[144,128]{1,0:T(8,128)S(1)} %get-tuple-element.46), channel_id=1, source_target_pairs={{0,4},{1,5},{2,6},{3,7},{4,0},{5,1},{6,2},{7,3},{8,12},{9,13},{10,... | collective-permute-start | bytes 221192 | tf_op jit(solution)/shard_map/ppermute | solution.py:554
  21.4 1.9 %collective-permute-start.8 = (f32[144,128]{1,0:T(8,128)S(1)}, f32[144,128]{1,0:T(8,128)S(1)}, u32[]{:S(2)}, u32[]{:S(2)}) collective-permute-start(f32[144,128]{1,0:T(8,128)S(1)} %get-tuple-element.47), channel_id=1, source_target_pairs={{0,5},{1,4},{2,7},{3,6},{4,1},{5,0},{6,3},{7,2},{8,13},{9,12},{10,... | collective-permute-start | bytes 221192 | tf_op jit(solution)/shard_map/ppermute | solution.py:554
  23.3 0.0 collective-permute-done.4.refs_1_
  23.3 2.1 %collective-permute-start.9 = (f32[144,128]{1,0:T(8,128)S(1)}, f32[144,128]{1,0:T(8,128)S(1)}, u32[]{:S(2)}, u32[]{:S(2)}) collective-permute-start(f32[144,128]{1,0:T(8,128)S(1)} %get-tuple-element.48), channel_id=1, source_target_pairs={{0,6},{1,7},{2,4},{3,5},{4,2},{5,3},{6,0},{7,1},{8,14},{9,15},{10,... | collective-permute-start | bytes 221192 | tf_op jit(solution)/shard_map/ppermute | solution.py:554
  25.4 0.0 collective-permute-done.5.refs_2_
  25.4 3.1 %collective-permute-start.10 = (f32[144,128]{1,0:T(8,128)S(1)}, f32[144,128]{1,0:T(8,128)S(1)}, u32[]{:S(2)}, u32[]{:S(2)}) collective-permute-start(f32[144,128]{1,0:T(8,128)S(1)} %get-tuple-element.49), channel_id=1, source_target_pairs={{0,7},{1,6},{2,5},{3,4},{4,3},{5,2},{6,1},{7,0},{8,15},{9,14},{10,... | collective-permute-start | bytes 221192 | tf_op jit(solution)/shard_map/ppermute | solution.py:554
  28.5 2.4 %levels.1 = (f32[2,2800,128]{2,1,0:T(8,128)S(1)}, f32[576,128]{1,0:T(8,128)S(1)}) custom-call(s32[4,8]{1,0:T(4,128)S(1)} %copy-done.2, f32[400,128]{1,0:T(8,128)S(1)} %get-tuple-element.27.weight_ref, f32[400,128]{1,0:T(8,128)S(1)} %get-tuple-element.28.carry_ref, f32[400,128]{1,0:T(8,128)S(1)} %get-tuple-element.29.back_ref, ...), custom_call_target="tpu_custom_call" | custom-call | tf_op jit(solution)/shard_map/levels/pallas_call | solution.py:557
  30.9 0.0 collective-permute-done.6.refs_3_
  30.9 0.5 %collective-permute-done.7.refs_4_ = f32[144,128]{1,0:T(8,128)S(1)} collective-permute-done((f32[144,128]{1,0:T(8,128)S(1)}, f32[144,128]{1,0:T(8,128)S(1)}, u32[]{:S(2)}, u32[]{:S(2)}) %collective-permute-start.7) | collective-permute-done | bytes 73760 | tf_op jit(solution)/shard_map/ppermute | solution.py:554
  31.4 2.6 %collective-permute-done.8.refs_5_ = f32[144,128]{1,0:T(8,128)S(1)} collective-permute-done((f32[144,128]{1,0:T(8,128)S(1)}, f32[144,128]{1,0:T(8,128)S(1)}, u32[]{:S(2)}, u32[]{:S(2)}) %collective-permute-start.8) | collective-permute-done | bytes 73760 | tf_op jit(solution)/shard_map/ppermute | solution.py:554
  34.0 0.0 collective-permute-done.9.refs_6_
  34.0 0.0 collective-permute-done.10.refs_7_
  34.0 3.8 %finish.1 = (f32[2,8,48,50]{3,2,1,0:T(8,128)}, f32[50,27,2,144]{3,2,1,0:T(2,128)}) custom-call(s32[4,8]{1,0:T(4,128)S(1)} %copy-done.2, s32[1]{0:T(128)S(6)} %copy.9.offset_ref, f32[576,128]{1,0:T(8,128)S(1)} %get-tuple-element.39.own_ref, f32[384,128]{1,0:T(8,128)S(1)} %get-tuple-element.40.pmid_ref, f32[128,128]{1,0:T(8,128)S(1)} %get-tuple-element.30.inverse_ref, ...), custom_call_target="tpu_custom_call" | custom-call | tf_op jit(solution)/shard_map/finish/pallas_call | solution.py:567
  (3 shorter events, 0.0 us)
Async XLA Ops:
  0.6 11.0 %copy-start.2 = (s32[4,8]{1,0:T(4,128)S(1)}, s32[4,8]{1,0:T(4,128)}, u32[]{:S(2)}) copy-start(s32[4,8]{1,0:T(4,128)} %cols_ref.7) | copy-start | bytes 388
  0.6 11.0 %copy-start.1 = (s32[27,144]{1,0:T(8,128)S(1)}, s32[27,144]{1,0:T(8,128)}, u32[]{:S(2)}) copy-start(s32[27,144]{1,0:T(8,128)} %cwet_ref.5) | copy-start | bytes 46660
  0.7 11.0 %copy-start = (f32[2,50,27,144]{3,0,2,1:T(2,128)S(1)}, f32[2,50,27,144]{3,0,2,1:T(2,128)}, u32[]{:S(2)}) copy-start(f32[2,50,27,144]{3,0,2,1:T(2,128)} %param.8) | copy-start | bytes 4665604
  0.7 11.0 %copy-start.3 = (f32[2,49]{1,0:T(2,128)S(1)}, f32[2,49]{1,0:T(2,128)}, u32[]{:S(2)}) copy-start(f32[2,49]{1,0:T(2,128)} %mix_ref.1) | copy-start | bytes 1180
  2.8 12.9 %collective-permute-start = (f32[256,128]{1,0:T(8,128)S(1)}, f32[256,128]{1,0:T(8,128)S(1)}, u32[]{:S(2)}, u32[]{:S(2)}) collective-permute-start(f32[256,128]{1,0:T(8,128)S(1)} %get-tuple-element.33), channel_id=1, source_target_pairs={{0,1},{1,2},{2,3},{3,4},{4,5},{5,6},{6,7},{7,8},{8,9},{9,10},{10,1... | collective-permute-start | bytes 393224 | tf_op jit(solution)/shard_map/ppermute | solution.py:470
  5.8 9.9 %collective-permute-start.1 = (f32[256,128]{1,0:T(8,128)S(1)}, f32[256,128]{1,0:T(8,128)S(1)}, u32[]{:S(2)}, u32[]{:S(2)}) collective-permute-start(f32[256,128]{1,0:T(8,128)S(1)} %get-tuple-element.34), channel_id=1, source_target_pairs={{0,31},{1,0},{2,1},{3,2},{4,3},{5,4},{6,5},{7,6},{8,7},{9,8},{10,9... | collective-permute-start | bytes 393224 | tf_op jit(solution)/shard_map/ppermute | solution.py:470
  9.3 6.4 %collective-permute-start.2 = (f32[8,128]{1,0:T(8,128)S(1)}, f32[8,128]{1,0:T(8,128)S(1)}, u32[]{:S(2)}, u32[]{:S(2)}) collective-permute-start(f32[8,128]{1,0:T(8,128)S(1)} %get-tuple-element.35), channel_id=1, source_target_pairs={{0,8},{8,16},{16,24},{24,0},{1,9},{9,17},{17,25},{25,1},{2,10},{10... | collective-permute-start | bytes 12296 | tf_op jit(solution)/shard_map/ppermute | solution.py:470
  9.3 6.4 %collective-permute-start.3 = (f32[8,128]{1,0:T(8,128)S(1)}, f32[8,128]{1,0:T(8,128)S(1)}, u32[]{:S(2)}, u32[]{:S(2)}) collective-permute-start(f32[8,128]{1,0:T(8,128)S(1)} %get-tuple-element.36), channel_id=1, source_target_pairs={{0,24},{8,0},{16,8},{24,16},{1,25},{9,1},{17,9},{25,17},{2,26},{10... | collective-permute-start | bytes 12296 | tf_op jit(solution)/shard_map/ppermute | solution.py:470
  17.3 6.0 %collective-permute-start.4 = (f32[144,128]{1,0:T(8,128)S(1)}, f32[144,128]{1,0:T(8,128)S(1)}, u32[]{:S(2)}, u32[]{:S(2)}) collective-permute-start(f32[144,128]{1,0:T(8,128)S(1)} %get-tuple-element.43), channel_id=1, source_target_pairs={{0,1},{1,0},{2,3},{3,2},{4,5},{5,4},{6,7},{7,6},{8,9},{9,8},{10,11... | collective-permute-start | bytes 221192 | tf_op jit(solution)/shard_map/ppermute | solution.py:554
  17.4 8.0 %collective-permute-start.5 = (f32[144,128]{1,0:T(8,128)S(1)}, f32[144,128]{1,0:T(8,128)S(1)}, u32[]{:S(2)}, u32[]{:S(2)}) collective-permute-start(f32[144,128]{1,0:T(8,128)S(1)} %get-tuple-element.44), channel_id=1, source_target_pairs={{0,2},{1,3},{2,0},{3,1},{4,6},{5,7},{6,4},{7,5},{8,10},{9,11},{10,... | collective-permute-start | bytes 221192 | tf_op jit(solution)/shard_map/ppermute | solution.py:554
  17.5 13.4 %collective-permute-start.6 = (f32[144,128]{1,0:T(8,128)S(1)}, f32[144,128]{1,0:T(8,128)S(1)}, u32[]{:S(2)}, u32[]{:S(2)}) collective-permute-start(f32[144,128]{1,0:T(8,128)S(1)} %get-tuple-element.45), channel_id=1, source_target_pairs={{0,3},{1,2},{2,1},{3,0},{4,7},{5,6},{6,5},{7,4},{8,11},{9,10},{10,... | collective-permute-start | bytes 221192 | tf_op jit(solution)/shard_map/ppermute | solution.py:554
  20.9 10.5 %collective-permute-start.7 = (f32[144,128]{1,0:T(8,128)S(1)}, f32[144,128]{1,0:T(8,128)S(1)}, u32[]{:S(2)}, u32[]{:S(2)}) collective-permute-start(f32[144,128]{1,0:T(8,128)S(1)} %get-tuple-element.46), channel_id=1, source_target_pairs={{0,4},{1,5},{2,6},{3,7},{4,0},{5,1},{6,2},{7,3},{8,12},{9,13},{10,... | collective-permute-start | bytes 221192 | tf_op jit(solution)/shard_map/ppermute | solution.py:554
  21.4 12.6 %collective-permute-start.8 = (f32[144,128]{1,0:T(8,128)S(1)}, f32[144,128]{1,0:T(8,128)S(1)}, u32[]{:S(2)}, u32[]{:S(2)}) collective-permute-start(f32[144,128]{1,0:T(8,128)S(1)} %get-tuple-element.47), channel_id=1, source_target_pairs={{0,5},{1,4},{2,7},{3,6},{4,1},{5,0},{6,3},{7,2},{8,13},{9,12},{10,... | collective-permute-start | bytes 221192 | tf_op jit(solution)/shard_map/ppermute | solution.py:554
  23.3 10.7 %collective-permute-start.9 = (f32[144,128]{1,0:T(8,128)S(1)}, f32[144,128]{1,0:T(8,128)S(1)}, u32[]{:S(2)}, u32[]{:S(2)}) collective-permute-start(f32[144,128]{1,0:T(8,128)S(1)} %get-tuple-element.48), channel_id=1, source_target_pairs={{0,6},{1,7},{2,4},{3,5},{4,2},{5,3},{6,0},{7,1},{8,14},{9,15},{10,... | collective-permute-start | bytes 221192 | tf_op jit(solution)/shard_map/ppermute | solution.py:554
  25.4 8.6 %collective-permute-start.10 = (f32[144,128]{1,0:T(8,128)S(1)}, f32[144,128]{1,0:T(8,128)S(1)}, u32[]{:S(2)}, u32[]{:S(2)}) collective-permute-start(f32[144,128]{1,0:T(8,128)S(1)} %get-tuple-element.49), channel_id=1, source_target_pairs={{0,7},{1,6},{2,5},{3,4},{4,3},{5,2},{6,1},{7,0},{8,15},{9,14},{10,... | collective-permute-start | bytes 221192 | tf_op jit(solution)/shard_map/ppermute | solution.py:554

commit v4 on v3

--- a/solution.py
+++ b/solution.py
@@ -24,6 +24,10 @@
 
 def in_hbm(x):
     return pltpu.with_memory_space_constraint(x, pltpu.HBM)
+
+
+def far_first(strips):
+    return list(reversed(range(strips)))
 
 
 def up(n, m):
@@ -89,9 +93,9 @@
 
 
 def prepare_kernel(
-    cols_hbm, parent_hbm, pwet_hbm, child_hbm, cwet_hbm,
-    flat_ref, forth_ref, back_ref, left_ref, right_ref,
-    cols_ref, parent_ref, pwet_ref, cwet_ref, edge_ref, turn_ref, row_ref, sems,
+    cols_hbm, mix_hbm, parent_hbm, pwet_hbm, child_hbm, cwet_hbm,
+    flat_ref, forth_ref, back_ref, left_ref, right_ref, weight_ref, carry_ref, below_ref, inverse_ref,
+    cols_ref, mix_ref, parent_ref, pwet_ref, cwet_ref, edge_ref, turn_ref, row_ref, d_ref, c_ref, sems,
 ):
     levels, capacity, tracers, child_rows = child_hbm.shape
     rows, width = pwet_ref.shape
@@ -103,13 +107,16 @@
     fetch_parent = pltpu.make_async_copy(parent_hbm, parent_ref, sems.at[2])
     fetch_cwet = pltpu.make_async_copy(cwet_hbm, cwet_ref, sems.at[3])
     fetch_first = pltpu.make_async_copy(child_hbm.at[:, pl.ds(0, 1)], edge_ref.at[1], sems.at[4])
-    for fetch in (fetch_cols, fetch_pwet, fetch_parent, fetch_first, fetch_cwet):
+    fetch_mix = pltpu.make_async_copy(mix_hbm, mix_ref, sems.at[6])
+    for fetch in (fetch_cols, fetch_mix, fetch_pwet, fetch_parent, fetch_first, fetch_cwet):
         fetch.start()
     fetch_cols.wait()
     last = 3 * my_cols(cols_ref) - 1
     fetch_last = pltpu.make_async_copy(child_hbm.at[:, pl.ds(last, 1)], edge_ref.at[0], sems.at[5])
     fetch_last.start()
     row_ref[...] = jnp.zeros_like(row_ref)
+    fetch_mix.wait()
+    coefficients(mix_ref, weight_ref, carry_ref, below_ref, inverse_ref, d_ref, c_ref)
     fetch_pwet.wait()
     turn_ref[:rows, :width] = pwet_ref[...].astype(jnp.float32)
     wet = turn_ref[...].T
@@ -149,16 +156,15 @@
 
 
 def inner_kernel(
-    cols_ref, mix_ref, child_ref, cwet_ref,
-    weight_ref, carry_ref, back_ref, inverse_ref, explicit_ref,
-    mask_ref, begin_ref, d_ref, c_ref,
+    cols_ref, child_ref, cwet_ref,
+    explicit_ref, mask_ref,
+    begin_ref,
 ):
     levels, capacity, tracers, child_rows = child_ref.shape
     tiles = tile_list(child_rows)
     live = capacity * tracers
     stored = up(live, 8)
     stride = begin_ref.shape[1] // levels
-    coefficients(mix_ref, weight_ref, carry_ref, back_ref, inverse_ref, d_ref, c_ref)
     masks(cols_ref, cwet_ref, mask_ref, tracers)
     flat_child = child_ref.reshape(levels * live, child_rows)
     lane = lax.broadcasted_iota(jnp.int32, (stored, LANES), 1)
@@ -191,7 +197,7 @@
             )
         return carry
 
-    lax.fori_loop(0, levels, explicit, 0, unroll=10 if levels % 10 == 0 else 1)
+    lax.fori_loop(0, levels, explicit, 0, unroll=25 if levels % 25 == 0 else 1)
 
 
 def pack_kernel(
@@ -353,13 +359,13 @@
 
 def finish_kernel(
     strips, rows, chunks,
-    cols_ref, offset_ref, own_ref, pmid_ref, inverse_ref, cmid_ref, cwet_ref,
+    cols_ref, offset_ref, own_ref, pmid_ref, inverse_ref, cmid_ref, mask_ref,
     *refs,
 ):
-    got_refs = refs[:strips]
+    got_refs = {s: ref for s, ref in zip(far_first(strips), refs)}
     (
         pnext_hbm, cnext_hbm,
-        panel_ref, wide_ref, ends_ref, long_ref, end_ref, add_ref, mask_ref, next_ref, pkeep_ref, ckeep_ref,
+        panel_ref, wide_ref, ends_ref, long_ref, end_ref, add_ref, next_ref, pkeep_ref, ckeep_ref,
         start_ref, sems,
     ) = refs[strips:]
     levels, capacity, tracers, child_rows = cnext_hbm.shape
@@ -377,8 +383,6 @@
     for j, start in enumerate(strip_starts(cols_ref, strips)):
         start_ref[j] = start
     offset = offset_ref[0]
-    masks(cols_ref, cwet_ref, mask_ref, tracers)
-
     ends_ref[...] = jnp.zeros_like(ends_ref)
     for q in range(narrow):
         for s in range(strips):
@@ -488,26 +492,30 @@
     parent = jnp.transpose(parent_tracer, (0, 2, 3, 1))
     child = jnp.transpose(child_tracer, (1, 2, 0, 3))
 
-    flat, forth, back, left_edge, right_edge = pl.pallas_call(
+    flat, forth, back, left_edge, right_edge, weight, carry, below, inverse = pl.pallas_call(
         prepare_kernel,
-        in_specs=[HBM] * 5,
-        out_specs=[VM] * 5,
+        in_specs=[HBM] * 6,
+        out_specs=[VM] * 9,
         out_shape=[
             f32(width * rows, LANES), f32(message, LANES), f32(message, LANES), f32(rows, LANES), f32(rows, LANES),
+            f32(8 * levels, LANES), f32(8 * levels, LANES), f32(8 * levels, LANES), f32(LANES, LANES),
         ],
         scratch_shapes=[
             pltpu.SMEM(strip_cols.shape, jnp.int32),
+            pltpu.SMEM(vert_mix.shape, jnp.float32),
             mem(*parent.shape),
             pltpu.VMEM(parent_wet.shape, jnp.int32),
             pltpu.VMEM(child_wet.shape, jnp.int32),
             mem(2, levels, 1, tracers, child_rows),
             mem(LANES, LANES),
             mem(rows, width, LANES),
-            pltpu.SemaphoreType.DMA((6,)),
+            mem(8 * levels, LANES),
+            mem(8 * levels, LANES),
+            pltpu.SemaphoreType.DMA((7,)),
         ],
         compiler_params=params(16),
         name="prepare",
-    )(*(in_hbm(x) for x in (strip_cols, parent, parent_wet, child, child_wet)))
+    )(*(in_hbm(x) for x in (strip_cols, vert_mix, parent, parent_wet, child, child_wet)))
 
     groups = lax.axis_size("parent")
     devices = groups * strips
@@ -516,20 +524,15 @@
     forth = ring(forth, ("parent", "child"), devices, 1)
     back = ring(back, ("parent", "child"), devices, -1)
 
-    weight, carry, below, inverse, explicit = pl.pallas_call(
+    explicit, mask = pl.pallas_call(
         inner_kernel,
-        in_specs=[SM, SM, VM, VM],
-        out_specs=[VM] * 5,
-        out_shape=[f32(8 * levels, LANES)] * 3 + [f32(LANES, LANES), f32(lane_tiles, levels * stored, LANES)],
-        scratch_shapes=[
-            mem(lane_tiles, stored, LANES),
-            mem(lane_tiles, levels * stride, LANES),
-            mem(8 * levels, LANES),
-            mem(8 * levels, LANES),
-        ],
+        in_specs=[SM, VM, VM],
+        out_specs=[VM] * 2,
+        out_shape=[f32(lane_tiles, levels * stored, LANES), f32(lane_tiles, stored, LANES)],
+        scratch_shapes=[mem(lane_tiles, levels * stride, LANES)],
         compiler_params=params(16),
         name="inner",
-    )(strip_cols, vert_mix, child, child_wet)
+    )(strip_cols, child, child_wet)
 
     block = f32(2 * narrow * rows, LANES)
     *blocks, parent_mid, own, halo = pl.pallas_call(
@@ -550,9 +553,10 @@
         name="pack",
     )(strip_cols, row_offset, flat, forth, back, right_edge, left_edge, inverse, explicit, child_wet)
 
-    got = [blocks[0]] + [
-        lax.ppermute(blocks[s], "child", [(i, i ^ s) for i in range(strips)]) for s in range(1, strips)
-    ]
+    got = {0: blocks[0]}
+    for s in far_first(strips)[:-1]:
+        got[s] = lax.ppermute(blocks[s], "child", [(i, i ^ s) for i in range(strips)])
+    got = [got[s] for s in far_first(strips)]
 
     child_mid, mean = pl.pallas_call(
         functools.partial(level_kernel, tracers, levels, capacity),
@@ -576,7 +580,6 @@
             mem(narrow * child_rows, LANES),
             mem(packed, LANES, LANES),
             mem(lane_tiles, levels * stored, LANES),
-            mem(lane_tiles, stored, LANES),
             mem(width * rows, LANES),
             mem(*parent.shape),
             mem(*child.shape),
@@ -585,7 +588,7 @@
         ],
         compiler_params=params(24),
         name="finish",
-    )(strip_cols, row_offset, mean, parent_mid, inverse, child_mid, child_wet, *got)
+    )(strip_cols, row_offset, mean, parent_mid, inverse, child_mid, mask, *got)
     return jnp.transpose(parent_next, (0, 3, 1, 2)), jnp.transpose(child_next, (2, 0, 1, 3))
 
 

time: 38 us -> 36.5 us (0.961)
  Pallas kernels: 13.8 us -> 13.1 us
  starting transfers between devices: 19.4 us -> 19 us
    pallas_call x2, Pallas kernels: 6.01 us -> 5.35 us  [the longest x1 3.32 us: body(): pl.pallas_call(inner_kernel, in_specs=[SM, VM, VM], out_specs=[VM] * 2, o...]
    ppermute x7, starting transfers between devices: 11.2 us -> 10.8 us  [body(): lax.ppermute(blocks[s], 'child', [(i, i ^ s) for i in range(strips)])]
  transfers between devices with their start and end apart: 11 -> 11, of which waited for: 2 -> 4; matrix products, arithmetic and copies ran while one was open for 0% -> 0% of each run, Pallas kernels for 17% -> 16%
where the time goes in v4:
time: 36.5 us; the launch traced here: 36.4 us
  starting transfers between devices  19 us (52%)
  Pallas kernels  13.1 us (36%)
  waiting for transfers between devices  2.85 us (8%)
  between operations  1.38 us (4%)
    ppermute x7, starting transfers between devices, body(): lax.ppermute(blocks[s], 'child', [(i, i ^ s) for i in range(strips)])  10.8 us
    ppermute x4, starting transfers between devices, ring(): lax.ppermute(block, axes, [(i, (i + step) % count) for i in range(count)])  8.24 us
    pallas_call x1, Pallas kernels, body(): pl.pallas_call(functools.partial(finish_kernel, strips, rows, chunks), in...  3.72 us
    pallas_call x1, Pallas kernels, body(): pl.pallas_call(inner_kernel, in_specs=[SM, VM, VM], out_specs=[VM] * 2, o...  3.32 us
    ppermute x7, waiting for transfers between devices, body(): lax.ppermute(blocks[s], 'child', [(i, i ^ s) for i in range(strips)])  2.84 us
    pallas_call x1, Pallas kernels, body(): pl.pallas_call(functools.partial(level_kernel, tracers, levels, capacity)...  2.41 us
    pallas_call x1, Pallas kernels, body(): pl.pallas_call(prepare_kernel, in_specs=[HBM] * 6, out_specs=[VM] * 9, ou...  2.03 us
    pallas_call x1, Pallas kernels, body(): pl.pallas_call(functools.partial(pack_kernel, groups, strips, rows, trace...  1.63 us
  transfers between devices with their start and end apart: 11, of which 4 were waited for; matrix products, arithmetic and copies ran while one was open for 0% of the time, Pallas kernels for 16%

profile of v4, /device:TPU:0, one launch (start us, length us, event | category | flops | bytes accessed | tf_op | source)
XLA Modules:
  0.0 36.4 jit_solution(995204237255303112)
XLA Ops:
  0.6 0.0 copy-start.2
  0.6 0.0 copy-start.1
  0.7 0.0 copy-start
  0.7 2.0 %prepare.1 = (f32[384,128]{1,0:T(8,128)S(1)}, f32[256,128]{1,0:T(8,128)S(1)}, f32[256,128]{1,0:T(8,128)S(1)}, f32[8,128]{1,0:T(8,128)S(1)}, f32[8,128]{1,0:T(8,1...) custom-call(s32[4,8]{1,0:T(4,128)} %cols_ref.7, ...), custom_call_target="tpu_custom_call" | custom-call | tf_op jit(solution)/shard_map/prepare/pallas_call | solution.py:495
  2.7 3.0 %collective-permute-start = (f32[256,128]{1,0:T(8,128)S(1)}, f32[256,128]{1,0:T(8,128)S(1)}, u32[]{:S(2)}, u32[]{:S(2)}) collective-permute-start(f32[256,128]{1,0:T(8,128)S(1)} %get-tuple-element.34), channel_id=1, source_target_pairs={{0,1},{1,2},{2,3},{3,4},{4,5},{5,6},{6,7},{7,8},{8,9},{9,10},{10,1... | collective-permute-start | bytes 393224 | tf_op jit(solution)/shard_map/ppermute | solution.py:474
  5.7 3.5 %collective-permute-start.1 = (f32[256,128]{1,0:T(8,128)S(1)}, f32[256,128]{1,0:T(8,128)S(1)}, u32[]{:S(2)}, u32[]{:S(2)}) collective-permute-start(f32[256,128]{1,0:T(8,128)S(1)} %get-tuple-element.35), channel_id=1, source_target_pairs={{0,31},{1,0},{2,1},{3,2},{4,3},{5,4},{6,5},{7,6},{8,7},{9,8},{10,9... | collective-permute-start | bytes 393224 | tf_op jit(solution)/shard_map/ppermute | solution.py:474
  9.2 0.0 collective-permute-start.2
  9.2 1.7 %collective-permute-start.3 = (f32[8,128]{1,0:T(8,128)S(1)}, f32[8,128]{1,0:T(8,128)S(1)}, u32[]{:S(2)}, u32[]{:S(2)}) collective-permute-start(f32[8,128]{1,0:T(8,128)S(1)} %get-tuple-element.37), channel_id=1, source_target_pairs={{0,24},{8,0},{16,8},{24,16},{1,25},{9,1},{17,9},{25,17},{2,26},{10... | collective-permute-start | bytes 12296 | tf_op jit(solution)/shard_map/ppermute | solution.py:474
  10.9 0.0 copy-done.2
  10.9 0.0 copy-done.1
  11.0 3.3 %inner.1 = (f32[2,2800,128]{2,1,0:T(8,128)S(1)}, f32[2,56,128]{2,1,0:T(8,128)S(1)}) custom-call(s32[4,8]{1,0:T(4,128)S(1)} %copy-done.2, f32[50,27,2,144]{3,2,1,0:T(2,128)S(1)} %bitcast.5, s32[27,144]{1,0:T(8,128)S(1)} %copy-done.1), custom_call_target="tpu_custom_call" | custom-call | tf_op jit(solution)/shard_map/inner/pallas_call | solution.py:527
  14.9 0.0 collective-permute-done.2.left_ref
  14.9 0.0 collective-permute-done.3.right_ref
  14.9 0.0 collective-permute-done.before_ref
  15.0 0.0 collective-permute-done.1.after_ref
  15.0 1.6 %pack.1 = (f32[144,128]{1,0:T(8,128)S(1)}, f32[144,128]{1,0:T(8,128)S(1)}, f32[144,128]{1,0:T(8,128)S(1)}, f32[144,128]{1,0:T(8,128)S(1)}, f32[144,128]{1,0:T(8,...) custom-call(s32[4,8]{1,0:T(4,128)S(1)} %copy-done.2, ...), custom_call_target="tpu_custom_call" | custom-call | tf_op jit(solution)/shard_map/pack/pallas_call | solution.py:538
  16.6 1.7 %collective-permute-start.4 = (f32[144,128]{1,0:T(8,128)S(1)}, f32[144,128]{1,0:T(8,128)S(1)}, u32[]{:S(2)}, u32[]{:S(2)}) collective-permute-start(f32[144,128]{1,0:T(8,128)S(1)} %get-tuple-element.44), channel_id=1, source_target_pairs={{0,7},{1,6},{2,5},{3,4},{4,3},{5,2},{6,1},{7,0},{8,15},{9,14},{10,... | collective-permute-start | bytes 221192 | tf_op jit(solution)/shard_map/ppermute | solution.py:558
  18.3 0.5 %collective-permute-start.5 = (f32[144,128]{1,0:T(8,128)S(1)}, f32[144,128]{1,0:T(8,128)S(1)}, u32[]{:S(2)}, u32[]{:S(2)}) collective-permute-start(f32[144,128]{1,0:T(8,128)S(1)} %get-tuple-element.45), channel_id=1, source_target_pairs={{0,6},{1,7},{2,4},{3,5},{4,2},{5,3},{6,0},{7,1},{8,14},{9,15},{10,... | collective-permute-start | bytes 221192 | tf_op jit(solution)/shard_map/ppermute | solution.py:558
  18.7 1.6 %collective-permute-start.6 = (f32[144,128]{1,0:T(8,128)S(1)}, f32[144,128]{1,0:T(8,128)S(1)}, u32[]{:S(2)}, u32[]{:S(2)}) collective-permute-start(f32[144,128]{1,0:T(8,128)S(1)} %get-tuple-element.46), channel_id=1, source_target_pairs={{0,5},{1,4},{2,7},{3,6},{4,1},{5,0},{6,3},{7,2},{8,13},{9,12},{10,... | collective-permute-start | bytes 221192 | tf_op jit(solution)/shard_map/ppermute | solution.py:558
  20.4 4.0 %collective-permute-start.7 = (f32[144,128]{1,0:T(8,128)S(1)}, f32[144,128]{1,0:T(8,128)S(1)}, u32[]{:S(2)}, u32[]{:S(2)}) collective-permute-start(f32[144,128]{1,0:T(8,128)S(1)} %get-tuple-element.47), channel_id=1, source_target_pairs={{0,4},{1,5},{2,6},{3,7},{4,0},{5,1},{6,2},{7,3},{8,12},{9,13},{10,... | collective-permute-start | bytes 221192 | tf_op jit(solution)/shard_map/ppermute | solution.py:558
  24.3 0.0 collective-permute-start.8
  24.3 0.0 collective-permute-done.4.refs_0_
  24.3 0.3 collective-permute-start.9
  24.6 0.4 %collective-permute-done.5.refs_1_ = f32[144,128]{1,0:T(8,128)S(1)} collective-permute-done((f32[144,128]{1,0:T(8,128)S(1)}, f32[144,128]{1,0:T(8,128)S(1)}, u32[]{:S(2)}, u32[]{:S(2)}) %collective-permute-start.5) | collective-permute-done | bytes 73760 | tf_op jit(solution)/shard_map/ppermute | solution.py:558
  25.0 2.8 %collective-permute-start.10 = (f32[144,128]{1,0:T(8,128)S(1)}, f32[144,128]{1,0:T(8,128)S(1)}, u32[]{:S(2)}, u32[]{:S(2)}) collective-permute-start(f32[144,128]{1,0:T(8,128)S(1)} %get-tuple-element.50), channel_id=1, source_target_pairs={{0,1},{1,0},{2,3},{3,2},{4,5},{5,4},{6,7},{7,6},{8,9},{9,8},{10,11... | collective-permute-start | bytes 221192 | tf_op jit(solution)/shard_map/ppermute | solution.py:558
  27.8 2.4 %levels.1 = (f32[2,2800,128]{2,1,0:T(8,128)S(1)}, f32[576,128]{1,0:T(8,128)S(1)}) custom-call(s32[4,8]{1,0:T(4,128)S(1)} %copy-done.2, f32[400,128]{1,0:T(8,128)S(1)} %get-tuple-element.28.weight_ref, f32[400,128]{1,0:T(8,128)S(1)} %get-tuple-element.29.carry_ref, f32[400,128]{1,0:T(8,128)S(1)} %get-tuple-element.30.back_ref, ...), custom_call_target="tpu_custom_call" | custom-call | tf_op jit(solution)/shard_map/levels/pallas_call | solution.py:561
  30.2 0.8 %collective-permute-done.6.refs_2_ = f32[144,128]{1,0:T(8,128)S(1)} collective-permute-done((f32[144,128]{1,0:T(8,128)S(1)}, f32[144,128]{1,0:T(8,128)S(1)}, u32[]{:S(2)}, u32[]{:S(2)}) %collective-permute-start.6) | collective-permute-done | bytes 73760 | tf_op jit(solution)/shard_map/ppermute | solution.py:558
  31.1 0.5 %collective-permute-done.7.refs_3_ = f32[144,128]{1,0:T(8,128)S(1)} collective-permute-done((f32[144,128]{1,0:T(8,128)S(1)}, f32[144,128]{1,0:T(8,128)S(1)}, u32[]{:S(2)}, u32[]{:S(2)}) %collective-permute-start.7) | collective-permute-done | bytes 73760 | tf_op jit(solution)/shard_map/ppermute | solution.py:558
  31.6 1.1 %collective-permute-done.8.refs_4_ = f32[144,128]{1,0:T(8,128)S(1)} collective-permute-done((f32[144,128]{1,0:T(8,128)S(1)}, f32[144,128]{1,0:T(8,128)S(1)}, u32[]{:S(2)}, u32[]{:S(2)}) %collective-permute-start.8) | collective-permute-done | bytes 73760 | tf_op jit(solution)/shard_map/ppermute | solution.py:558
  32.7 0.0 collective-permute-done.9.refs_5_
  32.7 0.0 collective-permute-done.10.refs_6_
  32.7 3.7 %finish.1 = (f32[2,8,48,50]{3,2,1,0:T(8,128)}, f32[50,27,2,144]{3,2,1,0:T(2,128)}) custom-call(s32[4,8]{1,0:T(4,128)S(1)} %copy-done.2, s32[1]{0:T(128)S(6)} %copy.9.offset_ref, f32[576,128]{1,0:T(8,128)S(1)} %get-tuple-element.40.own_ref, f32[384,128]{1,0:T(8,128)S(1)} %get-tuple-element.41.pmid_ref, f32[128,128]{1,0:T(8,128)S(1)} %get-tuple-element.31.inverse_ref, ...), custom_call_target="tpu_custom_call" | custom-call | tf_op jit(solution)/shard_map/finish/pallas_call | solution.py:571
  (1 shorter events, 0.0 us)
Async XLA Ops:
  0.6 10.3 %copy-start.2 = (s32[4,8]{1,0:T(4,128)S(1)}, s32[4,8]{1,0:T(4,128)}, u32[]{:S(2)}) copy-start(s32[4,8]{1,0:T(4,128)} %cols_ref.7) | copy-start | bytes 388
  0.6 10.3 %copy-start.1 = (s32[27,144]{1,0:T(8,128)S(1)}, s32[27,144]{1,0:T(8,128)}, u32[]{:S(2)}) copy-start(s32[27,144]{1,0:T(8,128)} %cwet_ref.3) | copy-start | bytes 46660
  0.7 10.3 %copy-start = (f32[2,50,27,144]{3,0,2,1:T(2,128)S(1)}, f32[2,50,27,144]{3,0,2,1:T(2,128)}, u32[]{:S(2)}) copy-start(f32[2,50,27,144]{3,0,2,1:T(2,128)} %param.8) | copy-start | bytes 4665604
  2.7 12.2 %collective-permute-start = (f32[256,128]{1,0:T(8,128)S(1)}, f32[256,128]{1,0:T(8,128)S(1)}, u32[]{:S(2)}, u32[]{:S(2)}) collective-permute-start(f32[256,128]{1,0:T(8,128)S(1)} %get-tuple-element.34), channel_id=1, source_target_pairs={{0,1},{1,2},{2,3},{3,4},{4,5},{5,6},{6,7},{7,8},{8,9},{9,10},{10,1... | collective-permute-start | bytes 393224 | tf_op jit(solution)/shard_map/ppermute | solution.py:474
  5.7 9.2 %collective-permute-start.1 = (f32[256,128]{1,0:T(8,128)S(1)}, f32[256,128]{1,0:T(8,128)S(1)}, u32[]{:S(2)}, u32[]{:S(2)}) collective-permute-start(f32[256,128]{1,0:T(8,128)S(1)} %get-tuple-element.35), channel_id=1, source_target_pairs={{0,31},{1,0},{2,1},{3,2},{4,3},{5,4},{6,5},{7,6},{8,7},{9,8},{10,9... | collective-permute-start | bytes 393224 | tf_op jit(solution)/shard_map/ppermute | solution.py:474
  9.2 5.7 %collective-permute-start.2 = (f32[8,128]{1,0:T(8,128)S(1)}, f32[8,128]{1,0:T(8,128)S(1)}, u32[]{:S(2)}, u32[]{:S(2)}) collective-permute-start(f32[8,128]{1,0:T(8,128)S(1)} %get-tuple-element.36), channel_id=1, source_target_pairs={{0,8},{8,16},{16,24},{24,0},{1,9},{9,17},{17,25},{25,1},{2,10},{10... | collective-permute-start | bytes 12296 | tf_op jit(solution)/shard_map/ppermute | solution.py:474
  9.2 5.7 %collective-permute-start.3 = (f32[8,128]{1,0:T(8,128)S(1)}, f32[8,128]{1,0:T(8,128)S(1)}, u32[]{:S(2)}, u32[]{:S(2)}) collective-permute-start(f32[8,128]{1,0:T(8,128)S(1)} %get-tuple-element.37), channel_id=1, source_target_pairs={{0,24},{8,0},{16,8},{24,16},{1,25},{9,1},{17,9},{25,17},{2,26},{10... | collective-permute-start | bytes 12296 | tf_op jit(solution)/shard_map/ppermute | solution.py:474
  16.6 7.7 %collective-permute-start.4 = (f32[144,128]{1,0:T(8,128)S(1)}, f32[144,128]{1,0:T(8,128)S(1)}, u32[]{:S(2)}, u32[]{:S(2)}) collective-permute-start(f32[144,128]{1,0:T(8,128)S(1)} %get-tuple-element.44), channel_id=1, source_target_pairs={{0,7},{1,6},{2,5},{3,4},{4,3},{5,2},{6,1},{7,0},{8,15},{9,14},{10,... | collective-permute-start | bytes 221192 | tf_op jit(solution)/shard_map/ppermute | solution.py:558
  18.3 6.7 %collective-permute-start.5 = (f32[144,128]{1,0:T(8,128)S(1)}, f32[144,128]{1,0:T(8,128)S(1)}, u32[]{:S(2)}, u32[]{:S(2)}) collective-permute-start(f32[144,128]{1,0:T(8,128)S(1)} %get-tuple-element.45), channel_id=1, source_target_pairs={{0,6},{1,7},{2,4},{3,5},{4,2},{5,3},{6,0},{7,1},{8,14},{9,15},{10,... | collective-permute-start | bytes 221192 | tf_op jit(solution)/shard_map/ppermute | solution.py:558
  18.7 12.3 %collective-permute-start.6 = (f32[144,128]{1,0:T(8,128)S(1)}, f32[144,128]{1,0:T(8,128)S(1)}, u32[]{:S(2)}, u32[]{:S(2)}) collective-permute-start(f32[144,128]{1,0:T(8,128)S(1)} %get-tuple-element.46), channel_id=1, source_target_pairs={{0,5},{1,4},{2,7},{3,6},{4,1},{5,0},{6,3},{7,2},{8,13},{9,12},{10,... | collective-permute-start | bytes 221192 | tf_op jit(solution)/shard_map/ppermute | solution.py:558
  20.4 11.2 %collective-permute-start.7 = (f32[144,128]{1,0:T(8,128)S(1)}, f32[144,128]{1,0:T(8,128)S(1)}, u32[]{:S(2)}, u32[]{:S(2)}) collective-permute-start(f32[144,128]{1,0:T(8,128)S(1)} %get-tuple-element.47), channel_id=1, source_target_pairs={{0,4},{1,5},{2,6},{3,7},{4,0},{5,1},{6,2},{7,3},{8,12},{9,13},{10,... | collective-permute-start | bytes 221192 | tf_op jit(solution)/shard_map/ppermute | solution.py:558
  24.3 8.3 %collective-permute-start.8 = (f32[144,128]{1,0:T(8,128)S(1)}, f32[144,128]{1,0:T(8,128)S(1)}, u32[]{:S(2)}, u32[]{:S(2)}) collective-permute-start(f32[144,128]{1,0:T(8,128)S(1)} %get-tuple-element.48), channel_id=1, source_target_pairs={{0,3},{1,2},{2,1},{3,0},{4,7},{5,6},{6,5},{7,4},{8,11},{9,10},{10,... | collective-permute-start | bytes 221192 | tf_op jit(solution)/shard_map/ppermute | solution.py:558
  24.3 8.3 %collective-permute-start.9 = (f32[144,128]{1,0:T(8,128)S(1)}, f32[144,128]{1,0:T(8,128)S(1)}, u32[]{:S(2)}, u32[]{:S(2)}) collective-permute-start(f32[144,128]{1,0:T(8,128)S(1)} %get-tuple-element.49), channel_id=1, source_target_pairs={{0,2},{1,3},{2,0},{3,1},{4,6},{5,7},{6,4},{7,5},{8,10},{9,11},{10,... | collective-permute-start | bytes 221192 | tf_op jit(solution)/shard_map/ppermute | solution.py:558
  25.0 7.7 %collective-permute-start.10 = (f32[144,128]{1,0:T(8,128)S(1)}, f32[144,128]{1,0:T(8,128)S(1)}, u32[]{:S(2)}, u32[]{:S(2)}) collective-permute-start(f32[144,128]{1,0:T(8,128)S(1)} %get-tuple-element.50), channel_id=1, source_target_pairs={{0,1},{1,0},{2,3},{3,2},{4,5},{5,4},{6,7},{7,6},{8,9},{9,8},{10,11... | collective-permute-start | bytes 221192 | tf_op jit(solution)/shard_map/ppermute | solution.py:558

commit v5 on v4

--- a/solution.py
+++ b/solution.py
@@ -94,7 +94,7 @@
 
 def prepare_kernel(
     cols_hbm, mix_hbm, parent_hbm, pwet_hbm, child_hbm, cwet_hbm,
-    flat_ref, forth_ref, back_ref, left_ref, right_ref, weight_ref, carry_ref, below_ref, inverse_ref,
+    flat_ref, forth_ref, back_ref, left_ref, right_ref, weight_ref, carry_ref, below_ref, inverse_ref, again_ref,
     cols_ref, mix_ref, parent_ref, pwet_ref, cwet_ref, edge_ref, turn_ref, row_ref, d_ref, c_ref, sems,
 ):
     levels, capacity, tracers, child_rows = child_hbm.shape
@@ -108,7 +108,8 @@
     fetch_cwet = pltpu.make_async_copy(cwet_hbm, cwet_ref, sems.at[3])
     fetch_first = pltpu.make_async_copy(child_hbm.at[:, pl.ds(0, 1)], edge_ref.at[1], sems.at[4])
     fetch_mix = pltpu.make_async_copy(mix_hbm, mix_ref, sems.at[6])
-    for fetch in (fetch_cols, fetch_mix, fetch_pwet, fetch_parent, fetch_first, fetch_cwet):
+    fetch_again = pltpu.make_async_copy(cols_hbm, again_ref, sems.at[7])
+    for fetch in (fetch_cols, fetch_mix, fetch_again, fetch_pwet, fetch_parent, fetch_first, fetch_cwet):
         fetch.start()
     fetch_cols.wait()
     last = 3 * my_cols(cols_ref) - 1
@@ -130,6 +131,7 @@
     left_ref[...] = flat_ref[:rows, :]
     right_ref[...] = flat_ref[(width - 1) * rows :, :]
     fetch_cwet.wait()
+    fetch_again.wait()
     base = len(tiles) * level_rows
     fetch_first.wait()
     fetch_last.wait()
@@ -192,7 +194,7 @@
                 north = jnp.where(lane == size - 1, 0.0, upper[n])
             west = begin_ref[n, pl.ds(start + 8 - tracers, stored), :]
             east = begin_ref[n, pl.ds(start + 8 + tracers, stored), :]
-            explicit_ref[n, pl.ds(pl.multiple_of(l * stored, 8), stored), :] = (diffusion * mask_ref[n]) * (
+            explicit_ref[n, pl.ds(pl.multiple_of(l * stored, 8), stored), :] = (diffusion * mask_ref[n, :stored, :]) * (
                 here[n] + west + east + south + north
             )
         return carry
@@ -309,7 +311,7 @@
     d_ref, h_ref,
 ):
     count = explicit_ref.shape[0]
-    stored = explicit_ref.shape[1] // levels
+    stored = up(capacity * tracers, 8)
     past = 3 * tracers * my_cols(cols_ref) - tracers
 
     def by_rows(factor, value):
@@ -425,7 +427,7 @@
             shift = (q % packs) * tail_size
             spread(pltpu.roll(turned, (LANES - shift) % LANES, 1) if shift else turned, tail, q)
 
-    flat_next = ckeep_ref.reshape(levels * live, child_rows)
+    flat_next = ckeep_ref.reshape((levels + 1) * live, child_rows)
 
     def write(l, carry):
         at = pl.ds(pl.multiple_of(l * stored, 8), live)
@@ -485,6 +487,7 @@
     packed = -(-narrow // (LANES // tiles[-1][1]))
     stored = up(capacity * tracers, 8)
     stride = stored + 16
+    plane = up(levels, 8) * stored
     chunks = 5
     message = lane_tiles * up(tracers * levels, 8) + width
     f32 = lambda *s: jax.ShapeDtypeStruct(s, jnp.float32)
@@ -492,13 +495,14 @@
     parent = jnp.transpose(parent_tracer, (0, 2, 3, 1))
     child = jnp.transpose(child_tracer, (1, 2, 0, 3))
 
-    flat, forth, back, left_edge, right_edge, weight, carry, below, inverse = pl.pallas_call(
+    flat, forth, back, left_edge, right_edge, weight, carry, below, inverse, cols = pl.pallas_call(
         prepare_kernel,
         in_specs=[HBM] * 6,
-        out_specs=[VM] * 9,
+        out_specs=[VM] * 10,
         out_shape=[
             f32(width * rows, LANES), f32(message, LANES), f32(message, LANES), f32(rows, LANES), f32(rows, LANES),
             f32(8 * levels, LANES), f32(8 * levels, LANES), f32(8 * levels, LANES), f32(LANES, LANES),
+            jax.ShapeDtypeStruct(strip_cols.shape, jnp.int32),
         ],
         scratch_shapes=[
             pltpu.SMEM(strip_cols.shape, jnp.int32),
@@ -511,7 +515,7 @@
             mem(rows, width, LANES),
             mem(8 * levels, LANES),
             mem(8 * levels, LANES),
-            pltpu.SemaphoreType.DMA((7,)),
+            pltpu.SemaphoreType.DMA((8,)),
         ],
         compiler_params=params(16),
         name="prepare",
@@ -528,11 +532,11 @@
         inner_kernel,
         in_specs=[SM, VM, VM],
         out_specs=[VM] * 2,
-        out_shape=[f32(lane_tiles, levels * stored, LANES), f32(lane_tiles, stored, LANES)],
+        out_shape=[f32(lane_tiles, plane, LANES), f32(lane_tiles, stored + 8, LANES)],
         scratch_shapes=[mem(lane_tiles, levels * stride, LANES)],
         compiler_params=params(16),
         name="inner",
-    )(strip_cols, child, child_wet)
+    )(cols, child, child_wet)
 
     block = f32(2 * narrow * rows, LANES)
     *blocks, parent_mid, own, halo = pl.pallas_call(
@@ -540,7 +544,7 @@
         in_specs=[SM, SM] + [VM] * 8,
         out_specs=[VM] * (strips + 3),
         out_shape=[block] * strips
-        + [f32(width * rows, LANES), f32(narrow * all_rows, LANES), f32(lane_tiles, 8 * levels, LANES)],
+        + [f32(width * rows, LANES), f32(narrow * all_rows, LANES), f32(lane_tiles, 8 * up(levels, 8), LANES)],
         scratch_shapes=[
             mem(width * rows, LANES),
             mem((width + narrow) * rows, LANES),
@@ -551,7 +555,7 @@
         ],
         compiler_params=params(16),
         name="pack",
-    )(strip_cols, row_offset, flat, forth, back, right_edge, left_edge, inverse, explicit, child_wet)
+    )(cols, row_offset, flat, forth, back, right_edge, left_edge, inverse, explicit, child_wet)
 
     got = {0: blocks[0]}
     for s in far_first(strips)[:-1]:
@@ -562,11 +566,11 @@
         functools.partial(level_kernel, tracers, levels, capacity),
         in_specs=[SM] + [VM] * 7,
         out_specs=[VM, VM],
-        out_shape=[f32(lane_tiles, levels * stored, LANES), f32(narrow * all_rows, LANES)],
+        out_shape=[f32(lane_tiles, plane, LANES), f32(narrow * all_rows, LANES)],
         scratch_shapes=[mem(lane_tiles, levels * stored, LANES), mem(lane_tiles, 8 * levels, LANES)],
         compiler_params=params(16),
         name="levels",
-    )(strip_cols, weight, carry, below, inverse, explicit, halo, own)
+    )(cols, weight, carry, below, inverse, explicit, halo, own)
 
     parent_next, child_next = pl.pallas_call(
         functools.partial(finish_kernel, strips, rows, chunks),
@@ -579,16 +583,16 @@
             mem(2 * up(narrow, 8), LANES),
             mem(narrow * child_rows, LANES),
             mem(packed, LANES, LANES),
-            mem(lane_tiles, levels * stored, LANES),
+            mem(lane_tiles, plane, LANES),
             mem(width * rows, LANES),
             mem(*parent.shape),
-            mem(*child.shape),
+            mem(levels + 1, *child.shape[1:]),
             pltpu.SMEM((strips,), jnp.int32),
             pltpu.SemaphoreType.DMA((1 + chunks,)),
         ],
         compiler_params=params(24),
         name="finish",
-    )(strip_cols, row_offset, mean, parent_mid, inverse, child_mid, mask, *got)
+    )(cols, row_offset, mean, parent_mid, inverse, child_mid, mask, *got)
     return jnp.transpose(parent_next, (0, 3, 1, 2)), jnp.transpose(child_next, (2, 0, 1, 3))
 
 

time: 36.5 us -> 36.6 us (level)
  no operation moved by 1% of the time
where the time goes in v5:
time: 36.6 us; the launch traced here: 36.4 us
  starting transfers between devices  19 us (52%)
  Pallas kernels  13.1 us (36%)
  waiting for transfers between devices  2.89 us (8%)
  between operations  1.39 us (4%)
    ppermute x7, starting transfers between devices, body(): lax.ppermute(blocks[s], 'child', [(i, i ^ s) for i in range(strips)])  10.7 us
    ppermute x4, starting transfers between devices, ring(): lax.ppermute(block, axes, [(i, (i + step) % count) for i in range(count)])  8.24 us
    pallas_call x1, Pallas kernels, body(): pl.pallas_call(functools.partial(finish_kernel, strips, rows, chunks), in...  3.75 us
    pallas_call x1, Pallas kernels, body(): pl.pallas_call(inner_kernel, in_specs=[SM, VM, VM], out_specs=[VM] * 2, o...  3.32 us
    ppermute x7, waiting for transfers between devices, body(): lax.ppermute(blocks[s], 'child', [(i, i ^ s) for i in range(strips)])  2.88 us
    pallas_call x1, Pallas kernels, body(): pl.pallas_call(functools.partial(level_kernel, tracers, levels, capacity)...  2.41 us
    pallas_call x1, Pallas kernels, body(): pl.pallas_call(prepare_kernel, in_specs=[HBM] * 6, out_specs=[VM] * 10, o...  2.04 us
    pallas_call x1, Pallas kernels, body(): pl.pallas_call(functools.partial(pack_kernel, groups, strips, rows, trace...  1.62 us
  transfers between devices with their start and end apart: 11, of which 4 were waited for; matrix products, arithmetic and copies ran while one was open for 0% of the time, Pallas kernels for 16%

profile of v5, /device:TPU:0, one launch (start us, length us, event | category | flops | bytes accessed | tf_op | source)
XLA Modules:
  0.0 36.4 jit_solution(3569159386227748936)
XLA Ops:
  0.6 0.0 copy-start.1
  0.6 0.0 copy-start
  0.7 2.0 %prepare.1 = (f32[384,128]{1,0:T(8,128)S(1)}, f32[256,128]{1,0:T(8,128)S(1)}, f32[256,128]{1,0:T(8,128)S(1)}, f32[8,128]{1,0:T(8,128)S(1)}, f32[8,128]{1,0:T(8,1...) custom-call(s32[4,8]{1,0:T(4,128)} %cols_hbm.1, ...), custom_call_target="tpu_custom_call" | custom-call | tf_op jit(solution)/shard_map/prepare/pallas_call | solution.py:498
  2.7 3.0 %collective-permute-start = (f32[256,128]{1,0:T(8,128)S(1)}, f32[256,128]{1,0:T(8,128)S(1)}, u32[]{:S(2)}, u32[]{:S(2)}) collective-permute-start(f32[256,128]{1,0:T(8,128)S(1)} %get-tuple-element.36), channel_id=1, source_target_pairs={{0,1},{1,2},{2,3},{3,4},{4,5},{5,6},{6,7},{7,8},{8,9},{9,10},{10,1... | collective-permute-start | bytes 393224 | tf_op jit(solution)/shard_map/ppermute | solution.py:476
  5.7 3.5 %collective-permute-start.1 = (f32[256,128]{1,0:T(8,128)S(1)}, f32[256,128]{1,0:T(8,128)S(1)}, u32[]{:S(2)}, u32[]{:S(2)}) collective-permute-start(f32[256,128]{1,0:T(8,128)S(1)} %get-tuple-element.37), channel_id=1, source_target_pairs={{0,31},{1,0},{2,1},{3,2},{4,3},{5,4},{6,5},{7,6},{8,7},{9,8},{10,9... | collective-permute-start | bytes 393224 | tf_op jit(solution)/shard_map/ppermute | solution.py:476
  9.2 0.0 collective-permute-start.2
  9.2 1.7 %collective-permute-start.3 = (f32[8,128]{1,0:T(8,128)S(1)}, f32[8,128]{1,0:T(8,128)S(1)}, u32[]{:S(2)}, u32[]{:S(2)}) collective-permute-start(f32[8,128]{1,0:T(8,128)S(1)} %get-tuple-element.39), channel_id=1, source_target_pairs={{0,24},{8,0},{16,8},{24,16},{1,25},{9,1},{17,9},{25,17},{2,26},{10... | collective-permute-start | bytes 12296 | tf_op jit(solution)/shard_map/ppermute | solution.py:476
  11.6 0.0 copy-done.1
  11.6 0.0 copy-done
  11.6 3.3 %inner.1 = (f32[2,3136,128]{2,1,0:T(8,128)S(1)}, f32[2,64,128]{2,1,0:T(8,128)S(1)}) custom-call(s32[4,8]{1,0:T(4,128)S(1)} %get-tuple-element.29.cols_ref, f32[50,27,2,144]{3,2,1,0:T(2,128)S(1)} %bitcast.5, s32[27,144]{1,0:T(8,128)S(1)} %copy-done.1), custom_call_target="tpu_custom_call" | custom-call | tf_op jit(solution)/shard_map/inner/pallas_call | solution.py:531
  14.9 0.0 collective-permute-done.2.left_ref
  15.0 0.0 collective-permute-done.3.right_ref
  15.0 0.0 collective-permute-done.before_ref
  15.0 0.0 collective-permute-done.1.after_ref
  15.0 1.6 %pack.1 = (f32[144,128]{1,0:T(8,128)S(1)}, f32[144,128]{1,0:T(8,128)S(1)}, f32[144,128]{1,0:T(8,128)S(1)}, f32[144,128]{1,0:T(8,128)S(1)}, f32[144,128]{1,0:T(8,...) custom-call(s32[4,8]{1,0:T(4,128)S(1)} %get-tuple-element.29.cols_re, ...), custom_call_target="tpu_custom_call" | custom-call | tf_op jit(solution)/shard_map/pack/pallas_call | solution.py:542
  16.6 1.7 %collective-permute-start.4 = (f32[144,128]{1,0:T(8,128)S(1)}, f32[144,128]{1,0:T(8,128)S(1)}, u32[]{:S(2)}, u32[]{:S(2)}) collective-permute-start(f32[144,128]{1,0:T(8,128)S(1)} %get-tuple-element.46), channel_id=1, source_target_pairs={{0,7},{1,6},{2,5},{3,4},{4,3},{5,2},{6,1},{7,0},{8,15},{9,14},{10,... | collective-permute-start | bytes 221192 | tf_op jit(solution)/shard_map/ppermute | solution.py:562
  18.3 0.4 %collective-permute-start.5 = (f32[144,128]{1,0:T(8,128)S(1)}, f32[144,128]{1,0:T(8,128)S(1)}, u32[]{:S(2)}, u32[]{:S(2)}) collective-permute-start(f32[144,128]{1,0:T(8,128)S(1)} %get-tuple-element.47), channel_id=1, source_target_pairs={{0,6},{1,7},{2,4},{3,5},{4,2},{5,3},{6,0},{7,1},{8,14},{9,15},{10,... | collective-permute-start | bytes 221192 | tf_op jit(solution)/shard_map/ppermute | solution.py:562
  18.7 1.6 %collective-permute-start.6 = (f32[144,128]{1,0:T(8,128)S(1)}, f32[144,128]{1,0:T(8,128)S(1)}, u32[]{:S(2)}, u32[]{:S(2)}) collective-permute-start(f32[144,128]{1,0:T(8,128)S(1)} %get-tuple-element.48), channel_id=1, source_target_pairs={{0,5},{1,4},{2,7},{3,6},{4,1},{5,0},{6,3},{7,2},{8,13},{9,12},{10,... | collective-permute-start | bytes 221192 | tf_op jit(solution)/shard_map/ppermute | solution.py:562
  20.3 4.0 %collective-permute-start.7 = (f32[144,128]{1,0:T(8,128)S(1)}, f32[144,128]{1,0:T(8,128)S(1)}, u32[]{:S(2)}, u32[]{:S(2)}) collective-permute-start(f32[144,128]{1,0:T(8,128)S(1)} %get-tuple-element.49), channel_id=1, source_target_pairs={{0,4},{1,5},{2,6},{3,7},{4,0},{5,1},{6,2},{7,3},{8,12},{9,13},{10,... | collective-permute-start | bytes 221192 | tf_op jit(solution)/shard_map/ppermute | solution.py:562
  24.3 0.0 collective-permute-start.8
  24.3 0.0 collective-permute-done.4.refs_0_
  24.3 0.2 collective-permute-start.9
  24.6 0.5 %collective-permute-done.5.refs_1_ = f32[144,128]{1,0:T(8,128)S(1)} collective-permute-done((f32[144,128]{1,0:T(8,128)S(1)}, f32[144,128]{1,0:T(8,128)S(1)}, u32[]{:S(2)}, u32[]{:S(2)}) %collective-permute-start.5) | collective-permute-done | bytes 73760 | tf_op jit(solution)/shard_map/ppermute | solution.py:562
  25.0 2.8 %collective-permute-start.10 = (f32[144,128]{1,0:T(8,128)S(1)}, f32[144,128]{1,0:T(8,128)S(1)}, u32[]{:S(2)}, u32[]{:S(2)}) collective-permute-start(f32[144,128]{1,0:T(8,128)S(1)} %get-tuple-element.52), channel_id=1, source_target_pairs={{0,1},{1,0},{2,3},{3,2},{4,5},{5,4},{6,7},{7,6},{8,9},{9,8},{10,11... | collective-permute-start | bytes 221192 | tf_op jit(solution)/shard_map/ppermute | solution.py:562
  27.8 2.4 %levels.1 = (f32[2,3136,128]{2,1,0:T(8,128)S(1)}, f32[576,128]{1,0:T(8,128)S(1)}) custom-call(s32[4,8]{1,0:T(4,128)S(1)} %get-tuple-element.29.cols_ref, f32[400,128]{1,0:T(8,128)S(1)} %get-tuple-element.30.weight_ref, f32[400,128]{1,0:T(8,128)S(1)} %get-tuple-element.31.carry_ref, f32[400,128]{1,0:T(8,128)S(1)} %get-tuple-element.32.back_ref, ...), custom_call_target="tpu_custom_call" | custom-call | tf_op jit(solution)/shard_map/levels/pallas_call | solution.py:565
  30.2 0.8 %collective-permute-done.6.refs_2_ = f32[144,128]{1,0:T(8,128)S(1)} collective-permute-done((f32[144,128]{1,0:T(8,128)S(1)}, f32[144,128]{1,0:T(8,128)S(1)}, u32[]{:S(2)}, u32[]{:S(2)}) %collective-permute-start.6) | collective-permute-done | bytes 73760 | tf_op jit(solution)/shard_map/ppermute | solution.py:562
  31.0 0.6 %collective-permute-done.7.refs_3_ = f32[144,128]{1,0:T(8,128)S(1)} collective-permute-done((f32[144,128]{1,0:T(8,128)S(1)}, f32[144,128]{1,0:T(8,128)S(1)}, u32[]{:S(2)}, u32[]{:S(2)}) %collective-permute-start.7) | collective-permute-done | bytes 73760 | tf_op jit(solution)/shard_map/ppermute | solution.py:562
  31.6 1.0 %collective-permute-done.8.refs_4_ = f32[144,128]{1,0:T(8,128)S(1)} collective-permute-done((f32[144,128]{1,0:T(8,128)S(1)}, f32[144,128]{1,0:T(8,128)S(1)}, u32[]{:S(2)}, u32[]{:S(2)}) %collective-permute-start.8) | collective-permute-done | bytes 73760 | tf_op jit(solution)/shard_map/ppermute | solution.py:562
  32.7 0.0 collective-permute-done.9.refs_5_
  32.7 0.0 collective-permute-done.10.refs_6_
  32.7 3.7 %finish.1 = (f32[2,8,48,50]{3,2,1,0:T(8,128)}, f32[50,27,2,144]{3,2,1,0:T(2,128)}) custom-call(s32[4,8]{1,0:T(4,128)S(1)} %get-tuple-element.29.cols_ref, s32[1]{0:T(128)S(6)} %copy.9.offset_ref, f32[576,128]{1,0:T(8,128)S(1)} %get-tuple-element.42.own_ref, f32[384,128]{1,0:T(8,128)S(1)} %get-tuple-element.43.pmid_ref, ...), custom_call_target="tpu_custom_call" | custom-call | tf_op jit(solution)/shard_map/finish/pallas_call | solution.py:575
Async XLA Ops:
  0.6 11.0 %copy-start.1 = (s32[27,144]{1,0:T(8,128)S(1)}, s32[27,144]{1,0:T(8,128)}, u32[]{:S(2)}) copy-start(s32[27,144]{1,0:T(8,128)} %cwet_ref.3) | copy-start | bytes 46660
  0.6 11.0 %copy-start = (f32[2,50,27,144]{3,0,2,1:T(2,128)S(1)}, f32[2,50,27,144]{3,0,2,1:T(2,128)}, u32[]{:S(2)}) copy-start(f32[2,50,27,144]{3,0,2,1:T(2,128)} %param.8) | copy-start | bytes 4665604
  2.7 12.3 %collective-permute-start = (f32[256,128]{1,0:T(8,128)S(1)}, f32[256,128]{1,0:T(8,128)S(1)}, u32[]{:S(2)}, u32[]{:S(2)}) collective-permute-start(f32[256,128]{1,0:T(8,128)S(1)} %get-tuple-element.36), channel_id=1, source_target_pairs={{0,1},{1,2},{2,3},{3,4},{4,5},{5,6},{6,7},{7,8},{8,9},{9,10},{10,1... | collective-permute-start | bytes 393224 | tf_op jit(solution)/shard_map/ppermute | solution.py:476
  5.7 9.3 %collective-permute-start.1 = (f32[256,128]{1,0:T(8,128)S(1)}, f32[256,128]{1,0:T(8,128)S(1)}, u32[]{:S(2)}, u32[]{:S(2)}) collective-permute-start(f32[256,128]{1,0:T(8,128)S(1)} %get-tuple-element.37), channel_id=1, source_target_pairs={{0,31},{1,0},{2,1},{3,2},{4,3},{5,4},{6,5},{7,6},{8,7},{9,8},{10,9... | collective-permute-start | bytes 393224 | tf_op jit(solution)/shard_map/ppermute | solution.py:476
  9.2 5.8 %collective-permute-start.2 = (f32[8,128]{1,0:T(8,128)S(1)}, f32[8,128]{1,0:T(8,128)S(1)}, u32[]{:S(2)}, u32[]{:S(2)}) collective-permute-start(f32[8,128]{1,0:T(8,128)S(1)} %get-tuple-element.38), channel_id=1, source_target_pairs={{0,8},{8,16},{16,24},{24,0},{1,9},{9,17},{17,25},{25,1},{2,10},{10... | collective-permute-start | bytes 12296 | tf_op jit(solution)/shard_map/ppermute | solution.py:476
  9.2 5.8 %collective-permute-start.3 = (f32[8,128]{1,0:T(8,128)S(1)}, f32[8,128]{1,0:T(8,128)S(1)}, u32[]{:S(2)}, u32[]{:S(2)}) collective-permute-start(f32[8,128]{1,0:T(8,128)S(1)} %get-tuple-element.39), channel_id=1, source_target_pairs={{0,24},{8,0},{16,8},{24,16},{1,25},{9,1},{17,9},{25,17},{2,26},{10... | collective-permute-start | bytes 12296 | tf_op jit(solution)/shard_map/ppermute | solution.py:476
  16.6 7.7 %collective-permute-start.4 = (f32[144,128]{1,0:T(8,128)S(1)}, f32[144,128]{1,0:T(8,128)S(1)}, u32[]{:S(2)}, u32[]{:S(2)}) collective-permute-start(f32[144,128]{1,0:T(8,128)S(1)} %get-tuple-element.46), channel_id=1, source_target_pairs={{0,7},{1,6},{2,5},{3,4},{4,3},{5,2},{6,1},{7,0},{8,15},{9,14},{10,... | collective-permute-start | bytes 221192 | tf_op jit(solution)/shard_map/ppermute | solution.py:562
  18.3 6.8 %collective-permute-start.5 = (f32[144,128]{1,0:T(8,128)S(1)}, f32[144,128]{1,0:T(8,128)S(1)}, u32[]{:S(2)}, u32[]{:S(2)}) collective-permute-start(f32[144,128]{1,0:T(8,128)S(1)} %get-tuple-element.47), channel_id=1, source_target_pairs={{0,6},{1,7},{2,4},{3,5},{4,2},{5,3},{6,0},{7,1},{8,14},{9,15},{10,... | collective-permute-start | bytes 221192 | tf_op jit(solution)/shard_map/ppermute | solution.py:562
  18.7 12.3 %collective-permute-start.6 = (f32[144,128]{1,0:T(8,128)S(1)}, f32[144,128]{1,0:T(8,128)S(1)}, u32[]{:S(2)}, u32[]{:S(2)}) collective-permute-start(f32[144,128]{1,0:T(8,128)S(1)} %get-tuple-element.48), channel_id=1, source_target_pairs={{0,5},{1,4},{2,7},{3,6},{4,1},{5,0},{6,3},{7,2},{8,13},{9,12},{10,... | collective-permute-start | bytes 221192 | tf_op jit(solution)/shard_map/ppermute | solution.py:562
  20.3 11.3 %collective-permute-start.7 = (f32[144,128]{1,0:T(8,128)S(1)}, f32[144,128]{1,0:T(8,128)S(1)}, u32[]{:S(2)}, u32[]{:S(2)}) collective-permute-start(f32[144,128]{1,0:T(8,128)S(1)} %get-tuple-element.49), channel_id=1, source_target_pairs={{0,4},{1,5},{2,6},{3,7},{4,0},{5,1},{6,2},{7,3},{8,12},{9,13},{10,... | collective-permute-start | bytes 221192 | tf_op jit(solution)/shard_map/ppermute | solution.py:562
  24.3 8.3 %collective-permute-start.8 = (f32[144,128]{1,0:T(8,128)S(1)}, f32[144,128]{1,0:T(8,128)S(1)}, u32[]{:S(2)}, u32[]{:S(2)}) collective-permute-start(f32[144,128]{1,0:T(8,128)S(1)} %get-tuple-element.50), channel_id=1, source_target_pairs={{0,3},{1,2},{2,1},{3,0},{4,7},{5,6},{6,5},{7,4},{8,11},{9,10},{10,... | collective-permute-start | bytes 221192 | tf_op jit(solution)/shard_map/ppermute | solution.py:562
  24.3 8.3 %collective-permute-start.9 = (f32[144,128]{1,0:T(8,128)S(1)}, f32[144,128]{1,0:T(8,128)S(1)}, u32[]{:S(2)}, u32[]{:S(2)}) collective-permute-start(f32[144,128]{1,0:T(8,128)S(1)} %get-tuple-element.51), channel_id=1, source_target_pairs={{0,2},{1,3},{2,0},{3,1},{4,6},{5,7},{6,4},{7,5},{8,10},{9,11},{10,... | collective-permute-start | bytes 221192 | tf_op jit(solution)/shard_map/ppermute | solution.py:562
  25.0 7.6 %collective-permute-start.10 = (f32[144,128]{1,0:T(8,128)S(1)}, f32[144,128]{1,0:T(8,128)S(1)}, u32[]{:S(2)}, u32[]{:S(2)}) collective-permute-start(f32[144,128]{1,0:T(8,128)S(1)} %get-tuple-element.52), channel_id=1, source_target_pairs={{0,1},{1,0},{2,3},{3,2},{4,5},{5,4},{6,7},{7,6},{8,9},{9,8},{10,11... | collective-permute-start | bytes 221192 | tf_op jit(solution)/shard_map/ppermute | solution.py:562

commit v6 on v5

--- a/solution.py
+++ b/solution.py
@@ -95,6 +95,7 @@
 def prepare_kernel(
     cols_hbm, mix_hbm, parent_hbm, pwet_hbm, child_hbm, cwet_hbm,
     flat_ref, forth_ref, back_ref, left_ref, right_ref, weight_ref, carry_ref, below_ref, inverse_ref, again_ref,
+    mask_ref,
     cols_ref, mix_ref, parent_ref, pwet_ref, cwet_ref, edge_ref, turn_ref, row_ref, d_ref, c_ref, sems,
 ):
     levels, capacity, tracers, child_rows = child_hbm.shape
@@ -131,6 +132,7 @@
     left_ref[...] = flat_ref[:rows, :]
     right_ref[...] = flat_ref[(width - 1) * rows :, :]
     fetch_cwet.wait()
+    masks(cols_ref, cwet_ref, mask_ref, tracers)
     fetch_again.wait()
     base = len(tiles) * level_rows
     fetch_first.wait()
@@ -158,8 +160,8 @@
 
 
 def inner_kernel(
-    cols_ref, child_ref, cwet_ref,
-    explicit_ref, mask_ref,
+    child_ref, mask_ref,
+    explicit_ref,
     begin_ref,
 ):
     levels, capacity, tracers, child_rows = child_ref.shape
@@ -167,7 +169,6 @@
     live = capacity * tracers
     stored = up(live, 8)
     stride = begin_ref.shape[1] // levels
-    masks(cols_ref, cwet_ref, mask_ref, tracers)
     flat_child = child_ref.reshape(levels * live, child_rows)
     lane = lax.broadcasted_iota(jnp.int32, (stored, LANES), 1)
     gap = jnp.zeros((tracers, LANES), jnp.float32)
@@ -495,14 +496,14 @@
     parent = jnp.transpose(parent_tracer, (0, 2, 3, 1))
     child = jnp.transpose(child_tracer, (1, 2, 0, 3))
 
-    flat, forth, back, left_edge, right_edge, weight, carry, below, inverse, cols = pl.pallas_call(
+    flat, forth, back, left_edge, right_edge, weight, carry, below, inverse, cols, mask = pl.pallas_call(
         prepare_kernel,
         in_specs=[HBM] * 6,
-        out_specs=[VM] * 10,
+        out_specs=[VM] * 11,
         out_shape=[
             f32(width * rows, LANES), f32(message, LANES), f32(message, LANES), f32(rows, LANES), f32(rows, LANES),
             f32(8 * levels, LANES), f32(8 * levels, LANES), f32(8 * levels, LANES), f32(LANES, LANES),
-            jax.ShapeDtypeStruct(strip_cols.shape, jnp.int32),
+            jax.ShapeDtypeStruct(strip_cols.shape, jnp.int32), f32(lane_tiles, stored + 8, LANES),
         ],
         scratch_shapes=[
             pltpu.SMEM(strip_cols.shape, jnp.int32),
@@ -528,15 +529,15 @@
     forth = ring(forth, ("parent", "child"), devices, 1)
     back = ring(back, ("parent", "child"), devices, -1)
 
-    explicit, mask = pl.pallas_call(
+    explicit = pl.pallas_call(
         inner_kernel,
-        in_specs=[SM, VM, VM],
-        out_specs=[VM] * 2,
-        out_shape=[f32(lane_tiles, plane, LANES), f32(lane_tiles, stored + 8, LANES)],
+        in_specs=[VM, VM],
+        out_specs=VM,
+        out_shape=f32(lane_tiles, plane, LANES),
         scratch_shapes=[mem(lane_tiles, levels * stride, LANES)],
         compiler_params=params(16),
         name="inner",
-    )(cols, child, child_wet)
+    )(child, mask)
 
     block = f32(2 * narrow * rows, LANES)
     *blocks, parent_mid, own, halo = pl.pallas_call(

time: 36.6 us -> 35.5 us (0.970)
  waiting for transfers between devices: 2.89 us -> 1.8 us
  Pallas kernels: 13.1 us -> 12.7 us
  starting transfers between devices: 19 us -> 19.4 us
    ppermute x7, waiting for transfers between devices: 2.88 us -> 1.79 us  [body(): lax.ppermute(blocks[s], 'child', [(i, i ^ s) for i in range(strips)])]
    ppermute x7, starting transfers between devices: 10.7 us -> 11.2 us  [body(): lax.ppermute(blocks[s], 'child', [(i, i ^ s) for i in range(strips)])]
    pallas_call x2, Pallas kernels: 5.37 us -> 4.97 us  [the longest x1 2.91 us: body(): pl.pallas_call(inner_kernel, in_specs=[VM, VM], out_specs=VM, out_shape=f...]
  transfers between devices with their start and end apart: 11 -> 11, of which waited for: 4 -> 3; matrix products, arithmetic and copies ran while one was open for 0% -> 0% of each run, Pallas kernels for 16% -> 15%
where the time goes in v6:
time: 35.5 us; the launch traced here: 35.4 us
  starting transfers between devices  19.4 us (55%)
  Pallas kernels  12.7 us (36%)
  waiting for transfers between devices  1.8 us (5%)
  between operations  1.39 us (4%)
    ppermute x7, starting transfers between devices, body(): lax.ppermute(blocks[s], 'child', [(i, i ^ s) for i in range(strips)])  11.2 us
    ppermute x4, starting transfers between devices, ring(): lax.ppermute(block, axes, [(i, (i + step) % count) for i in range(count)])  8.24 us
    pallas_call x1, Pallas kernels, body(): pl.pallas_call(functools.partial(finish_kernel, strips, rows, chunks), in...  3.73 us
    pallas_call x1, Pallas kernels, body(): pl.pallas_call(inner_kernel, in_specs=[VM, VM], out_specs=VM, out_shape=f...  2.91 us
    pallas_call x1, Pallas kernels, body(): pl.pallas_call(functools.partial(level_kernel, tracers, levels, capacity)...  2.41 us
    pallas_call x1, Pallas kernels, body(): pl.pallas_call(prepare_kernel, in_specs=[HBM] * 6, out_specs=[VM] * 11, o...  2.06 us
    ppermute x7, waiting for transfers between devices, body(): lax.ppermute(blocks[s], 'child', [(i, i ^ s) for i in range(strips)])  1.79 us
    pallas_call x1, Pallas kernels, body(): pl.pallas_call(functools.partial(pack_kernel, groups, strips, rows, trace...  1.62 us
  transfers between devices with their start and end apart: 11, of which 3 were waited for; matrix products, arithmetic and copies ran while one was open for 0% of the time, Pallas kernels for 15%

profile of v6, /device:TPU:0, one launch (start us, length us, event | category | flops | bytes accessed | tf_op | source)
XLA Modules:
  0.0 35.4 jit_solution(7894315660661649294)
XLA Ops:
  0.6 0.0 copy-start
  0.6 2.1 %prepare.1 = (f32[384,128]{1,0:T(8,128)S(1)}, f32[256,128]{1,0:T(8,128)S(1)}, f32[256,128]{1,0:T(8,128)S(1)}, f32[8,128]{1,0:T(8,128)S(1)}, f32[8,128]{1,0:T(8,1...) custom-call(s32[4,8]{1,0:T(4,128)} %cols_hbm.1, ...), custom_call_target="tpu_custom_call" | custom-call | tf_op jit(solution)/shard_map/prepare/pallas_call | solution.py:499
  2.7 0.0 copy-start.1
  2.7 3.0 %collective-permute-start = (f32[256,128]{1,0:T(8,128)S(1)}, f32[256,128]{1,0:T(8,128)S(1)}, u32[]{:S(2)}, u32[]{:S(2)}) collective-permute-start(f32[256,128]{1,0:T(8,128)S(1)} %get-tuple-element.35), channel_id=1, source_target_pairs={{0,1},{1,2},{2,3},{3,4},{4,5},{5,6},{6,7},{7,8},{8,9},{9,10},{10,1... | collective-permute-start | bytes 393224 | tf_op jit(solution)/shard_map/ppermute | solution.py:477
  5.7 3.5 %collective-permute-start.1 = (f32[256,128]{1,0:T(8,128)S(1)}, f32[256,128]{1,0:T(8,128)S(1)}, u32[]{:S(2)}, u32[]{:S(2)}) collective-permute-start(f32[256,128]{1,0:T(8,128)S(1)} %get-tuple-element.36), channel_id=1, source_target_pairs={{0,31},{1,0},{2,1},{3,2},{4,3},{5,4},{6,5},{7,6},{8,7},{9,8},{10,9... | collective-permute-start | bytes 393224 | tf_op jit(solution)/shard_map/ppermute | solution.py:477
  9.2 0.0 collective-permute-start.2
  9.2 1.7 %collective-permute-start.3 = (f32[8,128]{1,0:T(8,128)S(1)}, f32[8,128]{1,0:T(8,128)S(1)}, u32[]{:S(2)}, u32[]{:S(2)}) collective-permute-start(f32[8,128]{1,0:T(8,128)S(1)} %get-tuple-element.38), channel_id=1, source_target_pairs={{0,24},{8,0},{16,8},{24,16},{1,25},{9,1},{17,9},{25,17},{2,26},{10... | collective-permute-start | bytes 12296 | tf_op jit(solution)/shard_map/ppermute | solution.py:477
  11.6 0.0 copy-done
  11.6 2.9 %inner.1.explicit_ref = f32[2,3136,128]{2,1,0:T(8,128)S(1)} custom-call(f32[50,27,2,144]{3,2,1,0:T(2,128)S(1)} %bitcast.5, f32[2,64,128]{2,1,0:T(8,128)S(1)} %get-tuple-element.33.mask_ref), custom_call_target="tpu_custom_call" | custom-call | tf_op jit(solution)/shard_map/inner/pallas_call | solution.py:532
  14.5 0.0 collective-permute-done.2.left_ref
  14.5 0.0 collective-permute-done.3.right_ref
  14.6 0.0 collective-permute-done.before_ref
  14.6 0.0 collective-permute-done.1.after_ref
  14.6 0.0 copy-done.1
  14.6 1.6 %pack.1 = (f32[144,128]{1,0:T(8,128)S(1)}, f32[144,128]{1,0:T(8,128)S(1)}, f32[144,128]{1,0:T(8,128)S(1)}, f32[144,128]{1,0:T(8,128)S(1)}, f32[144,128]{1,0:T(8,...) custom-call(s32[4,8]{1,0:T(4,128)S(1)} %get-tuple-element.28.cols_re, ...), custom_call_target="tpu_custom_call" | custom-call | tf_op jit(solution)/shard_map/pack/pallas_call | solution.py:543
  16.2 1.9 %collective-permute-start.4 = (f32[144,128]{1,0:T(8,128)S(1)}, f32[144,128]{1,0:T(8,128)S(1)}, u32[]{:S(2)}, u32[]{:S(2)}) collective-permute-start(f32[144,128]{1,0:T(8,128)S(1)} %get-tuple-element.44), channel_id=1, source_target_pairs={{0,7},{1,6},{2,5},{3,4},{4,3},{5,2},{6,1},{7,0},{8,15},{9,14},{10,... | collective-permute-start | bytes 221192 | tf_op jit(solution)/shard_map/ppermute | solution.py:563
  18.1 0.6 %collective-permute-start.5 = (f32[144,128]{1,0:T(8,128)S(1)}, f32[144,128]{1,0:T(8,128)S(1)}, u32[]{:S(2)}, u32[]{:S(2)}) collective-permute-start(f32[144,128]{1,0:T(8,128)S(1)} %get-tuple-element.45), channel_id=1, source_target_pairs={{0,6},{1,7},{2,4},{3,5},{4,2},{5,3},{6,0},{7,1},{8,14},{9,15},{10,... | collective-permute-start | bytes 221192 | tf_op jit(solution)/shard_map/ppermute | solution.py:563
  18.7 1.6 %collective-permute-start.6 = (f32[144,128]{1,0:T(8,128)S(1)}, f32[144,128]{1,0:T(8,128)S(1)}, u32[]{:S(2)}, u32[]{:S(2)}) collective-permute-start(f32[144,128]{1,0:T(8,128)S(1)} %get-tuple-element.46), channel_id=1, source_target_pairs={{0,5},{1,4},{2,7},{3,6},{4,1},{5,0},{6,3},{7,2},{8,13},{9,12},{10,... | collective-permute-start | bytes 221192 | tf_op jit(solution)/shard_map/ppermute | solution.py:563
  20.4 3.6 %collective-permute-start.7 = (f32[144,128]{1,0:T(8,128)S(1)}, f32[144,128]{1,0:T(8,128)S(1)}, u32[]{:S(2)}, u32[]{:S(2)}) collective-permute-start(f32[144,128]{1,0:T(8,128)S(1)} %get-tuple-element.47), channel_id=1, source_target_pairs={{0,4},{1,5},{2,6},{3,7},{4,0},{5,1},{6,2},{7,3},{8,12},{9,13},{10,... | collective-permute-start | bytes 221192 | tf_op jit(solution)/shard_map/ppermute | solution.py:563
  23.9 0.0 collective-permute-start.8
  23.9 0.0 collective-permute-done.4.refs_0_
  23.9 0.7 %collective-permute-start.9 = (f32[144,128]{1,0:T(8,128)S(1)}, f32[144,128]{1,0:T(8,128)S(1)}, u32[]{:S(2)}, u32[]{:S(2)}) collective-permute-start(f32[144,128]{1,0:T(8,128)S(1)} %get-tuple-element.49), channel_id=1, source_target_pairs={{0,2},{1,3},{2,0},{3,1},{4,6},{5,7},{6,4},{7,5},{8,10},{9,11},{10,... | collective-permute-start | bytes 221192 | tf_op jit(solution)/shard_map/ppermute | solution.py:563
  24.6 0.1 collective-permute-done.5.refs_1_
  24.7 2.8 %collective-permute-start.10 = (f32[144,128]{1,0:T(8,128)S(1)}, f32[144,128]{1,0:T(8,128)S(1)}, u32[]{:S(2)}, u32[]{:S(2)}) collective-permute-start(f32[144,128]{1,0:T(8,128)S(1)} %get-tuple-element.50), channel_id=1, source_target_pairs={{0,1},{1,0},{2,3},{3,2},{4,5},{5,4},{6,7},{7,6},{8,9},{9,8},{10,11... | collective-permute-start | bytes 221192 | tf_op jit(solution)/shard_map/ppermute | solution.py:563
  27.6 2.4 %levels.1 = (f32[2,3136,128]{2,1,0:T(8,128)S(1)}, f32[576,128]{1,0:T(8,128)S(1)}) custom-call(s32[4,8]{1,0:T(4,128)S(1)} %get-tuple-element.28.cols_ref, f32[400,128]{1,0:T(8,128)S(1)} %get-tuple-element.29.weight_ref, f32[400,128]{1,0:T(8,128)S(1)} %get-tuple-element.30.carry_ref, f32[400,128]{1,0:T(8,128)S(1)} %get-tuple-element.31.back_ref, ...), custom_call_target="tpu_custom_call" | custom-call | tf_op jit(solution)/shard_map/levels/pallas_call | solution.py:566
  30.0 1.4 %collective-permute-done.6.refs_2_ = f32[144,128]{1,0:T(8,128)S(1)} collective-permute-done((f32[144,128]{1,0:T(8,128)S(1)}, f32[144,128]{1,0:T(8,128)S(1)}, u32[]{:S(2)}, u32[]{:S(2)}) %collective-permute-start.6) | collective-permute-done | bytes 73760 | tf_op jit(solution)/shard_map/ppermute | solution.py:563
  31.4 0.0 collective-permute-done.7.refs_3_
  31.4 0.0 collective-permute-done.8.refs_4_
  31.4 0.2 collective-permute-done.9.refs_5_
  31.6 0.0 collective-permute-done.10.refs_6_
  31.6 3.7 %finish.1 = (f32[2,8,48,50]{3,2,1,0:T(8,128)}, f32[50,27,2,144]{3,2,1,0:T(2,128)}) custom-call(s32[4,8]{1,0:T(4,128)S(1)} %get-tuple-element.28.cols_ref, s32[1]{0:T(128)S(6)} %copy.9.offset_ref, f32[576,128]{1,0:T(8,128)S(1)} %get-tuple-element.41.own_ref, f32[384,128]{1,0:T(8,128)S(1)} %get-tuple-element.42.pmid_ref, ...), custom_call_target="tpu_custom_call" | custom-call | tf_op jit(solution)/shard_map/finish/pallas_call | solution.py:576
Async XLA Ops:
  0.6 11.0 %copy-start = (f32[2,50,27,144]{3,0,2,1:T(2,128)S(1)}, f32[2,50,27,144]{3,0,2,1:T(2,128)}, u32[]{:S(2)}) copy-start(f32[2,50,27,144]{3,0,2,1:T(2,128)} %param.8) | copy-start | bytes 4665604
  2.7 11.9 %copy-start.1 = (s32[27,144]{1,0:T(8,128)S(1)}, s32[27,144]{1,0:T(8,128)}, u32[]{:S(2)}) copy-start(s32[27,144]{1,0:T(8,128)} %cwet_ref.1) | copy-start | bytes 46660
  2.7 11.8 %collective-permute-start = (f32[256,128]{1,0:T(8,128)S(1)}, f32[256,128]{1,0:T(8,128)S(1)}, u32[]{:S(2)}, u32[]{:S(2)}) collective-permute-start(f32[256,128]{1,0:T(8,128)S(1)} %get-tuple-element.35), channel_id=1, source_target_pairs={{0,1},{1,2},{2,3},{3,4},{4,5},{5,6},{6,7},{7,8},{8,9},{9,10},{10,1... | collective-permute-start | bytes 393224 | tf_op jit(solution)/shard_map/ppermute | solution.py:477
  5.7 8.8 %collective-permute-start.1 = (f32[256,128]{1,0:T(8,128)S(1)}, f32[256,128]{1,0:T(8,128)S(1)}, u32[]{:S(2)}, u32[]{:S(2)}) collective-permute-start(f32[256,128]{1,0:T(8,128)S(1)} %get-tuple-element.36), channel_id=1, source_target_pairs={{0,31},{1,0},{2,1},{3,2},{4,3},{5,4},{6,5},{7,6},{8,7},{9,8},{10,9... | collective-permute-start | bytes 393224 | tf_op jit(solution)/shard_map/ppermute | solution.py:477
  9.2 5.3 %collective-permute-start.2 = (f32[8,128]{1,0:T(8,128)S(1)}, f32[8,128]{1,0:T(8,128)S(1)}, u32[]{:S(2)}, u32[]{:S(2)}) collective-permute-start(f32[8,128]{1,0:T(8,128)S(1)} %get-tuple-element.37), channel_id=1, source_target_pairs={{0,8},{8,16},{16,24},{24,0},{1,9},{9,17},{17,25},{25,1},{2,10},{10... | collective-permute-start | bytes 12296 | tf_op jit(solution)/shard_map/ppermute | solution.py:477
  9.2 5.3 %collective-permute-start.3 = (f32[8,128]{1,0:T(8,128)S(1)}, f32[8,128]{1,0:T(8,128)S(1)}, u32[]{:S(2)}, u32[]{:S(2)}) collective-permute-start(f32[8,128]{1,0:T(8,128)S(1)} %get-tuple-element.38), channel_id=1, source_target_pairs={{0,24},{8,0},{16,8},{24,16},{1,25},{9,1},{17,9},{25,17},{2,26},{10... | collective-permute-start | bytes 12296 | tf_op jit(solution)/shard_map/ppermute | solution.py:477
  16.2 7.7 %collective-permute-start.4 = (f32[144,128]{1,0:T(8,128)S(1)}, f32[144,128]{1,0:T(8,128)S(1)}, u32[]{:S(2)}, u32[]{:S(2)}) collective-permute-start(f32[144,128]{1,0:T(8,128)S(1)} %get-tuple-element.44), channel_id=1, source_target_pairs={{0,7},{1,6},{2,5},{3,4},{4,3},{5,2},{6,1},{7,0},{8,15},{9,14},{10,... | collective-permute-start | bytes 221192 | tf_op jit(solution)/shard_map/ppermute | solution.py:563
  18.1 6.6 %collective-permute-start.5 = (f32[144,128]{1,0:T(8,128)S(1)}, f32[144,128]{1,0:T(8,128)S(1)}, u32[]{:S(2)}, u32[]{:S(2)}) collective-permute-start(f32[144,128]{1,0:T(8,128)S(1)} %get-tuple-element.45), channel_id=1, source_target_pairs={{0,6},{1,7},{2,4},{3,5},{4,2},{5,3},{6,0},{7,1},{8,14},{9,15},{10,... | collective-permute-start | bytes 221192 | tf_op jit(solution)/shard_map/ppermute | solution.py:563
  18.7 12.7 %collective-permute-start.6 = (f32[144,128]{1,0:T(8,128)S(1)}, f32[144,128]{1,0:T(8,128)S(1)}, u32[]{:S(2)}, u32[]{:S(2)}) collective-permute-start(f32[144,128]{1,0:T(8,128)S(1)} %get-tuple-element.46), channel_id=1, source_target_pairs={{0,5},{1,4},{2,7},{3,6},{4,1},{5,0},{6,3},{7,2},{8,13},{9,12},{10,... | collective-permute-start | bytes 221192 | tf_op jit(solution)/shard_map/ppermute | solution.py:563
  20.4 11.1 %collective-permute-start.7 = (f32[144,128]{1,0:T(8,128)S(1)}, f32[144,128]{1,0:T(8,128)S(1)}, u32[]{:S(2)}, u32[]{:S(2)}) collective-permute-start(f32[144,128]{1,0:T(8,128)S(1)} %get-tuple-element.47), channel_id=1, source_target_pairs={{0,4},{1,5},{2,6},{3,7},{4,0},{5,1},{6,2},{7,3},{8,12},{9,13},{10,... | collective-permute-start | bytes 221192 | tf_op jit(solution)/shard_map/ppermute | solution.py:563
  23.9 7.5 %collective-permute-start.8 = (f32[144,128]{1,0:T(8,128)S(1)}, f32[144,128]{1,0:T(8,128)S(1)}, u32[]{:S(2)}, u32[]{:S(2)}) collective-permute-start(f32[144,128]{1,0:T(8,128)S(1)} %get-tuple-element.48), channel_id=1, source_target_pairs={{0,3},{1,2},{2,1},{3,0},{4,7},{5,6},{6,5},{7,4},{8,11},{9,10},{10,... | collective-permute-start | bytes 221192 | tf_op jit(solution)/shard_map/ppermute | solution.py:563
  23.9 7.7 %collective-permute-start.9 = (f32[144,128]{1,0:T(8,128)S(1)}, f32[144,128]{1,0:T(8,128)S(1)}, u32[]{:S(2)}, u32[]{:S(2)}) collective-permute-start(f32[144,128]{1,0:T(8,128)S(1)} %get-tuple-element.49), channel_id=1, source_target_pairs={{0,2},{1,3},{2,0},{3,1},{4,6},{5,7},{6,4},{7,5},{8,10},{9,11},{10,... | collective-permute-start | bytes 221192 | tf_op jit(solution)/shard_map/ppermute | solution.py:563
  24.7 6.9 %collective-permute-start.10 = (f32[144,128]{1,0:T(8,128)S(1)}, f32[144,128]{1,0:T(8,128)S(1)}, u32[]{:S(2)}, u32[]{:S(2)}) collective-permute-start(f32[144,128]{1,0:T(8,128)S(1)} %get-tuple-element.50), channel_id=1, source_target_pairs={{0,1},{1,0},{2,3},{3,2},{4,5},{5,4},{6,7},{7,6},{8,9},{9,8},{10,11... | collective-permute-start | bytes 221192 | tf_op jit(solution)/shard_map/ppermute | solution.py:563

commit v7 on v6

--- a/solution.py
+++ b/solution.py
@@ -205,11 +205,13 @@
 
 def pack_kernel(
     groups, strips, rows, tracers, levels,
-    cols_ref, offset_ref, flat_ref, before_ref, after_ref, left_ref, right_ref, inverse_ref, explicit_ref, cwet_ref,
+    cols_hbm, offset_ref, flat_ref, before_ref, after_ref, left_ref, right_ref, inverse_ref, explicit_ref, cwet_ref,
     *refs,
 ):
     send_refs = refs[:strips]
-    pmid_ref, own_ref, halo_ref, step_ref, wide_ref, turn_ref, end_ref, long_ref, start_ref = refs[strips:]
+    pmid_ref, own_ref, halo_ref, step_ref, wide_ref, turn_ref, end_ref, long_ref, start_ref, cols_ref, sem = refs[strips:]
+    fetch_cols = pltpu.make_async_copy(cols_hbm, cols_ref, sem)
+    fetch_cols.start()
     capacity, child_rows = cwet_ref.shape
     stored = up(capacity * tracers, 8)
     slot = LANES // tracers
@@ -222,9 +224,6 @@
     base = len(tiles) * level_rows
     group, member = lax.axis_index("parent"), lax.axis_index("child")
     offset = offset_ref[0]
-    cols = my_cols(cols_ref)
-    for j, start in enumerate(strip_starts(cols_ref, strips)):
-        start_ref[j] = start
 
     has_before = (member > 0).astype(jnp.float32)
     has_after = (member < strips - 1).astype(jnp.float32)
@@ -245,6 +244,10 @@
     wide_ref[: width * rows, :] = solved
     wide_ref[width * rows :, :] = jnp.zeros((narrow * rows, LANES), jnp.float32)
     pmid_ref[...] = solved
+    fetch_cols.wait()
+    cols = my_cols(cols_ref)
+    for j, start in enumerate(strip_starts(cols_ref, strips)):
+        start_ref[j] = start
     for s in range(strips):
         start = start_ref[member ^ s]
         send_refs[s][: narrow * rows, :] = wide_ref[pl.ds(pl.multiple_of(start * rows, rows), narrow * rows), :]
@@ -362,15 +365,17 @@
 
 def finish_kernel(
     strips, rows, chunks,
-    cols_ref, offset_ref, own_ref, pmid_ref, inverse_ref, cmid_ref, mask_ref,
+    cols_hbm, offset_ref, own_ref, pmid_ref, inverse_ref, cmid_ref, mask_ref,
     *refs,
 ):
     got_refs = {s: ref for s, ref in zip(far_first(strips), refs)}
     (
         pnext_hbm, cnext_hbm,
         panel_ref, wide_ref, ends_ref, long_ref, end_ref, add_ref, next_ref, pkeep_ref, ckeep_ref,
-        start_ref, sems,
+        start_ref, cols_ref, sems,
     ) = refs[strips:]
+    fetch_cols = pltpu.make_async_copy(cols_hbm, cols_ref, sems.at[1 + chunks])
+    fetch_cols.start()
     levels, capacity, tracers, child_rows = cnext_hbm.shape
     slot = LANES // tracers
     width = pmid_ref.shape[0] // rows
@@ -383,8 +388,6 @@
     padded = up(narrow, 8)
     member = lax.axis_index("child")
     group = lax.axis_index("parent")
-    for j, start in enumerate(strip_starts(cols_ref, strips)):
-        start_ref[j] = start
     offset = offset_ref[0]
     ends_ref[...] = jnp.zeros_like(ends_ref)
     for q in range(narrow):
@@ -447,6 +450,9 @@
         sends.append(pltpu.make_async_copy(ckeep_ref.at[part], cnext_hbm.at[part], sems.at[1 + c]))
         sends[-1].start()
 
+    fetch_cols.wait()
+    for j, start in enumerate(strip_starts(cols_ref, strips)):
+        start_ref[j] = start
     for s in range(strips):
         j = member ^ s
         start, cols = start_ref[j], cols_ref[group, j]
@@ -542,7 +548,7 @@
     block = f32(2 * narrow * rows, LANES)
     *blocks, parent_mid, own, halo = pl.pallas_call(
         functools.partial(pack_kernel, groups, strips, rows, tracers, levels),
-        in_specs=[SM, SM] + [VM] * 8,
+        in_specs=[HBM, SM] + [VM] * 8,
         out_specs=[VM] * (strips + 3),
         out_shape=[block] * strips
         + [f32(width * rows, LANES), f32(narrow * all_rows, LANES), f32(lane_tiles, 8 * up(levels, 8), LANES)],
@@ -553,10 +559,12 @@
             mem(packed, LANES, LANES),
             mem(narrow * child_rows, LANES),
             pltpu.SMEM((strips,), jnp.int32),
+            pltpu.SMEM(strip_cols.shape, jnp.int32),
+            pltpu.SemaphoreType.DMA(()),
         ],
         compiler_params=params(16),
         name="pack",
-    )(cols, row_offset, flat, forth, back, right_edge, left_edge, inverse, explicit, child_wet)
+    )(in_hbm(strip_cols), row_offset, flat, forth, back, right_edge, left_edge, inverse, explicit, child_wet)
 
     got = {0: blocks[0]}
     for s in far_first(strips)[:-1]:
@@ -575,7 +583,7 @@
 
     parent_next, child_next = pl.pallas_call(
         functools.partial(finish_kernel, strips, rows, chunks),
-        in_specs=[SM, SM] + [VM] * (5 + strips),
+        in_specs=[HBM, SM] + [VM] * (5 + strips),
         out_specs=[HBM, HBM],
         out_shape=[f32(*parent.shape), f32(*child.shape)],
         scratch_shapes=[
@@ -589,11 +597,12 @@
             mem(*parent.shape),
             mem(levels + 1, *child.shape[1:]),
             pltpu.SMEM((strips,), jnp.int32),
-            pltpu.SemaphoreType.DMA((1 + chunks,)),
+            pltpu.SMEM(strip_cols.shape, jnp.int32),
+            pltpu.SemaphoreType.DMA((2 + chunks,)),
         ],
         compiler_params=params(24),
         name="finish",
-    )(cols, row_offset, mean, parent_mid, inverse, child_mid, mask, *got)
+    )(in_hbm(strip_cols), row_offset, mean, parent_mid, inverse, child_mid, mask, *got)
     return jnp.transpose(parent_next, (0, 3, 1, 2)), jnp.transpose(child_next, (2, 0, 1, 3))
 
 

time: 35.5 us -> 35.2 us (level)
  Pallas kernels: 12.7 us -> 12.3 us
    pallas_call x1, Pallas kernels: 3.73 us -> 3.27 us  [body(): pl.pallas_call(functools.partial(finish_kernel, strips, rows, chunks), in...]
where the time goes in v7:
time: 35.2 us; the launch traced here: 35 us
  starting transfers between devices  19.5 us (55%)
  Pallas kernels  12.3 us (35%)
  waiting for transfers between devices  1.8 us (5%)
  between operations  1.39 us (4%)
    ppermute x7, starting transfers between devices, body(): lax.ppermute(blocks[s], 'child', [(i, i ^ s) for i in range(strips)])  11.2 us
    ppermute x4, starting transfers between devices, ring(): lax.ppermute(block, axes, [(i, (i + step) % count) for i in range(count)])  8.24 us
    pallas_call x1, Pallas kernels, body(): pl.pallas_call(functools.partial(finish_kernel, strips, rows, chunks), in...  3.27 us
    pallas_call x1, Pallas kernels, body(): pl.pallas_call(inner_kernel, in_specs=[VM, VM], out_specs=VM, out_shape=f...  2.91 us
    pallas_call x1, Pallas kernels, body(): pl.pallas_call(functools.partial(level_kernel, tracers, levels, capacity)...  2.41 us
    pallas_call x1, Pallas kernels, body(): pl.pallas_call(prepare_kernel, in_specs=[HBM] * 6, out_specs=[VM] * 11, o...  2.06 us
    ppermute x7, waiting for transfers between devices, body(): lax.ppermute(blocks[s], 'child', [(i, i ^ s) for i in range(strips)])  1.79 us
    pallas_call x1, Pallas kernels, body(): pl.pallas_call(functools.partial(pack_kernel, groups, strips, rows, trace...  1.7 us
  transfers between devices with their start and end apart: 11, of which 3 were waited for; matrix products, arithmetic and copies ran while one was open for 0% of the time, Pallas kernels for 15%

profile of v7, /device:TPU:0, one launch (start us, length us, event | category | flops | bytes accessed | tf_op | source)
XLA Modules:
  0.0 35.0 jit_solution(13035463589931698347)
XLA Ops:
  0.6 0.0 copy-start
  0.6 2.1 %prepare.1 = (f32[384,128]{1,0:T(8,128)S(1)}, f32[256,128]{1,0:T(8,128)S(1)}, f32[256,128]{1,0:T(8,128)S(1)}, f32[8,128]{1,0:T(8,128)S(1)}, f32[8,128]{1,0:T(8,1...) custom-call(s32[4,8]{1,0:T(4,128)} %cols_hbm.5, ...), custom_call_target="tpu_custom_call" | custom-call | tf_op jit(solution)/shard_map/prepare/pallas_call | solution.py:505
  2.7 0.0 copy-start.1
  2.7 3.0 %collective-permute-start = (f32[256,128]{1,0:T(8,128)S(1)}, f32[256,128]{1,0:T(8,128)S(1)}, u32[]{:S(2)}, u32[]{:S(2)}) collective-permute-start(f32[256,128]{1,0:T(8,128)S(1)} %get-tuple-element.35), channel_id=1, source_target_pairs={{0,1},{1,2},{2,3},{3,4},{4,5},{5,6},{6,7},{7,8},{8,9},{9,10},{10,1... | collective-permute-start | bytes 393224 | tf_op jit(solution)/shard_map/ppermute | solution.py:483
  5.7 3.5 %collective-permute-start.1 = (f32[256,128]{1,0:T(8,128)S(1)}, f32[256,128]{1,0:T(8,128)S(1)}, u32[]{:S(2)}, u32[]{:S(2)}) collective-permute-start(f32[256,128]{1,0:T(8,128)S(1)} %get-tuple-element.36), channel_id=1, source_target_pairs={{0,31},{1,0},{2,1},{3,2},{4,3},{5,4},{6,5},{7,6},{8,7},{9,8},{10,9... | collective-permute-start | bytes 393224 | tf_op jit(solution)/shard_map/ppermute | solution.py:483
  9.2 0.0 collective-permute-start.2
  9.2 1.7 %collective-permute-start.3 = (f32[8,128]{1,0:T(8,128)S(1)}, f32[8,128]{1,0:T(8,128)S(1)}, u32[]{:S(2)}, u32[]{:S(2)}) collective-permute-start(f32[8,128]{1,0:T(8,128)S(1)} %get-tuple-element.38), channel_id=1, source_target_pairs={{0,24},{8,0},{16,8},{24,16},{1,25},{9,1},{17,9},{25,17},{2,26},{10... | collective-permute-start | bytes 12296 | tf_op jit(solution)/shard_map/ppermute | solution.py:483
  11.6 0.0 copy-done
  11.6 2.9 %inner.1.explicit_ref = f32[2,3136,128]{2,1,0:T(8,128)S(1)} custom-call(f32[50,27,2,144]{3,2,1,0:T(2,128)S(1)} %bitcast.5, f32[2,64,128]{2,1,0:T(8,128)S(1)} %get-tuple-element.33.mask_ref), custom_call_target="tpu_custom_call" | custom-call | tf_op jit(solution)/shard_map/inner/pallas_call | solution.py:538
  14.5 0.0 collective-permute-done.2.left_ref
  14.5 0.0 collective-permute-done.3.right_ref
  14.6 0.0 collective-permute-done.before_ref
  14.6 0.0 collective-permute-done.1.after_ref
  14.6 0.0 copy-done.1
  14.6 1.7 %pack.1 = (f32[144,128]{1,0:T(8,128)S(1)}, f32[144,128]{1,0:T(8,128)S(1)}, f32[144,128]{1,0:T(8,128)S(1)}, f32[144,128]{1,0:T(8,128)S(1)}, f32[144,128]{1,0:T(8,...) custom-call(s32[4,8]{1,0:T(4,128)} %cols_hbm.5, ...), custom_call_target="tpu_custom_call" | custom-call | tf_op jit(solution)/shard_map/pack/pallas_call | solution.py:549
  16.3 1.9 %collective-permute-start.4 = (f32[144,128]{1,0:T(8,128)S(1)}, f32[144,128]{1,0:T(8,128)S(1)}, u32[]{:S(2)}, u32[]{:S(2)}) collective-permute-start(f32[144,128]{1,0:T(8,128)S(1)} %get-tuple-element.44), channel_id=1, source_target_pairs={{0,7},{1,6},{2,5},{3,4},{4,3},{5,2},{6,1},{7,0},{8,15},{9,14},{10,... | collective-permute-start | bytes 221192 | tf_op jit(solution)/shard_map/ppermute | solution.py:571
  18.2 0.6 %collective-permute-start.5 = (f32[144,128]{1,0:T(8,128)S(1)}, f32[144,128]{1,0:T(8,128)S(1)}, u32[]{:S(2)}, u32[]{:S(2)}) collective-permute-start(f32[144,128]{1,0:T(8,128)S(1)} %get-tuple-element.45), channel_id=1, source_target_pairs={{0,6},{1,7},{2,4},{3,5},{4,2},{5,3},{6,0},{7,1},{8,14},{9,15},{10,... | collective-permute-start | bytes 221192 | tf_op jit(solution)/shard_map/ppermute | solution.py:571
  18.8 1.6 %collective-permute-start.6 = (f32[144,128]{1,0:T(8,128)S(1)}, f32[144,128]{1,0:T(8,128)S(1)}, u32[]{:S(2)}, u32[]{:S(2)}) collective-permute-start(f32[144,128]{1,0:T(8,128)S(1)} %get-tuple-element.46), channel_id=1, source_target_pairs={{0,5},{1,4},{2,7},{3,6},{4,1},{5,0},{6,3},{7,2},{8,13},{9,12},{10,... | collective-permute-start | bytes 221192 | tf_op jit(solution)/shard_map/ppermute | solution.py:571
  20.5 3.6 %collective-permute-start.7 = (f32[144,128]{1,0:T(8,128)S(1)}, f32[144,128]{1,0:T(8,128)S(1)}, u32[]{:S(2)}, u32[]{:S(2)}) collective-permute-start(f32[144,128]{1,0:T(8,128)S(1)} %get-tuple-element.47), channel_id=1, source_target_pairs={{0,4},{1,5},{2,6},{3,7},{4,0},{5,1},{6,2},{7,3},{8,12},{9,13},{10,... | collective-permute-start | bytes 221192 | tf_op jit(solution)/shard_map/ppermute | solution.py:571
  24.0 0.0 collective-permute-start.8
  24.0 0.0 collective-permute-done.4.refs_0_
  24.0 0.7 %collective-permute-start.9 = (f32[144,128]{1,0:T(8,128)S(1)}, f32[144,128]{1,0:T(8,128)S(1)}, u32[]{:S(2)}, u32[]{:S(2)}) collective-permute-start(f32[144,128]{1,0:T(8,128)S(1)} %get-tuple-element.49), channel_id=1, source_target_pairs={{0,2},{1,3},{2,0},{3,1},{4,6},{5,7},{6,4},{7,5},{8,10},{9,11},{10,... | collective-permute-start | bytes 221192 | tf_op jit(solution)/shard_map/ppermute | solution.py:571
  24.7 0.1 collective-permute-done.5.refs_1_
  24.8 2.8 %collective-permute-start.10 = (f32[144,128]{1,0:T(8,128)S(1)}, f32[144,128]{1,0:T(8,128)S(1)}, u32[]{:S(2)}, u32[]{:S(2)}) collective-permute-start(f32[144,128]{1,0:T(8,128)S(1)} %get-tuple-element.50), channel_id=1, source_target_pairs={{0,1},{1,0},{2,3},{3,2},{4,5},{5,4},{6,7},{7,6},{8,9},{9,8},{10,11... | collective-permute-start | bytes 221192 | tf_op jit(solution)/shard_map/ppermute | solution.py:571
  27.7 2.4 %levels.1 = (f32[2,3136,128]{2,1,0:T(8,128)S(1)}, f32[576,128]{1,0:T(8,128)S(1)}) custom-call(s32[4,8]{1,0:T(4,128)S(1)} %get-tuple-element.28.cols_ref, f32[400,128]{1,0:T(8,128)S(1)} %get-tuple-element.29.weight_ref, f32[400,128]{1,0:T(8,128)S(1)} %get-tuple-element.30.carry_ref, f32[400,128]{1,0:T(8,128)S(1)} %get-tuple-element.31.back_ref, ...), custom_call_target="tpu_custom_call" | custom-call | tf_op jit(solution)/shard_map/levels/pallas_call | solution.py:574
  30.1 1.4 %collective-permute-done.6.refs_2_ = f32[144,128]{1,0:T(8,128)S(1)} collective-permute-done((f32[144,128]{1,0:T(8,128)S(1)}, f32[144,128]{1,0:T(8,128)S(1)}, u32[]{:S(2)}, u32[]{:S(2)}) %collective-permute-start.6) | collective-permute-done | bytes 73760 | tf_op jit(solution)/shard_map/ppermute | solution.py:571
  31.5 0.0 collective-permute-done.7.refs_3_
  31.5 0.0 collective-permute-done.8.refs_4_
  31.5 0.2 collective-permute-done.9.refs_5_
  31.7 0.0 collective-permute-done.10.refs_6_
  31.7 3.3 %finish.1 = (f32[2,8,48,50]{3,2,1,0:T(8,128)}, f32[50,27,2,144]{3,2,1,0:T(2,128)}) custom-call(s32[4,8]{1,0:T(4,128)} %cols_hbm.5, s32[1]{0:T(128)S(6)} %copy.9.offset_ref, f32[576,128]{1,0:T(8,128)S(1)} %get-tuple-element.41.own_ref, f32[384,128]{1,0:T(8,128)S(1)} %get-tuple-element.42.pmid_ref, f32[128,128]{1,0:T(8,128)S(1)} %get-tuple-element.32.inverse_ref, ...), custom_call_target="tpu_custom_call" | custom-call | tf_op jit(solution)/shard_map/finish/pallas_call | solution.py:584
Async XLA Ops:
  0.6 11.0 %copy-start = (f32[2,50,27,144]{3,0,2,1:T(2,128)S(1)}, f32[2,50,27,144]{3,0,2,1:T(2,128)}, u32[]{:S(2)}) copy-start(f32[2,50,27,144]{3,0,2,1:T(2,128)} %param.8) | copy-start | bytes 4665604
  2.7 11.9 %copy-start.1 = (s32[27,144]{1,0:T(8,128)S(1)}, s32[27,144]{1,0:T(8,128)}, u32[]{:S(2)}) copy-start(s32[27,144]{1,0:T(8,128)} %cwet_ref.1) | copy-start | bytes 46660
  2.7 11.8 %collective-permute-start = (f32[256,128]{1,0:T(8,128)S(1)}, f32[256,128]{1,0:T(8,128)S(1)}, u32[]{:S(2)}, u32[]{:S(2)}) collective-permute-start(f32[256,128]{1,0:T(8,128)S(1)} %get-tuple-element.35), channel_id=1, source_target_pairs={{0,1},{1,2},{2,3},{3,4},{4,5},{5,6},{6,7},{7,8},{8,9},{9,10},{10,1... | collective-permute-start | bytes 393224 | tf_op jit(solution)/shard_map/ppermute | solution.py:483
  5.7 8.8 %collective-permute-start.1 = (f32[256,128]{1,0:T(8,128)S(1)}, f32[256,128]{1,0:T(8,128)S(1)}, u32[]{:S(2)}, u32[]{:S(2)}) collective-permute-start(f32[256,128]{1,0:T(8,128)S(1)} %get-tuple-element.36), channel_id=1, source_target_pairs={{0,31},{1,0},{2,1},{3,2},{4,3},{5,4},{6,5},{7,6},{8,7},{9,8},{10,9... | collective-permute-start | bytes 393224 | tf_op jit(solution)/shard_map/ppermute | solution.py:483
  9.2 5.3 %collective-permute-start.2 = (f32[8,128]{1,0:T(8,128)S(1)}, f32[8,128]{1,0:T(8,128)S(1)}, u32[]{:S(2)}, u32[]{:S(2)}) collective-permute-start(f32[8,128]{1,0:T(8,128)S(1)} %get-tuple-element.37), channel_id=1, source_target_pairs={{0,8},{8,16},{16,24},{24,0},{1,9},{9,17},{17,25},{25,1},{2,10},{10... | collective-permute-start | bytes 12296 | tf_op jit(solution)/shard_map/ppermute | solution.py:483
  9.2 5.3 %collective-permute-start.3 = (f32[8,128]{1,0:T(8,128)S(1)}, f32[8,128]{1,0:T(8,128)S(1)}, u32[]{:S(2)}, u32[]{:S(2)}) collective-permute-start(f32[8,128]{1,0:T(8,128)S(1)} %get-tuple-element.38), channel_id=1, source_target_pairs={{0,24},{8,0},{16,8},{24,16},{1,25},{9,1},{17,9},{25,17},{2,26},{10... | collective-permute-start | bytes 12296 | tf_op jit(solution)/shard_map/ppermute | solution.py:483
  16.3 7.7 %collective-permute-start.4 = (f32[144,128]{1,0:T(8,128)S(1)}, f32[144,128]{1,0:T(8,128)S(1)}, u32[]{:S(2)}, u32[]{:S(2)}) collective-permute-start(f32[144,128]{1,0:T(8,128)S(1)} %get-tuple-element.44), channel_id=1, source_target_pairs={{0,7},{1,6},{2,5},{3,4},{4,3},{5,2},{6,1},{7,0},{8,15},{9,14},{10,... | collective-permute-start | bytes 221192 | tf_op jit(solution)/shard_map/ppermute | solution.py:571
  18.2 6.6 %collective-permute-start.5 = (f32[144,128]{1,0:T(8,128)S(1)}, f32[144,128]{1,0:T(8,128)S(1)}, u32[]{:S(2)}, u32[]{:S(2)}) collective-permute-start(f32[144,128]{1,0:T(8,128)S(1)} %get-tuple-element.45), channel_id=1, source_target_pairs={{0,6},{1,7},{2,4},{3,5},{4,2},{5,3},{6,0},{7,1},{8,14},{9,15},{10,... | collective-permute-start | bytes 221192 | tf_op jit(solution)/shard_map/ppermute | solution.py:571
  18.8 12.7 %collective-permute-start.6 = (f32[144,128]{1,0:T(8,128)S(1)}, f32[144,128]{1,0:T(8,128)S(1)}, u32[]{:S(2)}, u32[]{:S(2)}) collective-permute-start(f32[144,128]{1,0:T(8,128)S(1)} %get-tuple-element.46), channel_id=1, source_target_pairs={{0,5},{1,4},{2,7},{3,6},{4,1},{5,0},{6,3},{7,2},{8,13},{9,12},{10,... | collective-permute-start | bytes 221192 | tf_op jit(solution)/shard_map/ppermute | solution.py:571
  20.5 11.0 %collective-permute-start.7 = (f32[144,128]{1,0:T(8,128)S(1)}, f32[144,128]{1,0:T(8,128)S(1)}, u32[]{:S(2)}, u32[]{:S(2)}) collective-permute-start(f32[144,128]{1,0:T(8,128)S(1)} %get-tuple-element.47), channel_id=1, source_target_pairs={{0,4},{1,5},{2,6},{3,7},{4,0},{5,1},{6,2},{7,3},{8,12},{9,13},{10,... | collective-permute-start | bytes 221192 | tf_op jit(solution)/shard_map/ppermute | solution.py:571
  24.0 7.5 %collective-permute-start.8 = (f32[144,128]{1,0:T(8,128)S(1)}, f32[144,128]{1,0:T(8,128)S(1)}, u32[]{:S(2)}, u32[]{:S(2)}) collective-permute-start(f32[144,128]{1,0:T(8,128)S(1)} %get-tuple-element.48), channel_id=1, source_target_pairs={{0,3},{1,2},{2,1},{3,0},{4,7},{5,6},{6,5},{7,4},{8,11},{9,10},{10,... | collective-permute-start | bytes 221192 | tf_op jit(solution)/shard_map/ppermute | solution.py:571
  24.0 7.7 %collective-permute-start.9 = (f32[144,128]{1,0:T(8,128)S(1)}, f32[144,128]{1,0:T(8,128)S(1)}, u32[]{:S(2)}, u32[]{:S(2)}) collective-permute-start(f32[144,128]{1,0:T(8,128)S(1)} %get-tuple-element.49), channel_id=1, source_target_pairs={{0,2},{1,3},{2,0},{3,1},{4,6},{5,7},{6,4},{7,5},{8,10},{9,11},{10,... | collective-permute-start | bytes 221192 | tf_op jit(solution)/shard_map/ppermute | solution.py:571
  24.8 6.9 %collective-permute-start.10 = (f32[144,128]{1,0:T(8,128)S(1)}, f32[144,128]{1,0:T(8,128)S(1)}, u32[]{:S(2)}, u32[]{:S(2)}) collective-permute-start(f32[144,128]{1,0:T(8,128)S(1)} %get-tuple-element.50), channel_id=1, source_target_pairs={{0,1},{1,0},{2,3},{3,2},{4,5},{5,4},{6,7},{7,6},{8,9},{9,8},{10,11... | collective-permute-start | bytes 221192 | tf_op jit(solution)/shard_map/ppermute | solution.py:571
